TPU v7x, 512 devices: a whole 4x4x16 slice. The times are simulated.
512 devices in a mesh: scen: 64 (over x, z), per: 8 (over y, core).
Axes of the slice: x: 4, y: 4, z: 16, core: 2. Of those that a mesh axis runs over, the one named last changes fastest.
Arguments:
- dual_start: float32 [512, 16, 8192], P('scen', 'per'), may hold values from -6 to 6
- demand: float32 [512, 16, 8192], P('scen', 'per'), may hold values from -6 to 6
- cost: float32 [16, 8192], P('per'), may hold values from -6 to 6
- upper: float32 [16, 8192], P('per'), may hold values from 0.2 to 1
- carry: float32 [16, 8192], P('per'), may hold values from 0.3 to 1
- prob: float32 [512], P('scen'), may hold values from 1 to 10
- section_size: int32 [16], P('per'), may hold values from 1 to 512, as said below
- block_cols: int32 [16, 16, 3], P('per'), may hold values from 0 to 15, as said below
- block_pool: int32 [16, 16, 3], P('per'), may hold values from 0 to 2
- pool_tiles: float32 [3, 512, 512], replicated, may hold values from -0.15625 to 0.15625
- step_table: float32 [4, 2], replicated, may hold values from 0.1 to 0.4
- subtree_step: int32 [8], replicated, may hold values from 0 to 3
- restart: int32 [2, 16], P(None, 'per'), may hold values 0 or 1
Outputs:
- primal: float32 [512, 16, 8192], P('scen', 'per')
- dual: float32 [512, 16, 8192], P('scen', 'per')
Inputs may be any that keep to these rules, and one draw needn't show every extreme that they name: `section_size`: each value is a power of two that divides the one before it; the first period's is 512 and the last period's is 1. `block_cols`: the 3 column blocks named for one block row of one period differ.
All inputs are finite; a program needn't handle non-finite values. No bound on the sum of `restart` on one device may be relied on, other than what follows from the above.
Results may differ from a plain program's by a relative error of at most 0.0001.
Values sent between devices are 32-bit elements; how exact they have to be, the bound alone decides.
No kernel may reach another device: no remote copies, remote signals or barrier semaphores. Data moves between devices by JAX's collectives and lax.ppermute only.
A program may use at most 64 MiB of HBM per device.

v0:
```python
import jax
import jax.numpy as jnp
from jax import lax
from jax.sharding import PartitionSpec as P

TILE = 512
NPOOL = 3
ITERS = 2
SUBTREES = 8
NSTEP = 4
RB = 16


HIGHEST = lax.Precision.HIGHEST


def shifted(block, axis, distance):
    devices = range(lax.axis_size(axis))
    route = [(i - distance, i) for i in devices if i - distance in devices]
    return lax.ppermute(block, axis, route)


def selection(block_cols, block_pool):
    labels = block_pool * RB + block_cols
    labels_all = jnp.arange(NPOOL * RB, dtype=jnp.int32)
    counted = jnp.sum((labels[..., None] == labels_all).astype(jnp.float32), axis=2)
    return counted.reshape(counted.shape[0], RB, NPOOL, RB)


def apply_blocks(fields, select, pool_tiles):
    scenarios, periods, feature = fields.shape
    blocks = fields.reshape(scenarios, periods, RB, TILE)
    images = jnp.einsum("spct,jut->spjcu", blocks, pool_tiles, precision=HIGHEST)
    result = jnp.einsum("pijc,spjcu->spiu", select, images, precision=HIGHEST)
    return result.reshape(scenarios, periods, feature)


def apply_blocks_transposed(fields, select, pool_tiles):
    scenarios, periods, feature = fields.shape
    blocks = fields.reshape(scenarios, periods, RB, TILE)
    images = jnp.einsum("spiu,jut->spjit", blocks, pool_tiles, precision=HIGHEST)
    result = jnp.einsum("pijc,spjit->spct", select, images, precision=HIGHEST)
    return result.reshape(scenarios, periods, feature)


def per_device(
    dual_start,
    demand,
    cost,
    upper,
    carry,
    prob,
    section_size,
    block_cols,
    block_pool,
    pool_tiles,
    step_table,
    subtree_step,
    restart,
):
    scen_local, per_local, feature = dual_start.shape
    devices = lax.axis_size("scen")
    device = lax.axis_index("scen")
    total_scen = scen_local * devices
    scen_ids = device * scen_local + jnp.arange(scen_local, dtype=jnp.int32)
    subtree = scen_ids // (total_scen // SUBTREES)
    subtree_hot = (subtree[:, None] == jnp.arange(SUBTREES, dtype=jnp.int32)[None, :]).astype(
        jnp.int32
    )
    entry = jnp.sum(subtree_hot * subtree_step[None, :], axis=1)
    entry_hot = (entry[:, None] == jnp.arange(NSTEP, dtype=jnp.int32)[None, :]).astype(jnp.float32)
    step_pair = jnp.dot(entry_hot, step_table, precision=HIGHEST)
    primal_step = step_pair[:, 0][:, None, None]
    dual_step = step_pair[:, 1][:, None, None]
    select = selection(block_cols, block_pool)
    span = jnp.maximum(section_size // scen_local, 1)
    inside = jnp.minimum(section_size, scen_local)
    local_ids = jnp.arange(scen_local, dtype=jnp.int32)
    local_group = local_ids[None, :] // inside[:, None]
    same_group = (local_group[:, :, None] == local_group[:, None, :]).astype(jnp.float32)
    weighting = same_group * prob[None, None, :]
    local_total = jnp.sum(weighting, axis=2)
    spread = span > 1
    total_row = jnp.full((per_local,), jnp.sum(prob), jnp.float32)
    primal = jnp.zeros_like(dual_start)
    dual = dual_start
    primal_mean = primal
    dual_mean = dual
    count = jnp.ones((per_local,), jnp.float32)
    for iteration in range(ITERS):
        carried = carry[None] * dual
        outgoing = shifted(carried[:, 0], "per", -1)
        following = jnp.concatenate([carried[:, 1:], outgoing[:, None]], axis=1)
        gradient = cost[None] - (apply_blocks_transposed(dual, select, pool_tiles) - following)
        values = primal - primal_step * gradient
        local_sum = jnp.einsum("psq,qpr->spr", weighting, values, precision=HIGHEST)
        device_sum = jnp.sum(prob[:, None, None] * values, axis=0)
        every_sum = lax.all_gather(device_sum[None], "scen", axis=0, tiled=True)
        every_total = lax.all_gather(total_row[None], "scen", axis=0, tiled=True)
        device_ids = jnp.arange(devices, dtype=jnp.int32)
        member = (device_ids[:, None] // span[None, :] == (device // span)[None, :]).astype(
            jnp.float32
        )
        cross_sum = jnp.einsum("np,npr->pr", member, every_sum, precision=HIGHEST)
        cross_total = jnp.sum(member * every_total, axis=0)
        numerator = jnp.where(spread[None, :, None], cross_sum[None], local_sum)
        denominator = jnp.where(spread[None, :], cross_total[None, :], local_total.T)
        averaged = numerator / denominator[:, :, None]
        primal_new = jnp.minimum(jnp.maximum(averaged, 0.0), upper[None])
        probe = 2.0 * primal_new - primal
        incoming = shifted(probe[:, -1], "per", 1)
        previous = jnp.concatenate([incoming[:, None], probe[:, :-1]], axis=1)
        dual_new = dual + dual_step * (
            demand - (apply_blocks(probe, select, pool_tiles) - carry[None] * previous)
        )
        weight_old = count[None, :, None]
        primal_mean = (weight_old * primal_mean + primal_new) / (weight_old + 1.0)
        dual_mean = (weight_old * dual_mean + dual_new) / (weight_old + 1.0)
        flagged = restart[iteration] == 1
        primal = jnp.where(flagged[None, :, None], primal_mean, primal_new)
        dual = jnp.where(flagged[None, :, None], dual_mean, dual_new)
        count = jnp.where(flagged, jnp.float32(1.0), count + 1.0)
    return (primal, dual)


def solution(mesh):
    return jax.shard_map(
        per_device,
        mesh=mesh,
        in_specs=(
            P("scen", "per", None),
            P("scen", "per", None),
            P("per", None),
            P("per", None),
            P("per", None),
            P("scen"),
            P("per"),
            P("per", None, None),
            P("per", None, None),
            P(),
            P(),
            P(),
            P(None, "per"),
        ),
        out_specs=(P("scen", "per", None), P("scen", "per", None)),
        check_vma=False,
    )
```

profile of v0, /device:TPU:1, one launch (start us, length us, event | category | flops | bytes accessed | tf_op | source)
XLA Modules:
  0.0 389.3 jit_solution(9140417718238913007)
XLA Ops:
  7.2 0.0 copy-start
  7.2 0.0 all-gather.5.cloned.1.call-start
  7.3 1.5 copy_multiply_fusion
  8.8 0.7 fusion.96
  9.5 8.8 %collective-permute-start = (f32[8,8192]{1,0:T(8,128)}, f32[8,8192]{1,0:T(8,128)}, u32[]{:S(2)}, u32[]{:S(2)}) collective-permute-start(f32[8,8192]{1,0:T(8,128)} %get-tuple-element.28), channel_id=1, source_target_pairs={{1,0},{2,1},{3,2},{4,3},{5,4},{6,5},{7,6},{9,8},{10,9},{11,10},{12... | collective-permute-start | bytes 786440 | tf_op jit(solution)/shard_map/ppermute | solution.py:20
  18.3 2.3 reshape.230
  20.7 0.2 select_reduce_fusion.1
  20.8 0.2 fusion.83
  21.0 5.2 %fusion.18 = f32[3,512,8,2,16]{1,4,0,2,3:T(8,128)} fusion(f32[3,512,512]{2,1,0:T(8,128)S(1)} %copy-done, f32[8,2,16,512]{3,2,1,0:T(8,128)} %reshape.230), kind=kOutput, calls=%fused_computation.20 | convolution fusion | flops 2415919104 | bytes 5242880 | tf_op jit(solution)/shard_map/spiu,jut->spjit/dot_general | solution.py:41
  26.2 0.1 convert_reduce_fusion
  26.3 0.1 reshape.231
  26.4 0.1 copy.70
  26.5 0.2 copy.150
  26.7 0.9 copy.151
  27.5 0.5 slice_bitcast_fusion.4
  28.0 0.0 collective-permute-done
  28.0 1.1 copy.149
  29.2 3.8 fusion.44
  33.0 1.5 broadcast_in_dim.135
  34.5 0.0 all-gather.5.cloned.1.call-update
  34.5 0.0 all-gather.7.cloned.1.call-start
  34.6 0.6 reduce_sum.70
  35.2 1.3 dynamic-slice
  36.4 1.3 dynamic-update-slice
  37.8 118.0 %all-reduce = f32[64]{0:T(128)} all-reduce(f32[64]{0:T(128)S(1)} %dynamic-update-slice), channel_id=2, replica_groups=mesh['scen'=64,'per'=8] {'scen'}, use_global_device_ids=true, to_apply=%add | all-reduce | flops 64 | bytes 512
  155.7 0.2 and_select_fusion.1
  155.9 0.2 select_reduce_fusion
  156.1 0.1 broadcast_maximum_fusion
  156.3 0.6 compare_bitcast_fusion.1
  156.8 1.0 select_reduce_fusion.2
  157.8 0.1 select_bitcast_fusion
  157.9 1.9 reshape.232
  159.8 12.3 %all-gather.5.cloned.1.call-done = f32[64,2,8192]{2,1,0:T(2,128)} async-done(((f32[1,2,8192]{2,1,0:T(2,128)}), f32[64,2,8192]{2,1,0:T(2,128)}) %all-gather.5.cloned.1.call-update) | async-done | bytes 4194320 | tf_op jit(solution)/shard_map/all_gather | solution.py:98
  172.1 5.8 %fusion.10 = f32[2,1,8192]{2,1,0:T(1,128)S(1)} fusion(f32[64,2,8192]{2,1,0:T(2,128)} %all-gather.5.cloned.1.call-done, pred[64,2,1]{0,1,2:T(4,128)(4,1)S(1)} %bitcast.180), kind=kOutput, calls=%fused_computation.12 | convolution fusion | flops 12582912 | bytes 4259968 | tf_op jit(solution)/shard_map/np,npr->pr/dot_general | solution.py:104
  178.0 0.1 copy.153
  178.1 2.5 broadcast_multiply_fusion
  180.6 0.7 slice_bitcast_fusion.2
  181.3 18.2 %collective-permute-start.1 = (f32[8,8192]{1,0:T(8,128)}, f32[8,8192]{1,0:T(8,128)}, u32[]{:S(2)}, u32[]{:S(2)}) collective-permute-start(f32[8,8192]{1,0:T(8,128)} %get-tuple-element.25), channel_id=1, source_target_pairs={{0,1},{1,2},{2,3},{3,4},{4,5},{5,6},{6,7},{8,9},{9,10},{10,11},{11... | collective-permute-start | bytes 786440 | tf_op jit(solution)/shard_map/ppermute | solution.py:20
  199.5 0.0 copy-start.2
  199.5 3.1 fusion.16
  202.6 1.8 fusion.31
  204.4 2.0 reshape.234
  206.3 0.0 collective-permute-done.1
  206.3 2.1 broadcast_multiply_fusion.1
  208.5 0.8 fusion.95
  209.3 1.9 collective-permute-start.2
  211.2 3.1 fusion.14
  214.4 1.8 fusion.34
  216.1 2.0 reshape.236
  218.1 3.1 multiply_reduce_fusion
  221.2 0.0 all-gather.7.cloned.1.call-update
  221.2 1.2 select_multiply_fusion
  222.4 125.9 %all-gather.7.cloned.1.call-done = f32[64,2,8192]{2,1,0:T(2,128)} async-done(((f32[1,2,8192]{2,1,0:T(2,128)}), f32[64,2,8192]{2,1,0:T(2,128)}) %all-gather.7.cloned.1.call-update) | async-done | bytes 4194320 | tf_op jit(solution)/shard_map/all_gather | solution.py:98
  348.4 5.9 %fusion.8 = f32[2,1,8192]{2,1,0:T(1,128)S(1)} fusion(f32[64,2,8192]{2,1,0:T(2,128)} %all-gather.7.cloned.1.call-done, pred[64,2,1]{0,1,2:T(4,128)(4,1)S(1)} %bitcast.181), kind=kOutput, calls=%fused_computation.10 | convolution fusion | flops 12582912 | bytes 4259968 | tf_op jit(solution)/shard_map/np,npr->pr/dot_general | solution.py:104
  354.2 0.1 copy.152
  354.3 2.3 multiply_subtract_fusion
  356.6 0.8 slice_bitcast_fusion
  357.5 12.0 %collective-permute-start.3 = (f32[8,8192]{1,0:T(8,128)}, f32[8,8192]{1,0:T(8,128)}, u32[]{:S(2)}, u32[]{:S(2)}) collective-permute-start(f32[8,8192]{1,0:T(8,128)} %get-tuple-element.21), channel_id=1, source_target_pairs={{0,1},{1,2},{2,3},{3,4},{4,5},{5,6},{6,7},{8,9},{9,10},{10,11},{11... | collective-permute-start | bytes 786440 | tf_op jit(solution)/shard_map/ppermute | solution.py:20
  369.5 3.1 fusion.12
  372.6 1.8 fusion.37
  374.4 2.0 reshape.238
  376.3 2.2 copy.67
  378.6 2.6 divide_select_fusion
  381.2 1.2 copy.68
  (65 shorter events, 0.2 us)
Async XLA Ops:
  7.2 13.9 %copy-start = (f32[3,512,512]{2,1,0:T(8,128)S(1)}, f32[3,512,512]{2,1,0:T(8,128)}, u32[]{:S(2)}) copy-start(f32[3,512,512]{2,1,0:T(8,128)} %param.24) | copy-start | bytes 9437188
  7.2 13.4 %copy-start.12 = (s32[2,16,3]{1,0,2:T(2,128)S(1)}, s32[2,16,3]{1,0,2:T(2,128)}, u32[]{:S(2)}) copy-start(s32[2,16,3]{1,0,2:T(2,128)} %param.22) | copy-start | bytes 1156
  7.2 13.4 %copy-start.13 = (s32[2,16,3]{1,0,2:T(2,128)S(1)}, s32[2,16,3]{1,0,2:T(2,128)}, u32[]{:S(2)}) copy-start(s32[2,16,3]{1,0,2:T(2,128)} %param.23) | copy-start | bytes 1156
  7.2 13.4 %copy-start.26 = (s32[8]{0:T(128)S(1)}, s32[8]{0:T(128)}, u32[]{:S(2)}) copy-start(s32[8]{0:T(128)} %param.26) | copy-start | bytes 100
  7.2 13.6 %copy-start.25 = (f32[4,2]{0,1:T(2,128)S(1)}, f32[4,2]{0,1:T(2,128)}, u32[]{:S(2)}) copy-start(f32[4,2]{0,1:T(2,128)} %param.25) | copy-start | bytes 100
  7.2 164.9 %all-gather.5.cloned.1.call-start = ((), (), s32[]{:S(2)}) async-start(), calls=%async_computation | async-start | bytes 4259840 | tf_op jit(solution)/shard_map/all_gather | solution.py:98
  9.5 18.5 %collective-permute-start = (f32[8,8192]{1,0:T(8,128)}, f32[8,8192]{1,0:T(8,128)}, u32[]{:S(2)}, u32[]{:S(2)}) collective-permute-start(f32[8,8192]{1,0:T(8,128)} %get-tuple-element.28), channel_id=1, source_target_pairs={{1,0},{2,1},{3,2},{4,3},{5,4},{6,5},{7,6},{9,8},{10,9},{11,10},{12... | collective-permute-start | bytes 786440 | tf_op jit(solution)/shard_map/ppermute | solution.py:20
  21.0 8.1 %copy-start.9 = (f32[8]{0:T(128)S(1)}, f32[8]{0:T(128)}, u32[]{:S(2)}) copy-start(f32[8]{0:T(128)} %param.20) | copy-start | bytes 100
  26.2 129.5 %copy-start.27 = (s32[2]{0:T(128)S(1)}, s32[2]{0:T(128)}, u32[]{:S(2)}) copy-start(s32[2]{0:T(128)} %param.21) | copy-start | bytes 28
  26.2 130.0 %copy-start.16 = (s32[2,2]{1,0:T(2,128)S(1)}, s32[2,2]{1,0:T(2,128)}, u32[]{:S(2)}) copy-start(s32[2,2]{1,0:T(2,128)} %param.27) | copy-start | bytes 52
  26.5 151.5 %copy-start.6 = (f32[2,16,3,16,1]{1,3,2,4,0:T(8,128)}, f32[2,16,3,16,1]{1,3,2,4,0:T(8,128)S(1)}, u32[]{:S(2)}) copy-start(f32[2,16,3,16,1]{1,3,2,4,0:T(8,128)S(1)} %copy.70) | copy-start | bytes 18436
  34.5 313.8 %all-gather.7.cloned.1.call-start = ((), (), s32[]{:S(2)}) async-start(), calls=%async_computation.1 | async-start | bytes 4259840 | tf_op jit(solution)/shard_map/all_gather | solution.py:98
  156.1 1.7 copy-start.17
  157.9 22.7 %copy-start.15 = (f32[8,2]{0,1:T(2,128)}, f32[8,2]{0,1:T(2,128)S(1)}, u32[]{:S(2)}) copy-start(f32[8,2]{0,1:T(2,128)S(1)} %select_bitcast_fusion) | copy-start | bytes 196
  157.9 20.2 %copy-start.18 = (pred[2]{0:T(512)(128)(4,1)S(1)}, pred[2]{0:T(512)(128)(4,1)}, u32[]{:S(2)}) copy-start(pred[2]{0:T(512)(128)(4,1)} %copy-done.17) | copy-start | bytes 10
  172.1 5.9 %copy-start.5 = (f32[8,2,8192]{2,0,1:T(8,128)S(1)}, f32[8,2,8192]{2,0,1:T(8,128)}, u32[]{:S(2)}) copy-start(f32[8,2,8192]{2,0,1:T(8,128)} %reshape.232) | copy-start | bytes 1572868
  172.1 5.9 %copy-start.8 = (f32[2,8192]{1,0:T(2,128)S(1)}, f32[2,8192]{1,0:T(2,128)}, u32[]{:S(2)}) copy-start(f32[2,8192]{1,0:T(2,128)} %param.17) | copy-start | bytes 196612
  172.1 5.9 %copy-start.23 = (f32[2,8192]{1,0:T(2,128)S(1)}, f32[2,8192]{1,0:T(2,128)}, u32[]{:S(2)}) copy-start(f32[2,8192]{1,0:T(2,128)} %param.18) | copy-start | bytes 196612
  181.3 25.0 %collective-permute-start.1 = (f32[8,8192]{1,0:T(8,128)}, f32[8,8192]{1,0:T(8,128)}, u32[]{:S(2)}, u32[]{:S(2)}) collective-permute-start(f32[8,8192]{1,0:T(8,128)} %get-tuple-element.25), channel_id=1, source_target_pairs={{0,1},{1,2},{2,3},{3,4},{4,5},{5,6},{6,7},{8,9},{9,10},{10,11},{11... | collective-permute-start | bytes 786440 | tf_op jit(solution)/shard_map/ppermute | solution.py:20
  199.5 6.8 %copy-start.2 = (f32[2,8192]{1,0:T(2,128)S(1)}, f32[2,8192]{1,0:T(2,128)}, u32[]{:S(2)}) copy-start(f32[2,8192]{1,0:T(2,128)} %param.19) | copy-start | bytes 196612
  208.5 5.9 %copy-start.1 = (f32[8,2,8192]{2,0,1:T(8,128)}, f32[8,2,8192]{2,0,1:T(8,128)S(1)}, u32[]{:S(2)}) copy-start(f32[8,2,8192]{2,0,1:T(8,128)S(1)} %get-tuple-element.14) | copy-start | bytes 1572868
  208.5 5.9 %copy-start.7 = (f32[2,16,3,16,1]{1,3,2,4,0:T(8,128)S(1)}, f32[2,16,3,16,1]{1,3,2,4,0:T(8,128)}, u32[]{:S(2)}) copy-start(f32[2,16,3,16,1]{1,3,2,4,0:T(8,128)} %copy-done.6) | copy-start | bytes 18436
  209.3 8.8 %collective-permute-start.2 = (f32[8,8192]{1,0:T(8,128)}, f32[8,8192]{1,0:T(8,128)}, u32[]{:S(2)}, u32[]{:S(2)}) collective-permute-start(f32[8,8192]{1,0:T(8,128)} %get-tuple-element.24), channel_id=1, source_target_pairs={{1,0},{2,1},{3,2},{4,3},{5,4},{6,5},{7,6},{9,8},{10,9},{11,10},{12... | collective-permute-start | bytes 786440 | tf_op jit(solution)/shard_map/ppermute | solution.py:20
  221.2 133.1 %copy-start.10 = (pred[2]{0:T(512)(128)(4,1)S(1)}, pred[2]{0:T(512)(128)(4,1)}, u32[]{:S(2)}) copy-start(pred[2]{0:T(512)(128)(4,1)} %get-tuple-element.30) | copy-start | bytes 10
  348.3 5.9 %copy-start.3 = (f32[8,2,8192]{2,0,1:T(8,128)S(1)}, f32[8,2,8192]{2,0,1:T(8,128)}, u32[]{:S(2)}) copy-start(f32[8,2,8192]{2,0,1:T(8,128)} %get-tuple-element.42) | copy-start | bytes 1572868
  348.3 6.0 %copy-start.4 = (f32[8,2,8192]{2,0,1:T(8,128)S(1)}, f32[8,2,8192]{2,0,1:T(8,128)}, u32[]{:S(2)}) copy-start(f32[8,2,8192]{2,0,1:T(8,128)} %get-tuple-element.12) | copy-start | bytes 1572868
  348.3 6.0 %copy-start.19 = (f32[2]{0:T(128)S(1)}, f32[2]{0:T(128)}, u32[]{:S(2)}) copy-start(f32[2]{0:T(128)} %get-tuple-element.31) | copy-start | bytes 28
  348.3 6.0 %copy-start.21 = (f32[2]{0:T(128)S(1)}, f32[2]{0:T(128)}, u32[]{:S(2)}) copy-start(f32[2]{0:T(128)} %get-tuple-element.32) | copy-start | bytes 28
  348.3 6.0 %copy-start.24 = (f32[2,8192]{1,0:T(2,128)S(1)}, f32[2,8192]{1,0:T(2,128)}, u32[]{:S(2)}) copy-start(f32[2,8192]{1,0:T(2,128)} %param.18) | copy-start | bytes 196612
  357.5 21.1 %collective-permute-start.3 = (f32[8,8192]{1,0:T(8,128)}, f32[8,8192]{1,0:T(8,128)}, u32[]{:S(2)}, u32[]{:S(2)}) collective-permute-start(f32[8,8192]{1,0:T(8,128)} %get-tuple-element.21), channel_id=1, source_target_pairs={{0,1},{1,2},{2,3},{3,4},{4,5},{5,6},{6,7},{8,9},{9,10},{10,11},{11... | collective-permute-start | bytes 786440 | tf_op jit(solution)/shard_map/ppermute | solution.py:20
  372.6 6.0 %copy-start.11 = (f32[8]{0:T(128)S(1)}, f32[8]{0:T(128)}, u32[]{:S(2)}) copy-start(f32[8]{0:T(128)} %get-tuple-element.33) | copy-start | bytes 100
  372.6 6.0 %copy-start.14 = (pred[2]{0:T(512)(128)(4,1)S(1)}, pred[2]{0:T(512)(128)(4,1)}, u32[]{:S(2)}) copy-start(pred[2]{0:T(512)(128)(4,1)} %get-tuple-element.29) | copy-start | bytes 10
  372.6 6.0 %copy-start.20 = (f32[2]{0:T(128)S(1)}, f32[2]{0:T(128)}, u32[]{:S(2)}) copy-start(f32[2]{0:T(128)} %get-tuple-element.31) | copy-start | bytes 28
  372.6 6.0 %copy-start.22 = (f32[2]{0:T(128)S(1)}, f32[2]{0:T(128)}, u32[]{:S(2)}) copy-start(f32[2]{0:T(128)} %get-tuple-element.32) | copy-start | bytes 28
Sparse Core Ops, SparseCore 0:
  34.6 137.4 all-gather.4
  221.3 126.9 all-gather.6
where the time goes:
time: 390 us; the launch traced here: 389 us
  waiting for transfers between devices  138 us (35%)
  blocking collectives  118 us (30%)
  starting transfers between devices  40.9 us (10%)
  matrix products  40.2 us (10%)
  local copies, waits for them, and re-layouts  23.8 us (6%)
  between operations  14.5 us (4%)
  other arithmetic  13.5 us (3%)
    all_gather x2, waiting for transfers between devices, per_device(): every_sum = lax.all_gather(device_sum[None], 'scen', axis=0, tiled=True)  138 us
    unnamed x1, blocking collectives  118 us
    ppermute x4, starting transfers between devices, shifted(): return lax.ppermute(block, axis, route)  40.9 us
    dot_general x2, matrix products, per_device(): cross_sum = jnp.einsum('np,npr->pr', member, every_sum, precision=HIGHEST)  11.7 us
    dot_general x2, matrix products, apply_blocks_transposed(): jnp.einsum('spiu,jut->spjit', blocks, pool_tiles, precision=HIGHEST)  8.29 us
    unnamed x64, local copies, waits for them, and re-layouts  8.25 us
  transfers between devices with their start and end apart: 6, of which 2 were waited for; matrix products, arithmetic and copies ran while one was open for 10% of the time, Pallas kernels for 0%

commit v1 on v0

v1 whole, which is shorter than its diff:
```python
import jax
import jax.numpy as jnp
from jax import lax
from jax.sharding import PartitionSpec as P

TILE = 512
NPOOL = 3
SUBTREES = 8
RB = 16
LANES = 128


HIGHEST = lax.Precision.HIGHEST


def shifted(block, axis, distance):
    devices = range(lax.axis_size(axis))
    route = [(i - distance, i) for i in devices if i - distance in devices]
    return lax.ppermute(block, axis, route)


def selection(block_cols, block_pool):
    labels = block_pool * RB + block_cols
    labels_all = jnp.arange(NPOOL * RB, dtype=jnp.int32)
    counted = jnp.sum((labels[..., None] == labels_all).astype(jnp.float32), axis=2)
    return counted.reshape(counted.shape[0], RB, NPOOL, RB)


def apply_blocks(fields, select, pool_tiles):
    periods, rows, feature = fields.shape
    blocks = fields.reshape(periods, rows, RB, TILE)
    images = jnp.einsum("psct,jut->psjcu", blocks, pool_tiles, precision=HIGHEST)
    result = jnp.einsum("pijc,psjcu->psiu", select, images, precision=HIGHEST)
    return result.reshape(periods, rows, feature)


def apply_blocks_transposed(fields, select, pool_tiles):
    periods, rows, feature = fields.shape
    blocks = fields.reshape(periods, rows, RB, TILE)
    images = jnp.einsum("psiu,jut->psjit", blocks, pool_tiles, precision=HIGHEST)
    result = jnp.einsum("pijc,psjit->psct", select, images, precision=HIGHEST)
    return result.reshape(periods, rows, feature)


def local_weights(section, prob):
    rows = prob.shape[0]
    inside = jnp.clip(section, 1, rows)
    group = jnp.arange(rows, dtype=jnp.int32)[None, :] // inside[:, None]
    same = (group[:, :, None] == group[:, None, :]).astype(jnp.float32) * prob[None, None, :]
    return same / jnp.sum(same, axis=2, keepdims=True)


def membership(section, rows, devices):
    span = jnp.maximum(section // rows, 1)
    group = jnp.arange(devices, dtype=jnp.int32)[None, :] // span[:, None]
    return (group[:, :, None] == group[:, None, :]).astype(jnp.float32)


def clipped(values, upper):
    return jnp.minimum(jnp.maximum(values, 0.0), upper)


def mixed(matrix, values):
    return jnp.einsum("pnm,pmr->pnr", matrix, values, precision=HIGHEST)


def per_device(
    dual_start,
    demand,
    cost,
    upper,
    carry,
    prob,
    section_size,
    block_cols,
    block_pool,
    pool_tiles,
    step_table,
    subtree_step,
    restart,
):
    rows, periods, feature = dual_start.shape
    devices = lax.axis_size("scen")
    device = lax.axis_index("scen")
    chunk = feature // devices
    device_ids = jnp.arange(devices, dtype=jnp.int32)
    steps = step_table[subtree_step[device_ids // (devices // SUBTREES)]]
    product_all = steps[:, 0] * steps[:, 1]
    rate, dual_rate = steps[device, 0], steps[device, 1]
    product = rate * dual_rate
    select = selection(block_cols, block_pool)
    damp = jnp.where(restart[0] == 1, 0.5, 1.0).astype(jnp.float32)
    start = dual_start.transpose(1, 0, 2)
    target = demand.transpose(1, 0, 2)
    moved = start + damp[:, None, None] * dual_rate * target
    both = jnp.concatenate([start, moved], axis=1)
    carried = carry[:, None] * both
    arriving = shifted(carried[0], "per", -1)
    square = carry * carry * damp[:, None]
    square_next = jnp.stack([square[1], shifted(square[0], "per", -1)])
    section_before = jnp.stack([shifted(section_size[1], "per", 1), section_size[0]])
    following = jnp.stack([carried[1], arriving])
    raw = rate * (apply_blocks_transposed(both, select, pool_tiles) - following - cost[:, None])
    weights = local_weights(section_size, prob)
    first_local = mixed(weights, raw[:, :rows])
    second_local = mixed(weights, raw[:, rows:])
    new_local = clipped(first_local, upper[:, None])
    mass = jnp.sum(prob)
    wide = (section_size > rows)[:, None]
    pushed = product * jnp.sum(prob[None, :, None] * new_local, axis=1)
    sums = jnp.where(wide, mass * first_local[:, 0], pushed)
    packed = jnp.concatenate(
        [sums, mass * second_local[:, 0], jnp.full((1, feature), 1.0) * mass, jnp.zeros((3, feature))]
    )
    sent = packed.reshape(8, devices, chunk).transpose(1, 0, 2)
    gathered = lax.all_to_all(sent, "scen", 0, 0, tiled=True).transpose(1, 0, 2)
    mass_all = gathered[4, :, 0]
    member = membership(section_size, rows, devices)
    member_before = membership(section_before, rows, devices)
    total = jnp.sum(member * mass_all, axis=2)
    total_before = jnp.sum(member_before * mass_all, axis=2)
    upper_chunk = lax.dynamic_slice_in_dim(upper, device * chunk, chunk, 1)
    new_chunk = clipped(mixed(member, gathered[0:2]) / total[:, :, None], upper_chunk[:, None])
    source = jnp.where(wide[:, None], (mass_all * product_all)[None, :, None] * new_chunk, gathered[0:2])
    pushed_chunk = mixed(member_before, source) / total_before[:, :, None]
    second_chunk = mixed(member, gathered[2:4]) / total[:, :, None]
    back = jnp.concatenate([new_chunk, second_chunk, pushed_chunk, jnp.zeros((2, devices, chunk))])
    returned = lax.all_to_all(back.transpose(1, 0, 2), "scen", 0, 0, tiled=True)
    returned = returned.transpose(1, 0, 2).reshape(8, 1, feature)
    mean_product = jnp.sum(member[:, device] * (mass_all * product_all), axis=1) / total[:, device]
    new = jnp.where(wide[:, None], returned[0:2], new_local)
    second = jnp.where(wide[:, None], returned[2:4], second_local)
    wide_before = (section_before > rows)[:, None, None]
    weights_before = local_weights(section_before, prob)
    pushed = jnp.where(wide_before, returned[4:6], product * mixed(weights_before, new))
    images = apply_blocks(jnp.concatenate([new, pushed], axis=1), select, pool_tiles)
    new_image = images[:, :rows]
    pulled = 2.0 * (carry * damp[:, None])[:, None] * images[:, rows:]
    pulled_next = jnp.stack([pulled[1], shifted(pulled[0], "per", -1)])
    new_before = jnp.stack([shifted(new[1], "per", 1), new[0]])
    net = 2.0 * (new_image - carry[:, None] * new_before)
    mean_damped = (damp * mean_product)[:, None, None]
    reaction = mean_damped * apply_blocks_transposed(net, select, pool_tiles)
    primal = damp[:, None, None] * new
    averaged = (
        primal + second - reaction + pulled_next
        - 2.0 * square_next[:, None] * mean_product[:, None, None] * new
    )
    primal_new = clipped(averaged, upper[:, None])
    probe = 2.0 * primal_new - primal
    probe_before = jnp.stack([shifted(probe[1], "per", 1), probe[0]])
    change = dual_rate * (target - net)
    dual = start + damp[:, None, None] * change
    dual_new = dual + dual_rate * (
        target - (apply_blocks(probe, select, pool_tiles) - carry[:, None] * probe_before)
    )
    count = jnp.where(restart[0] == 1, 1.0, 2.0)[:, None, None]
    flagged = (restart[1] == 1)[:, None, None]
    primal_mean = (count * (0.5 * new) + primal_new) / (count + 1.0)
    dual_mean = (count * (start + 0.5 * change) + dual_new) / (count + 1.0)
    primal = jnp.where(flagged, primal_mean, primal_new)
    dual = jnp.where(flagged, dual_mean, dual_new)
    return primal.transpose(1, 0, 2), dual.transpose(1, 0, 2)


def solution(mesh):
    return jax.shard_map(
        per_device,
        mesh=mesh,
        in_specs=(
            P("scen", "per", None),
            P("scen", "per", None),
            P("per", None),
            P("per", None),
            P("per", None),
            P("scen"),
            P("per"),
            P("per", None, None),
            P("per", None, None),
            P(),
            P(),
            P(),
            P(None, "per"),
        ),
        out_specs=(P("scen", "per", None), P("scen", "per", None)),
        check_vma=False,
    )
```

time: 390 us -> 176 us (0.45)
  blocking collectives: 118 us -> 0 us
  waiting for transfers between devices: 138 us -> 24.4 us
  other arithmetic: 13.5 us -> 35.8 us
  between operations: 14.5 us -> 2.43 us
  local copies, waits for them, and re-layouts: 23.8 us -> 32.5 us
  matrix products: 40.2 us -> 33 us
  starting transfers between devices: 40.9 us -> 46.5 us
    all_gather x2 -> x0, waiting for transfers between devices: 138 us -> none  [per_device(): every_sum = lax.all_gather(device_sum[None], 'scen', axis=0, tiled=True)]
    unnamed x1 -> x0, blocking collectives: 118 us -> none
    all_to_all x0 -> x2, waiting for transfers between devices: none -> 24.3 us  [the longest x1 13.8 us: per_device(): returned = lax.all_to_all(back.transpose(1, 0, 2), 'scen', 0, 0, tiled=True)]
    all_to_all x0 -> x2, starting transfers between devices: none -> 20.9 us  [the longest x1 14.3 us: per_device(): gathered = lax.all_to_all(sent, 'scen', 0, 0, tiled=True).transpose(1, 0, 2)]
    ppermute x4 -> x6, starting transfers between devices: 40.9 us -> 25.6 us  [shifted(): return lax.ppermute(block, axis, route)]
    mul x3 -> x12, other arithmetic: 4.83 us -> 12.6 us  [the longest x1 2.33 us: per_device(): rate * (apply_blocks_transposed(both, select, pool_tiles) - following - c...]
    dot_general x13 -> x14, matrix products: 40.2 us -> 33 us  [the longest x2 9.7 us: apply_blocks_transposed(): jnp.einsum('psiu,jut->psjit', blocks, pool_tiles, precision=HIGHEST)]
    reshape x5 -> x4, local copies, waits for them, and re-layouts: 10.1 us -> 8.72 us  [the longest x2 4.38 us: apply_blocks_transposed(): return result.reshape(periods, rows, feature)]
  transfers between devices with their start and end apart: 6 -> 8, of which waited for: 2 -> 2; matrix products, arithmetic and copies ran while one was open for 10% -> 37% of each run, Pallas kernels for 0% -> 0%
where the time goes in v1:
time: 176 us; the launch traced here: 175 us
  starting transfers between devices  46.5 us (26%)
  other arithmetic  35.8 us (20%)
  matrix products  33 us (19%)
  local copies, waits for them, and re-layouts  32.5 us (18%)
  waiting for transfers between devices  24.4 us (14%)
  between operations  2.43 us (1%)
    ppermute x6, starting transfers between devices, shifted(): return lax.ppermute(block, axis, route)  25.6 us
    all_to_all x1, starting transfers between devices, per_device(): gathered = lax.all_to_all(sent, 'scen', 0, 0, tiled=True).transpose(1, 0, 2)  14.3 us
    all_to_all x1, waiting for transfers between devices, per_device(): returned = lax.all_to_all(back.transpose(1, 0, 2), 'scen', 0, 0, tiled=True)  13.8 us
    all_to_all x1, waiting for transfers between devices, per_device(): gathered = lax.all_to_all(sent, 'scen', 0, 0, tiled=True).transpose(1, 0, 2)  10.6 us
    unnamed x64, local copies, waits for them, and re-layouts  10 us
    dot_general x2, matrix products, apply_blocks_transposed(): jnp.einsum('psiu,jut->psjit', blocks, pool_tiles, precision=HIGHEST)  9.7 us
    dot_general x2, matrix products, apply_blocks(): jnp.einsum('psct,jut->psjcu', blocks, pool_tiles, precision=HIGHEST)  8.5 us
    all_to_all x1, starting transfers between devices, per_device(): returned = lax.all_to_all(back.transpose(1, 0, 2), 'scen', 0, 0, tiled=True)  6.62 us
  transfers between devices with their start and end apart: 8, of which 2 were waited for; matrix products, arithmetic and copies ran while one was open for 37% of the time, Pallas kernels for 0%

profile of v1, /device:TPU:1, one launch (start us, length us, event | category | flops | bytes accessed | tf_op | source)
XLA Modules:
  0.0 174.6 jit_solution(10574931624285224892)
XLA Ops:
  0.6 1.6 fusion.106
  2.3 5.0 %fusion.89 = s32[64]{0:T(128)S(1)} fusion(s32[]{:T(128)} %bitcast.9, s32[]{:T(128)} %bitcast.10, s32[]{:T(128)} %bitcast.11, s32[]{:T(128)} %bitcast.12, s32[]{:T(128)} %bitcast.13, s32[]{:T(128)} %bitcast.15, s32[]{:T(128)} %bitcast.14, s32[]{:T(128)} %bitcast.8), kind=kLoop, calls=%fused_computation.176 | loop fusion | flops 1792 | bytes 288 | tf_op jit(solution)/shard_map/select_n | solution.py:87
  7.3 0.8 copy.72
  8.0 2.1 %copy.146 = f32[8,2,8192]{2,0,1:T(8,128)} copy(f32[8,2,8192]{2,1,0:T(2,128)} %param.17) | data formatting | bytes 1048576 | tf_op args[0]
  11.4 1.2 broadcast_multiply_fusion.3
  12.6 1.8 %fusion.48 = f32[2,8,8192]{2,1,0:T(8,128)S(1)} fusion(f32[8,2,8192]{2,1,0:T(2,128)} %param.18, f32[2]{0:T(128)S(1)} %broadcast_multiply_fusion.3, f32[8,2,8192]{2,1,0:T(2,128)} %param.17), kind=kLoop, calls=%fused_computation.56 | loop fusion | flops 262144 | bytes 1572872 | tf_op jit(solution)/shard_map/add | solution.py:95
  14.4 1.2 broadcast_multiply_fusion
  15.7 1.0 fusion.102
  16.7 8.8 %collective-permute-start = (f32[16,8192]{1,0:T(8,128)}, f32[16,8192]{1,0:T(8,128)}, u32[]{:S(2)}, u32[]{:S(2)}) collective-permute-start(f32[16,8192]{1,0:T(8,128)} %get-tuple-element.34), channel_id=1, source_target_pairs={{1,0},{2,1},{3,2},{4,3},{5,4},{6,5},{7,6},{9,8},{10,9},{11,10},{12... | collective-permute-start | bytes 1572872 | tf_op jit(solution)/shard_map/ppermute | solution.py:19
  26.1 1.9 %collective-permute-start.1 = (s32[]{:T(128)}, s32[]{:T(128)}, u32[]{:S(2)}, u32[]{:S(2)}) collective-permute-start(s32[]{:T(128)} %bitcast.39), channel_id=1, source_target_pairs={{0,1},{1,2},{2,3},{3,4},{4,5},{5,6},{6,7},{8,9},{9,10},{10,11},{11... | collective-permute-start | bytes 20 | tf_op jit(solution)/shard_map/ppermute | solution.py:19
  28.1 1.6 copy.120
  30.5 6.6 %fusion.8 = f32[2,16,16,3,512]{4,2,3,1,0:T(8,128)S(1)} fusion(f32[3,512,512]{2,1,0:T(8,128)S(1)} %copy-done, f32[2,16,16,512,1]{3,2,1,0,4:T(8,128)} %bitcast.240), kind=kOutput, calls=%fused_computation.10 | convolution fusion | flops 4831838208 | bytes 7340032 | tf_op jit(solution)/shard_map/psiu,jut->psjit/dot_general | solution.py:40
  37.2 2.8 %fusion.16 = f32[2,16,16,512]{3,2,1,0:T(8,128)} fusion(f32[2,16,3,16,1]{1,3,2,4,0:T(8,128)S(1)} %copy.97, f32[2,16,16,3,512]{4,2,3,1,0:T(8,128)S(1)} %fusion.8), kind=kOutput, calls=%fused_computation.18 | convolution fusion | flops 150994944 | bytes 4200448 | tf_op jit(solution)/shard_map/pijc,psjit->psct/dot_general | solution.py:41
  39.9 2.4 %reshape.450 = f32[2,16,8192]{2,1,0:T(8,128)} reshape(f32[2,16,16,512]{3,2,1,0:T(8,128)} %fusion.16) | data formatting | bytes 2097152 | tf_op jit(solution)/shard_map/reshape | solution.py:42
  44.3 0.7 pad.20.clone
  45.1 0.8 multiply_multiply_fusion.1
  45.9 1.4 sign_bitcast_fusion.1
  48.2 2.3 %fusion.31 = f32[2,16,8192]{2,1,0:T(8,128)S(1)} fusion(f32[2,16,8192]{2,1,0:T(8,128)} %reshape.450, f32[1,16,8192]{2,1,0:T(8,128)} %bitcast.33, f32[1,16,8192]{2,1,0:T(8,128)} %get-tuple-element.33, f32[2,8192]{1,0:T(2,128)S(1)} %copy-done.14, f32[]{:T(128)} %bitcast.19), kind=kLoop, calls=%fused_computation.30 | loop fusion | flops 1048576 | bytes 3211268 | tf_op jit(solution)/shard_map/mul | solution.py:103
  51.2 0.8 multiply_reduce_fusion
  52.0 0.8 copy-done.1
  52.8 0.7 slice_multiply_fusion.1
  53.8 0.8 maximum_bitcast_fusion
  54.6 14.3 %all-to-all-start = ((f32[64,8,128]{2,1,0:T(8,128)}), f32[64,8,128]{2,1,0:T(8,128)S(1)}, u32[]{:S(2)}, u32[]{:S(2)}) async-start(f32[64,8,128]{2,1,0:T(8,128)} %maximum_bitcast_fusion), calls=%async_computation | async-start | bytes 524288 | tf_op jit(solution)/shard_map/all_to_all | solution.py:116
  68.9 1.6 fusion.104
  70.5 2.1 %collective-permute-start.4 = (f32[8192]{0:T(1024)}, f32[8192]{0:T(1024)}, u32[]{:S(2)}, u32[]{:S(2)}) collective-permute-start(f32[8192]{0:T(1024)} %bitcast.75), channel_id=1, source_target_pairs={{1,0},{2,1},{3,2},{4,3},{5,4},{6,5},{7,6},{9,8},{10,9},{11,10},{12... | collective-permute-start | bytes 98312 | tf_op jit(solution)/shard_map/ppermute | solution.py:19
  72.5 1.3 constant_dynamic-slice_fusion.1
  73.8 0.7 fusion.64
  75.3 0.7 copy.71
  76.0 0.7 copy.83
  76.7 1.9 %add_compare_fusion = pred[2]{0:T(512)(128)(4,1)} fusion(s32[1]{0:T(128)} %get-tuple-element.62, s32[1]{0:T(128)} %bitcast.52), kind=kLoop, calls=%fused_computation.178 | loop fusion | flops 4 | bytes 10 | tf_op jit(solution)/shard_map/gt | solution.py:133
  78.6 10.6 %all-to-all-done = f32[64,8,128]{2,1,0:T(8,128)S(1)} async-done(((f32[64,8,128]{2,1,0:T(8,128)}), f32[64,8,128]{2,1,0:T(8,128)S(1)}, u32[]{:S(2)}, u32[]{:S(2)}) %all-to-all-start) | async-done | bytes 262176 | tf_op jit(solution)/shard_map/all_to_all | solution.py:116
  89.2 0.8 fusion.59
  90.0 1.6 select_reduce_fusion
  91.7 1.0 convolution_divide_fusion.1
  92.7 1.0 fusion.29
  93.8 1.1 convolution_divide_fusion
  95.0 0.9 copy.87
  95.8 6.6 %all-to-all-start.1 = ((f32[64,8,128]{2,1,0:T(8,128)}), f32[64,8,128]{2,1,0:T(8,128)S(1)}, u32[]{:S(2)}, u32[]{:S(2)}) async-start(f32[64,8,128]{2,1,0:T(8,128)} %copy.87), calls=%async_computation.1 | async-start | bytes 524288 | tf_op jit(solution)/shard_map/all_to_all | solution.py:128
  103.1 0.8 fusion.82
  103.9 1.3 fusion.97
  105.8 1.5 maximum_multiply_fusion.2
  107.2 13.8 %all-to-all-done.1 = f32[64,8,128]{2,1,0:T(8,128)S(1)} async-done(((f32[64,8,128]{2,1,0:T(8,128)}), f32[64,8,128]{2,1,0:T(8,128)S(1)}, u32[]{:S(2)}, u32[]{:S(2)}) %all-to-all-start.1) | async-done | bytes 262176 | tf_op jit(solution)/shard_map/all_to_all | solution.py:128
  121.7 1.2 fusion.50
  122.9 0.7 slice_bitcast_fusion.3
  123.6 1.2 broadcast_select_fusion
  125.6 7.1 %collective-permute-start.2 = (f32[8,8192]{1,0:T(8,128)}, f32[8,8192]{1,0:T(8,128)}, u32[]{:S(2)}, u32[]{:S(2)}) collective-permute-start(f32[8,8192]{1,0:T(8,128)} %get-tuple-element.39), channel_id=1, source_target_pairs={{0,1},{1,2},{2,3},{3,4},{4,5},{5,6},{6,7},{8,9},{9,10},{10,11},{11... | collective-permute-start | bytes 786440 | tf_op jit(solution)/shard_map/ppermute | solution.py:19
  132.7 5.4 %fusion.6 = f32[2,16,16,3,512]{4,2,3,1,0:T(8,128)S(1)} fusion(f32[3,512,512]{2,1,0:T(8,128)S(1)} %copy-done, f32[2,16,16,512,1]{3,2,1,0,4:T(8,128)S(1)} %bitcast.241), kind=kOutput, calls=%fused_computation.8 | convolution fusion | flops 4831838208 | bytes 7340032 | tf_op jit(solution)/shard_map/psct,jut->psjcu/dot_general | solution.py:32
  138.1 2.7 %fusion.19 = f32[2,16,16,512]{3,2,1,0:T(8,128)} fusion(f32[2,16,16,3,512]{4,2,3,1,0:T(8,128)S(1)} %fusion.6, f32[2,16,3,16,1]{3,2,1,0,4:T(4,128)S(1)} %bitcast.245), kind=kOutput, calls=%fused_computation.19 | convolution fusion | flops 150994944 | bytes 4200448 | tf_op jit(solution)/shard_map/pijc,psjcu->psiu/dot_general | solution.py:33
  140.8 2.4 %reshape.452 = f32[2,16,8192]{2,1,0:T(8,128)} reshape(f32[2,16,16,512]{3,2,1,0:T(8,128)} %fusion.19) | data formatting | bytes 2097152 | tf_op jit(solution)/shard_map/reshape | solution.py:34
  143.2 1.4 fusion.34
  144.7 0.8 fusion.103
  145.4 2.1 %collective-permute-start.3 = (f32[8,8192]{1,0:T(8,128)}, f32[8,8192]{1,0:T(8,128)}, u32[]{:S(2)}, u32[]{:S(2)}) collective-permute-start(f32[8,8192]{1,0:T(8,128)} %get-tuple-element.42), channel_id=1, source_target_pairs={{1,0},{2,1},{3,2},{4,3},{5,4},{6,5},{7,6},{9,8},{10,9},{11,10},{12... | collective-permute-start | bytes 786440 | tf_op jit(solution)/shard_map/ppermute | solution.py:19
  147.6 3.1 %fusion.4 = f32[2,8,16,3,512]{4,2,3,1,0:T(8,128)S(1)} fusion(f32[3,512,512]{2,1,0:T(8,128)S(1)} %copy-done, f32[2,8,16,512,1]{3,1,2,0,4:T(8,128)S(1)} %bitcast.238), kind=kOutput, calls=%fused_computation.6 | convolution fusion | flops 2415919104 | bytes 5242880 | tf_op jit(solution)/shard_map/psiu,jut->psjit/dot_general | solution.py:40
  150.7 1.8 %fusion.22 = f32[2,8,16,512]{3,2,1,0:T(8,128)} fusion(f32[2,16,3,16,1]{1,3,2,4,0:T(8,128)S(1)} %copy-done.11, f32[2,8,16,3,512]{4,2,3,1,0:T(8,128)S(1)} %fusion.4), kind=kOutput, calls=%fused_computation.20 | convolution fusion | flops 75497472 | bytes 2103296 | tf_op jit(solution)/shard_map/pijc,psjit->psct/dot_general | solution.py:41
  152.5 1.9 %reshape.454 = f32[2,8,8192]{2,1,0:T(8,128)} reshape(f32[2,8,16,512]{3,2,1,0:T(8,128)} %fusion.22) | data formatting | bytes 1048576 | tf_op jit(solution)/shard_map/reshape | solution.py:42
  154.4 2.7 %multiply_subtract_fusion = (f32[2,8,8192]{2,1,0:T(8,128)S(1)}, f32[8,2,8192]{2,0,1:T(8,128)}) fusion(f32[2]{0:T(128)S(1)} %copy-done.19, f32[2,8192]{1,0:T(2,128)} %param.20, f32[2,8192]{1,0:T(2,128)} %maximum_multiply_fusion.2, f32[1,8,8192]{2,1,0:T(8,128)} %bitcast.74, f32[1,8,8192]{2,1,0:T(8,128)S(1)} %get-tuple-element.41, f32[2,8,8192]{2,1,0:T(8,128)} %reshape.454, ...), kind=kLoop, calls=%fused_computation.60 | loop fusion | flops 2621440 | bytes 3407908 | tf_op jit(solution)/shard_map/sub | solution.py:150
  157.1 0.8 slice_bitcast_fusion.1
  157.9 3.6 %collective-permute-start.5 = (f32[8,8192]{1,0:T(8,128)}, f32[8,8192]{1,0:T(8,128)}, u32[]{:S(2)}, u32[]{:S(2)}) collective-permute-start(f32[8,8192]{1,0:T(8,128)} %get-tuple-element.37), channel_id=1, source_target_pairs={{0,1},{1,2},{2,3},{3,4},{4,5},{5,6},{6,7},{8,9},{9,10},{10,11},{11... | collective-permute-start | bytes 786440 | tf_op jit(solution)/shard_map/ppermute | solution.py:19
  161.5 3.1 %fusion.2 = f32[2,8,16,3,512]{4,2,3,1,0:T(8,128)S(1)} fusion(f32[3,512,512]{2,1,0:T(8,128)S(1)} %copy-done, f32[2,8,16,512,1]{3,1,2,0,4:T(8,128)S(1)} %bitcast.237), kind=kOutput, calls=%fused_computation.4 | convolution fusion | flops 2415919104 | bytes 5242880 | tf_op jit(solution)/shard_map/psct,jut->psjcu/dot_general | solution.py:32
  164.6 1.8 %fusion.25 = f32[2,8,16,512]{3,2,1,0:T(8,128)} fusion(f32[2,8,16,3,512]{4,2,3,1,0:T(8,128)S(1)} %fusion.2, f32[2,16,3,16,1]{3,2,1,0,4:T(4,128)S(1)} %bitcast.246), kind=kOutput, calls=%fused_computation.21 | convolution fusion | flops 75497472 | bytes 2103296 | tf_op jit(solution)/shard_map/pijc,psjcu->psiu/dot_general | solution.py:33
  166.4 1.9 %reshape.456 = f32[2,8,8192]{2,1,0:T(8,128)} reshape(f32[2,8,16,512]{3,2,1,0:T(8,128)} %fusion.25) | data formatting | bytes 1048576 | tf_op jit(solution)/shard_map/reshape | solution.py:34
  168.3 2.2 %copy.93 = f32[8,2,8192]{2,1,0:T(2,128)} copy(f32[8,2,8192]{2,0,1:T(8,128)} %get-tuple-element.30) | data formatting | bytes 1048576
  170.6 2.8 %select_bitcast_fusion = f32[8,2,8192]{2,0,1:T(8,128)S(1)} fusion(f32[2,8,8192]{2,1,0:T(8,128)} %reshape.456, f32[1,8,8192]{2,1,0:T(8,128)S(1)} %get-tuple-element.38, f32[1,8,8192]{2,1,0:T(8,128)} %bitcast.86, f32[2,8,8192]{2,1,0:T(8,128)} %copy-done.2, f32[8,2,8192]{2,1,0:T(2,128)} %param.18, f32[]{:T(128)} %bitcast.22, f32[2]{0:T(128)S(1)} %get-tuple-element.53, ...), kind=kLoop, calls=%fused_computation.59 | loop fusion | flops 2097152 | bytes 3211294 | tf_op jit(solution)/shard_map/transpose | solution.py:163
  173.4 1.2 copy.94
  (102 shorter events, 8.8 us)
Async XLA Ops:
  0.6 29.9 %copy-start = (f32[3,512,512]{2,1,0:T(8,128)S(1)}, f32[3,512,512]{2,1,0:T(8,128)}, u32[]{:S(2)}) copy-start(f32[3,512,512]{2,1,0:T(8,128)} %param.26) | copy-start | bytes 9437188
  12.6 12.9 %copy-start.17 = (s32[2]{0:T(128)S(1)}, s32[2]{0:T(128)}, u32[]{:S(2)}) copy-start(s32[2]{0:T(128)} %param.23) | copy-start | bytes 28
  12.6 15.5 %copy-start.27 = (s32[2,2]{1,0:T(2,128)S(1)}, s32[2,2]{1,0:T(2,128)}, u32[]{:S(2)}) copy-start(s32[2,2]{1,0:T(2,128)} %param.29) | copy-start | bytes 52
  14.4 15.3 %copy-start.22 = (s32[2,16,3]{1,0,2:T(2,128)S(1)}, s32[2,16,3]{1,0,2:T(2,128)}, u32[]{:S(2)}) copy-start(s32[2,16,3]{1,0,2:T(2,128)} %param.24) | copy-start | bytes 1156
  14.4 15.3 %copy-start.23 = (s32[2,16,3]{1,0,2:T(2,128)S(1)}, s32[2,16,3]{1,0,2:T(2,128)}, u32[]{:S(2)}) copy-start(s32[2,16,3]{1,0,2:T(2,128)} %param.25) | copy-start | bytes 1156
  16.7 31.5 %collective-permute-start = (f32[16,8192]{1,0:T(8,128)}, f32[16,8192]{1,0:T(8,128)}, u32[]{:S(2)}, u32[]{:S(2)}) collective-permute-start(f32[16,8192]{1,0:T(8,128)} %get-tuple-element.34), channel_id=1, source_target_pairs={{1,0},{2,1},{3,2},{4,3},{5,4},{6,5},{7,6},{9,8},{10,9},{11,10},{12... | collective-permute-start | bytes 1572872 | tf_op jit(solution)/shard_map/ppermute | solution.py:19
  26.1 19.8 %collective-permute-start.1 = (s32[]{:T(128)}, s32[]{:T(128)}, u32[]{:S(2)}, u32[]{:S(2)}) collective-permute-start(s32[]{:T(128)} %bitcast.39), channel_id=1, source_target_pairs={{0,1},{1,2},{2,3},{3,4},{4,5},{5,6},{6,7},{8,9},{9,10},{10,11},{11... | collective-permute-start | bytes 20 | tf_op jit(solution)/shard_map/ppermute | solution.py:19
  28.1 25.5 %copy-start.20 = (pred[2]{0:T(512)(128)(4,1)}, pred[2]{0:T(512)(128)(4,1)S(1)}, u32[]{:S(2)}) copy-start(pred[2]{0:T(512)(128)(4,1)S(1)} %broadcast_compare_fusion.2) | copy-start | bytes 10
  28.1 17.0 %copy-start.18 = (f32[2]{0:T(128)}, f32[2]{0:T(128)S(1)}, u32[]{:S(2)}) copy-start(f32[2]{0:T(128)S(1)} %fusion.85) | copy-start | bytes 28
  29.9 0.6 copy-start.5
  30.0 7.1 %copy-start.10 = (f32[2,16,3,16,1]{1,3,2,4,0:T(8,128)}, f32[2,16,3,16,1]{1,3,2,4,0:T(8,128)S(1)}, u32[]{:S(2)}) copy-start(f32[2,16,3,16,1]{1,3,2,4,0:T(8,128)S(1)} %copy.97) | copy-start | bytes 18436
  37.1 6.5 %copy-start.16 = (f32[8]{0:T(128)S(1)}, f32[8]{0:T(128)}, u32[]{:S(2)}) copy-start(f32[8]{0:T(128)} %param.22) | copy-start | bytes 100
  37.2 8.0 %copy-start.4 = (f32[2,8192]{1,0:T(2,128)S(1)}, f32[2,8192]{1,0:T(2,128)}, u32[]{:S(2)}) copy-start(f32[2,8192]{1,0:T(2,128)} %param.21) | copy-start | bytes 196612
  37.2 11.0 %copy-start.14 = (f32[2,8192]{1,0:T(2,128)S(1)}, f32[2,8192]{1,0:T(2,128)}, u32[]{:S(2)}) copy-start(f32[2,8192]{1,0:T(2,128)} %param.19) | copy-start | bytes 196612
  39.9 11.2 %copy-start.7 = (f32[2,8192]{1,0:T(2,128)S(1)}, f32[2,8192]{1,0:T(2,128)}, u32[]{:S(2)}) copy-start(f32[2,8192]{1,0:T(2,128)} %param.20) | copy-start | bytes 196612
  48.2 26.4 %copy-start.28 = (s32[2,2]{1,0:T(2,128)S(1)}, s32[2,2]{1,0:T(2,128)}, u32[]{:S(2)}) copy-start(s32[2,2]{1,0:T(2,128)} %param.29) | copy-start | bytes 52
  51.2 2.4 %copy-start.3 = (f32[2,8,8192]{2,1,0:T(8,128)}, f32[2,8,8192]{2,1,0:T(8,128)S(1)}, u32[]{:S(2)}) copy-start(f32[2,8,8192]{2,1,0:T(8,128)S(1)} %fusion.35) | copy-start | bytes 1572868
  52.0 0.8 copy-start.1
  54.6 34.6 %all-to-all-start = ((f32[64,8,128]{2,1,0:T(8,128)}), f32[64,8,128]{2,1,0:T(8,128)S(1)}, u32[]{:S(2)}, u32[]{:S(2)}) async-start(f32[64,8,128]{2,1,0:T(8,128)} %maximum_bitcast_fusion), calls=%async_computation | async-start | bytes 524288 | tf_op jit(solution)/shard_map/all_to_all | solution.py:116
  70.5 35.3 %collective-permute-start.4 = (f32[8192]{0:T(1024)}, f32[8192]{0:T(1024)}, u32[]{:S(2)}, u32[]{:S(2)}) collective-permute-start(f32[8192]{0:T(1024)} %bitcast.75), channel_id=1, source_target_pairs={{1,0},{2,1},{3,2},{4,3},{5,4},{6,5},{7,6},{9,8},{10,9},{11,10},{12... | collective-permute-start | bytes 98312 | tf_op jit(solution)/shard_map/ppermute | solution.py:19
  89.2 0.8 copy-start.12
  90.0 3.8 %copy-start.24 = (f32[64]{0:T(128)}, f32[64]{0:T(128)S(1)}, u32[]{:S(2)}) copy-start(f32[64]{0:T(128)S(1)} %get-tuple-element.13) | copy-start | bytes 772
  90.0 31.7 %copy-start.8 = (f32[2,8192]{1,0:T(2,128)S(1)}, f32[2,8192]{1,0:T(2,128)}, u32[]{:S(2)}) copy-start(f32[2,8192]{1,0:T(2,128)} %param.20) | copy-start | bytes 196612
  91.6 2.2 %copy-start.15 = (pred[2,64,64]{2,0,1:T(4,128)(4,1)}, pred[2,64,64]{2,0,1:T(4,128)(4,1)S(1)}, u32[]{:S(2)}) copy-start(pred[2,64,64]{2,0,1:T(4,128)(4,1)S(1)} %get-tuple-element.22) | copy-start | bytes 24580
  91.6 2.2 %copy-start.13 = (f32[2,64]{0,1:T(8,128)}, f32[2,64]{0,1:T(8,128)S(1)}, u32[]{:S(2)}) copy-start(f32[2,64]{0,1:T(8,128)S(1)} %get-tuple-element.17) | copy-start | bytes 1540
  91.6 30.1 %copy-start.21 = (pred[2]{0:T(512)(128)(4,1)S(1)}, pred[2]{0:T(512)(128)(4,1)}, u32[]{:S(2)}) copy-start(pred[2]{0:T(512)(128)(4,1)} %copy-done.20) | copy-start | bytes 10
  95.8 25.2 %all-to-all-start.1 = ((f32[64,8,128]{2,1,0:T(8,128)}), f32[64,8,128]{2,1,0:T(8,128)S(1)}, u32[]{:S(2)}, u32[]{:S(2)}) async-start(f32[64,8,128]{2,1,0:T(8,128)} %copy.87), calls=%async_computation.1 | async-start | bytes 524288 | tf_op jit(solution)/shard_map/all_to_all | solution.py:128
  121.7 1.9 %copy-start.9 = (f32[2,8192]{1,0:T(2,128)}, f32[2,8192]{1,0:T(2,128)S(1)}, u32[]{:S(2)}) copy-start(f32[2,8192]{1,0:T(2,128)S(1)} %get-tuple-element.45) | copy-start | bytes 196612
  125.6 17.7 %collective-permute-start.2 = (f32[8,8192]{1,0:T(8,128)}, f32[8,8192]{1,0:T(8,128)}, u32[]{:S(2)}, u32[]{:S(2)}) collective-permute-start(f32[8,8192]{1,0:T(8,128)} %get-tuple-element.39), channel_id=1, source_target_pairs={{0,1},{1,2},{2,3},{3,4},{4,5},{5,6},{6,7},{8,9},{9,10},{10,11},{11... | collective-permute-start | bytes 786440 | tf_op jit(solution)/shard_map/ppermute | solution.py:19
  132.7 5.4 %copy-start.6 = (f32[2,16,3,16]{3,2,1,0:T(4,128)S(1)}, f32[2,16,3,16]{3,2,1,0:T(4,128)}, u32[]{:S(2)}) copy-start(f32[2,16,3,16]{3,2,1,0:T(4,128)} %copy-done.5) | copy-start | bytes 18436
  144.7 6.0 %copy-start.2 = (f32[2,8,8192]{2,1,0:T(8,128)}, f32[2,8,8192]{2,1,0:T(8,128)S(1)}, u32[]{:S(2)}) copy-start(f32[2,8,8192]{2,1,0:T(8,128)S(1)} %get-tuple-element.31) | copy-start | bytes 1572868
  144.7 6.0 %copy-start.11 = (f32[2,16,3,16,1]{1,3,2,4,0:T(8,128)S(1)}, f32[2,16,3,16,1]{1,3,2,4,0:T(8,128)}, u32[]{:S(2)}) copy-start(f32[2,16,3,16,1]{1,3,2,4,0:T(8,128)} %copy-done.10) | copy-start | bytes 18436
  145.4 9.0 %collective-permute-start.3 = (f32[8,8192]{1,0:T(8,128)}, f32[8,8192]{1,0:T(8,128)}, u32[]{:S(2)}, u32[]{:S(2)}) collective-permute-start(f32[8,8192]{1,0:T(8,128)} %get-tuple-element.42), channel_id=1, source_target_pairs={{1,0},{2,1},{3,2},{4,3},{5,4},{6,5},{7,6},{9,8},{10,9},{11,10},{12... | collective-permute-start | bytes 786440 | tf_op jit(solution)/shard_map/ppermute | solution.py:19
  147.6 6.9 %copy-start.19 = (f32[2]{0:T(128)S(1)}, f32[2]{0:T(128)}, u32[]{:S(2)}) copy-start(f32[2]{0:T(128)} %copy-done.18) | copy-start | bytes 28
  147.6 6.8 %copy-start.25 = (pred[2]{0:T(512)(128)(4,1)S(1)}, pred[2]{0:T(512)(128)(4,1)}, u32[]{:S(2)}) copy-start(pred[2]{0:T(512)(128)(4,1)} %compare_bitcast_fusion) | copy-start | bytes 10
  157.9 12.7 %collective-permute-start.5 = (f32[8,8192]{1,0:T(8,128)}, f32[8,8192]{1,0:T(8,128)}, u32[]{:S(2)}, u32[]{:S(2)}) collective-permute-start(f32[8,8192]{1,0:T(8,128)} %get-tuple-element.37), channel_id=1, source_target_pairs={{0,1},{1,2},{2,3},{3,4},{4,5},{5,6},{6,7},{8,9},{9,10},{10,11},{11... | collective-permute-start | bytes 786440 | tf_op jit(solution)/shard_map/ppermute | solution.py:19
  164.6 6.0 %copy-start.26 = (f32[2]{0:T(128)S(1)}, f32[2]{0:T(128)}, u32[]{:S(2)}) copy-start(f32[2]{0:T(128)} %broadcast_add_fusion) | copy-start | bytes 28

commit v2 on v0

v2 whole, which is shorter than its diff:
```python
import jax
import jax.numpy as jnp
from jax import lax
from jax.experimental import pallas as pl
from jax.experimental.pallas import tpu as pltpu
from jax.sharding import PartitionSpec as P

TILE = 512
NPOOL = 3
NB = 3
SUBTREES = 8
RB = 16
LANES = 128
ROWS = 8
PER = 2
QUARTERS = TILE // LANES
MIB = 1 << 20
F32 = jnp.float32
BF16 = jnp.bfloat16

VM = pl.BlockSpec(memory_space=pltpu.VMEM)
SM = pl.BlockSpec(memory_space=pltpu.SMEM)


def shifted(block, axis, distance):
    devices = range(lax.axis_size(axis))
    route = [(i - distance, i) for i in devices if i - distance in devices]
    return lax.ppermute(block, axis, route)


def call(body, specs, outs, scratch=(), limit=16):
    return pl.pallas_call(
        body,
        out_shape=[jax.ShapeDtypeStruct(shape, dtype) for shape, dtype in outs],
        in_specs=specs,
        out_specs=[VM] * len(outs),
        scratch_shapes=list(scratch),
        compiler_params=pltpu.CompilerParams(vmem_limit_bytes=limit * MIB),
    )


def step_pair(steps_ref, subtree_ref):
    device = lax.axis_index("scen")
    entry = subtree_ref[device // (lax.axis_size("scen") // SUBTREES)]
    return steps_ref[entry, 0], steps_ref[entry, 1]


def damping(restart_ref, period):
    return jnp.where(restart_ref[0, period] == 1, 0.5, 1.0).astype(F32)


def lanes_of(ref, row, block):
    return ref[row : row + 1, block * TILE : (block + 1) * TILE]


def prob_column(prob_ref):
    row = lax.broadcasted_iota(jnp.int32, (ROWS, LANES), 0)
    column = jnp.zeros((ROWS, LANES), F32)
    for s in range(ROWS):
        column = jnp.where(row == s, prob_ref[s], column)
    return column


def widened(column):
    return jnp.concatenate([column] * QUARTERS, axis=1)


def group_sum(values, inside):
    row = lax.broadcasted_iota(jnp.int32, values.shape, 0)
    for step in (1, 2, 4):
        partner = jnp.where(
            (row & step) != 0,
            pltpu.roll(values, step, 0),
            pltpu.roll(values, ROWS - step, 0),
        )
        values = jnp.where(inside > step, values + partner, values)
    return values


def halves(values):
    high = values.astype(BF16)
    return high, (values - high.astype(F32)).astype(BF16)


def product_images(lhs_ref, high_ref, low_ref, image_ref, transposed):
    rows = lhs_ref.shape[0]
    high, low = halves(lhs_ref[...])
    both = jnp.concatenate([high, low], axis=0)
    dims = (((1,), (0,)), ((), ())) if transposed else (((1,), (1,)), ((), ()))

    def dot(a, b):
        return lax.dot_general(a, b, dims, preferred_element_type=F32)

    for j in range(NPOOL):
        main = dot(both, high_ref[j])
        image_ref[j] = main[:rows] + main[rows:] + dot(high, low_ref[j])


def gathered_blocks(image_ref, code_ref, period, block, height):
    total = None
    for k in range(NB):
        code = code_ref[(period * RB + block) * NB + k]
        first = pl.multiple_of((period * RB + code % RB) * height, height)
        part = image_ref[code // RB, pl.ds(first, height), :]
        total = part if total is None else total + part
    return total


def scattered_blocks(image_ref, code_ref, out_ref, height):
    out_ref[...] = jnp.zeros_like(out_ref)
    for period in range(PER):
        for block in range(RB):
            first = (period * RB + block) * height
            for k in range(NB):
                code = code_ref[(period * RB + block) * NB + k]
                part = image_ref[code // RB, first : first + height, :]
                place = pl.multiple_of((period * RB + code % RB) * height, height)
                out_ref[pl.ds(place, height), :] += part


def relayout_kernel(dual_ref, demand_ref, carry_ref, steps_ref, subtree_ref, restart_ref,
                    start_ref, target_ref, carried_ref):
    _, dual_rate = step_pair(steps_ref, subtree_ref)
    for period in range(PER):
        for s in range(ROWS):
            a = dual_ref[s, period : period + 1, :]
            b = demand_ref[s, period : period + 1, :]
            for block in range(RB):
                lanes = slice(block * TILE, (block + 1) * TILE)
                start_ref[period, block, s : s + 1, :] = a[:, lanes]
                target_ref[period, block, s : s + 1, :] = b[:, lanes]
    factor = damping(restart_ref, 0) * dual_rate
    for block in range(RB):
        weight = lanes_of(carry_ref, 0, block)
        a, b = start_ref[0, block], target_ref[0, block]
        carried_ref[block, 0:ROWS, :] = weight * a
        carried_ref[block, ROWS : 2 * ROWS, :] = weight * (a + factor * b)


def pull_kernel(start_ref, target_ref, pool_ref, code_ref, steps_ref, subtree_ref, restart_ref,
                pulled_ref, high_ref, low_ref, lhs_ref, image_ref):
    _, dual_rate = step_pair(steps_ref, subtree_ref)
    for j in range(NPOOL):
        high, low = halves(pool_ref[j])
        high_ref[j] = high
        low_ref[j] = low
    for period in range(PER):
        factor = damping(restart_ref, period) * dual_rate
        for block in range(RB):
            first = (period * RB + block) * 2 * ROWS
            a, b = start_ref[period, block], target_ref[period, block]
            lhs_ref[first : first + ROWS, :] = a
            lhs_ref[first + ROWS : first + 2 * ROWS, :] = a + factor * b
    product_images(lhs_ref, high_ref, low_ref, image_ref, True)
    scattered_blocks(image_ref, code_ref, pulled_ref, 2 * ROWS)


def local_kernel(pulled_ref, start_ref, target_ref, arriving_ref, cost_ref, upper_ref, carry_ref,
                 prob_ref, section_ref, steps_ref, subtree_ref, restart_ref,
                 new_ref, second_ref, message_ref):
    rate, dual_rate = step_pair(steps_ref, subtree_ref)
    product = rate * dual_rate
    narrow = prob_column(prob_ref)
    mass = jnp.sum(narrow, axis=0, keepdims=True)
    weight = widened(narrow)
    total_mass = widened(mass)
    factor = damping(restart_ref, 1) * dual_rate
    for period in range(PER):
        section = section_ref[period]
        inverse = 1.0 / group_sum(weight, section)
        wide = section > ROWS
        for block in range(RB):
            first = (period * RB + block) * 2 * ROWS
            if period == 0:
                carry = lanes_of(carry_ref, 1, block)
                a = start_ref[1, block]
                follow_first = carry * a
                follow_second = carry * (a + factor * target_ref[1, block])
            else:
                follow_first = arriving_ref[block, 0:ROWS, :]
                follow_second = arriving_ref[block, ROWS : 2 * ROWS, :]
            cost = lanes_of(cost_ref, period, block)
            raw = rate * (pulled_ref[first : first + ROWS, :] - follow_first - cost)
            other = rate * (pulled_ref[first + ROWS : first + 2 * ROWS, :] - follow_second - cost)
            averaged = group_sum(weight * raw, section) * inverse
            second = group_sum(weight * other, section) * inverse
            new = jnp.minimum(jnp.maximum(averaged, 0.0), lanes_of(upper_ref, period, block))
            new_ref[period, block] = new
            second_ref[period, block] = second
            pushed = product * jnp.sum(weight * new, axis=0, keepdims=True)
            sums = jnp.where(wide, total_mass * averaged[0:1], pushed)
            second_sums = total_mass * second[0:1]
            for quarter in range(QUARTERS):
                lanes = slice(quarter * LANES, (quarter + 1) * LANES)
                chunk = block * QUARTERS + quarter
                message_ref[chunk, period : period + 1, :] = sums[:, lanes]
                message_ref[chunk, 2 + period : 3 + period, :] = second_sums[:, lanes]
    for chunk in range(RB * QUARTERS):
        message_ref[chunk, 4:5, :] = mass
        message_ref[chunk, 5:6, :] = product * mass
        message_ref[chunk, 6:8, :] = jnp.zeros((2, LANES), F32)


def reduce_kernel(got_ref, upper_ref, section_ref, before_ref, back_ref):
    devices = got_ref.shape[0]
    row = lax.broadcasted_iota(jnp.int32, (devices, devices), 0)
    column = lax.broadcasted_iota(jnp.int32, (devices, devices), 1)

    def member(section):
        span = jnp.maximum(section // ROWS, 1)
        return ((row & -span) == (column & -span)).astype(F32)

    def dot(a, b):
        return jnp.dot(a, b, precision=lax.Precision.HIGHEST, preferred_element_type=F32)

    place = pl.multiple_of(lax.axis_index("scen") * LANES, LANES)
    mass = got_ref[:, 4, :]
    moment = got_ref[:, 5, :]
    sections = (section_ref[0], section_ref[1])
    befores = (before_ref[0], section_ref[0])
    for period in range(PER):
        same = member(sections[period])
        inverse = 1.0 / dot(same, mass)
        sums = got_ref[:, period, :]
        upper = upper_ref[period : period + 1, pl.ds(place, LANES)]
        new = jnp.minimum(jnp.maximum(dot(same, sums) * inverse, 0.0), upper)
        back_ref[:, period, :] = new
        back_ref[:, 2 + period, :] = dot(same, got_ref[:, 2 + period, :]) * inverse
        back_ref[:, 6 + period, :] = dot(same, moment) * inverse
        source = jnp.where(sections[period] > ROWS, moment * new, sums)
        same = member(befores[period])
        back_ref[:, 4 + period, :] = dot(same, source) / dot(same, mass)


def row_of(returned_ref, index, block):
    parts = [
        returned_ref[block * QUARTERS + quarter, index : index + 1, :] for quarter in range(QUARTERS)
    ]
    return jnp.concatenate(parts, axis=1)


def select_kernel(returned_ref, local_ref, local_second_ref, prob_ref, section_ref, before_ref,
                  steps_ref, subtree_ref, early_ref, late_ref, second_ref, pushed_ref):
    rate, dual_rate = step_pair(steps_ref, subtree_ref)
    product = rate * dual_rate
    weight = widened(prob_column(prob_ref))
    befores = (before_ref[0], section_ref[0])
    for period in range(PER):
        out_ref = (early_ref, late_ref)[period]
        wide = section_ref[period] > ROWS
        wide_before = befores[period] > ROWS
        scale = product / group_sum(weight, befores[period])
        for block in range(RB):
            shape = (ROWS, TILE)
            row = jnp.broadcast_to(row_of(returned_ref, period, block), shape)
            new = jnp.where(wide, row, local_ref[period, block])
            out_ref[block] = new
            row = jnp.broadcast_to(row_of(returned_ref, 2 + period, block), shape)
            second_ref[period, block] = jnp.where(wide, row, local_second_ref[period, block])
            row = jnp.broadcast_to(row_of(returned_ref, 4 + period, block), shape)
            averaged = scale * group_sum(weight * new, befores[period])
            pushed_ref[period, block] = jnp.where(wide_before, row, averaged)


def push_kernel(early_ref, late_ref, pushed_ref, high_ref, low_ref, code_ref, carry_ref, restart_ref,
                image_out_ref, first_ref, next_ref, lhs_ref, image_ref):
    for period in range(PER):
        new_ref = (early_ref, late_ref)[period]
        for block in range(RB):
            first = (period * RB + block) * 2 * ROWS
            lhs_ref[first : first + ROWS, :] = new_ref[block]
            lhs_ref[first + ROWS : first + 2 * ROWS, :] = pushed_ref[period, block]
    product_images(lhs_ref, high_ref, low_ref, image_ref, False)
    for period in range(PER):
        out_ref = (first_ref, next_ref)[period]
        factor = 2.0 * damping(restart_ref, period)
        for block in range(RB):
            both = gathered_blocks(image_ref, code_ref, period, block, 2 * ROWS)
            image_out_ref[period, block] = both[:ROWS]
            out_ref[block] = factor * lanes_of(carry_ref, period, block) * both[ROWS:]


def second_kernel(early_ref, late_ref, before_ref, images_ref, second_ref, near_ref, far_ref,
                  returned_ref, square_ref, upper_ref, carry_ref, high_ref, low_ref, code_ref,
                  restart_ref, net_ref, primal_ref, early_probe_ref, late_probe_ref,
                  lhs_ref, image_ref, pulled_ref):
    for period in range(PER):
        previous_ref = (before_ref, early_ref)[period]
        damp = damping(restart_ref, period)
        for block in range(RB):
            carry = lanes_of(carry_ref, period, block)
            net = 2.0 * (images_ref[period, block] - carry * previous_ref[block])
            net_ref[period, block] = net
            first = (period * RB + block) * ROWS
            lhs_ref[first : first + ROWS, :] = damp * row_of(returned_ref, 6 + period, block) * net
    product_images(lhs_ref, high_ref, low_ref, image_ref, True)
    scattered_blocks(image_ref, code_ref, pulled_ref, ROWS)
    damp_late = damping(restart_ref, 1)
    for period in range(PER):
        new_ref = (early_ref, late_ref)[period]
        next_ref = (near_ref, far_ref)[period]
        probe_ref = (early_probe_ref, late_probe_ref)[period]
        damp = damping(restart_ref, period)
        for block in range(RB):
            if period == 0:
                carry = lanes_of(carry_ref, 1, block)
                square = damp_late * carry * carry
            else:
                square = lanes_of(square_ref, 0, block)
            first = (period * RB + block) * ROWS
            new = new_ref[block]
            primal = damp * new
            averaged = (
                primal + second_ref[period, block] - pulled_ref[first : first + ROWS, :]
                + next_ref[block]
                - 2.0 * square * row_of(returned_ref, 6 + period, block) * new
            )
            primal_new = jnp.minimum(jnp.maximum(averaged, 0.0), lanes_of(upper_ref, period, block))
            primal_ref[period, block] = primal_new
            probe_ref[block] = 2.0 * primal_new - primal


def probe_kernel(early_ref, late_ref, high_ref, low_ref, code_ref, out_ref, lhs_ref, image_ref):
    for period in range(PER):
        probe_ref = (early_ref, late_ref)[period]
        for block in range(RB):
            first = (period * RB + block) * ROWS
            lhs_ref[first : first + ROWS, :] = probe_ref[block]
    product_images(lhs_ref, high_ref, low_ref, image_ref, False)
    for period in range(PER):
        for block in range(RB):
            out_ref[period, block] = gathered_blocks(image_ref, code_ref, period, block, ROWS)


def final_kernel(image_ref, early_probe_ref, before_ref, start_ref, target_ref, net_ref,
                 early_ref, late_ref, new_ref, carry_ref, steps_ref, subtree_ref, restart_ref,
                 primal_ref, dual_ref):
    _, dual_rate = step_pair(steps_ref, subtree_ref)
    for period in range(PER):
        previous_ref = (before_ref, early_probe_ref)[period]
        first_ref = (early_ref, late_ref)[period]
        damp = damping(restart_ref, period)
        count = jnp.where(restart_ref[0, period] == 1, 1.0, 2.0).astype(F32)
        flagged = restart_ref[1, period] == 1
        share = 1.0 / (count + jnp.ones((ROWS, TILE), F32))
        for block in range(RB):
            start, target = start_ref[period, block], target_ref[period, block]
            change = dual_rate * (target - net_ref[period, block])
            carry = lanes_of(carry_ref, period, block)
            image = image_ref[period, block] - carry * previous_ref[block]
            dual_new = start + damp * change + dual_rate * (target - image)
            dual_mean = (count * (start + 0.5 * change) + dual_new) * share
            primal_new = new_ref[period, block]
            primal_mean = (count * (0.5 * first_ref[block]) + primal_new) * share
            primal = jnp.where(flagged, primal_mean, primal_new)
            dual = jnp.where(flagged, dual_mean, dual_new)
            lanes = slice(block * TILE, (block + 1) * TILE)
            for s in range(ROWS):
                primal_ref[s, period : period + 1, lanes] = primal[s : s + 1]
                dual_ref[s, period : period + 1, lanes] = dual[s : s + 1]


def per_device(
    dual_start,
    demand,
    cost,
    upper,
    carry,
    prob,
    section_size,
    block_cols,
    block_pool,
    pool_tiles,
    step_table,
    subtree_step,
    restart,
):
    rows, periods, feature = dual_start.shape
    devices = lax.axis_size("scen")
    field = (PER, RB, ROWS, TILE)
    slab = (RB, ROWS, TILE)
    tiles = (NPOOL, TILE, TILE)
    exchange = (devices, 8, LANES)
    code = (block_pool * RB + block_cols).reshape(PER * RB * NB)
    steps = (step_table, subtree_step)

    def scratch(height):
        count = PER * RB * height
        return [pltpu.VMEM((count, TILE), F32), pltpu.VMEM((NPOOL, count, TILE), F32)]

    with jax.named_scope("relayout"):
        start, target, carried = call(
            relayout_kernel, [VM] * 3 + [SM] * 3,
            [(field, F32), (field, F32), ((RB, 2 * ROWS, TILE), F32)],
        )(dual_start, demand, carry, *steps, restart)
    arriving = shifted(carried, "per", -1)
    with jax.named_scope("first_pull"):
        pulled, high, low = call(
            pull_kernel, [VM] * 3 + [SM] * 4,
            [((PER * RB * 2 * ROWS, TILE), F32), (tiles, BF16), (tiles, BF16)],
            scratch(2 * ROWS), 32,
        )(start, target, pool_tiles, code, *steps, restart)
    with jax.named_scope("local_average"):
        local, local_second, message = call(
            local_kernel, [VM] * 7 + [SM] * 5, [(field, F32), (field, F32), (exchange, F32)],
        )(pulled, start, target, arriving, cost, upper, carry, prob, section_size, *steps, restart)
    late_section, late_square, message = lax.optimization_barrier(
        (section_size[1:], carry[0:1] * carry[0:1] * jnp.where(restart[0, 0] == 1, 0.5, 1.0), message)
    )
    got = lax.all_to_all(message, "scen", 0, 0, tiled=True)
    before = shifted(late_section, "per", 1)
    square = shifted(late_square, "per", -1)
    with jax.named_scope("section_average"):
        (back,) = call(reduce_kernel, [VM] * 2 + [SM] * 2, [(exchange, F32)])(
            got, upper, section_size, before
        )
    returned = lax.all_to_all(back, "scen", 0, 0, tiled=True)
    with jax.named_scope("selected"):
        early, late, second, pushed = call(
            select_kernel, [VM] * 3 + [SM] * 5,
            [(slab, F32), (slab, F32), (field, F32), (field, F32)],
        )(returned, local, local_second, prob, section_size, before, *steps)
    new_before = shifted(late, "per", 1)
    with jax.named_scope("push"):
        images, first, near = call(
            push_kernel, [VM] * 5 + [SM] + [VM] + [SM],
            [(field, F32), (slab, F32), (slab, F32)], scratch(2 * ROWS), 32,
        )(early, late, pushed, high, low, code, carry, restart)
    far = shifted(first, "per", -1)
    with jax.named_scope("second_pull"):
        net, primal_new, early_probe, late_probe = call(
            second_kernel, [VM] * 13 + [SM] * 2,
            [(field, F32), (field, F32), (slab, F32), (slab, F32)],
            scratch(ROWS) + [pltpu.VMEM((PER * RB * ROWS, TILE), F32)], 32,
        )(early, late, new_before, images, second, near, far, returned, square, upper, carry,
          high, low, code, restart)
    probe_before = shifted(late_probe, "per", 1)
    with jax.named_scope("second_push"):
        (image,) = call(
            probe_kernel, [VM] * 4 + [SM], [(field, F32)], scratch(ROWS), 32,
        )(early_probe, late_probe, high, low, code)
    with jax.named_scope("result"):
        primal, dual = call(
            final_kernel, [VM] * 10 + [SM] * 3, [(dual_start.shape, F32), (dual_start.shape, F32)],
        )(image, early_probe, probe_before, start, target, net, early, late, primal_new, carry,
          *steps, restart)
    return primal, dual


def solution(mesh):
    return jax.shard_map(
        per_device,
        mesh=mesh,
        in_specs=(
            P("scen", "per", None),
            P("scen", "per", None),
            P("per", None),
            P("per", None),
            P("per", None),
            P("scen"),
            P("per"),
            P("per", None, None),
            P("per", None, None),
            P(),
            P(),
            P(),
            P(None, "per"),
        ),
        out_specs=(P("scen", "per", None), P("scen", "per", None)),
        check_vma=False,
    )
```

time: 390 us -> 131 us (0.34)
  waiting for transfers between devices: 138 us -> 21.6 us
  blocking collectives: 118 us -> 25.3 us
  matrix products: 40.2 us -> 0 us
  Pallas kernels: 0 us -> 22.4 us
  between operations: 14.5 us -> 1.45 us
  other arithmetic: 13.5 us -> 1.35 us
  local copies, waits for them, and re-layouts: 23.8 us -> 19.5 us
    all_gather x2 -> x0, waiting for transfers between devices: 138 us -> none  [per_device(): every_sum = lax.all_gather(device_sum[None], 'scen', axis=0, tiled=True)]
    unnamed x1 -> x0, blocking collectives: 118 us -> none
    dot_general x13 -> x0, matrix products: 40.2 us -> none  [the longest x2 11.7 us: per_device(): cross_sum = jnp.einsum('np,npr->pr', member, every_sum, precision=HIGHEST)]
    all_to_all x0 -> x1, blocking collectives: none -> 25.3 us  [per_device(): returned = lax.all_to_all(back, 'scen', 0, 0, tiled=True)]
    pallas_call x0 -> x9, Pallas kernels: none -> 22.4 us  [the longest x1 3.86 us: per_device(): call(pull_kernel, [VM] * 3 + [SM] * 4, [((PER * RB * 2 * ROWS, TILE), F32...]
    ppermute x4 -> x6, starting transfers between devices: 40.9 us -> 24.2 us  [shifted(): return lax.ppermute(block, axis, route)]
    all_to_all x0 -> x1, waiting for transfers between devices: none -> 16.1 us  [per_device(): got = lax.all_to_all(message, 'scen', 0, 0, tiled=True)]
    all_to_all x0 -> x1, starting transfers between devices: none -> 13 us  [per_device(): got = lax.all_to_all(message, 'scen', 0, 0, tiled=True)]
  transfers between devices with their start and end apart: 6 -> 7, of which waited for: 2 -> 4; matrix products, arithmetic and copies ran while one was open for 10% -> 3% of each run, Pallas kernels for 0% -> 8%
where the time goes in v2:
time: 131 us; the launch traced here: 129 us
  starting transfers between devices  37.3 us (28%)
  blocking collectives  25.3 us (19%)
  Pallas kernels  22.4 us (17%)
  waiting for transfers between devices  21.6 us (16%)
  local copies, waits for them, and re-layouts  19.5 us (15%)
  between operations  1.45 us (1%)
  other arithmetic  1.35 us (1%)
    all_to_all x1, blocking collectives, per_device(): returned = lax.all_to_all(back, 'scen', 0, 0, tiled=True)  25.3 us
    ppermute x6, starting transfers between devices, shifted(): return lax.ppermute(block, axis, route)  24.2 us
    unnamed x59, local copies, waits for them, and re-layouts  17.7 us
    all_to_all x1, waiting for transfers between devices, per_device(): got = lax.all_to_all(message, 'scen', 0, 0, tiled=True)  16.1 us
    all_to_all x1, starting transfers between devices, per_device(): got = lax.all_to_all(message, 'scen', 0, 0, tiled=True)  13 us
    ppermute x6, waiting for transfers between devices, shifted(): return lax.ppermute(block, axis, route)  5.44 us
    pallas_call x1, Pallas kernels, per_device(): call(pull_kernel, [VM] * 3 + [SM] * 4, [((PER * RB * 2 * ROWS, TILE), F32...  3.86 us
    pallas_call x1, Pallas kernels, per_device(): call(push_kernel, [VM] * 5 + [SM] + [VM] + [SM], [(field, F32), (slab, F3...  3.82 us
  transfers between devices with their start and end apart: 7, of which 4 were waited for; matrix products, arithmetic and copies ran while one was open for 3% of the time, Pallas kernels for 8%

profile of v2, /device:TPU:1, one launch (start us, length us, event | category | flops | bytes accessed | tf_op | source)
XLA Modules:
  0.0 128.9 jit_solution(17637447688231248272)
XLA Ops:
  0.6 0.8 copy.21.steps_ref
  1.4 0.8 copy-done.7
  2.2 1.0 copy-done.10
  3.3 1.0 copy-done.11
  4.3 0.7 copy-done.18
  5.0 0.7 copy-done.21
  5.7 1.7 %relayout.1 = (f32[2,16,8,512]{3,2,1,0:T(8,128)S(1)}, f32[2,16,8,512]{3,2,1,0:T(8,128)S(1)}, f32[16,16,512]{2,1,0:T(8,128)}) custom-call(f32[8,2,8192]{2,1,0:T(2,128)S(1)} %copy-done.10, f32[8,2,8192]{2,1,0:T(2,128)S(1)} %copy-done.11, f32[2,8192]{1,0:T(2,128)S(1)} %copy-done.7, f32[4,2]{1,0:T(4,128)S(1)} %copy.21.steps_ref, s32[8]{0:T(128)S(1)} %copy-done.21, ...), custom_call_target="tpu_custom_call" | custom-call | tf_op jit(solution)/shard_map/relayout/pallas_call | solution.py:392
  7.4 0.8 copy-done
  8.1 0.8 copy-done.3
  8.9 8.8 %collective-permute-start = (f32[16,16,512]{2,1,0:T(8,128)}, f32[16,16,512]{2,1,0:T(8,128)}, u32[]{:S(2)}, u32[]{:S(2)}) collective-permute-start(f32[16,16,512]{2,1,0:T(8,128)} %get-tuple-element.28), channel_id=1, source_target_pairs={{1,0},{2,1},{3,2},{4,3},{5,4},{6,5},{7,6},{9,8},{10,9},{11,10},{12... | collective-permute-start | bytes 1572872 | tf_op jit(solution)/shard_map/ppermute | solution.py:28
  17.7 0.5 slice.12
  18.7 0.6 multiply_multiply_fusion
  19.4 1.2 slice.10
  20.6 0.7 multiply_add_fusion
  21.3 0.1 copy.22
  21.4 0.1 reshape.12.code_ref
  21.5 0.0 copy-start.1
  21.5 1.0 copy-done.1
  22.5 1.0 copy-done.4
  23.6 1.9 %copy-done.6 = f32[3,512,512]{2,1,0:T(8,128)S(1)} copy-done((f32[3,512,512]{2,1,0:T(8,128)S(1)}, f32[3,512,512]{2,1,0:T(8,128)}, u32[]{:S(2)}) %copy-start.6) | copy-done | bytes 3145752
  25.5 0.7 copy-done.19
  26.2 0.7 copy-done.22
  26.8 0.0 copy-start.26
  26.8 3.9 %first_pull.1 = (f32[512,512]{1,0:T(8,128)S(1)}, bf16[3,512,512]{2,1,0:T(8,128)(2,1)S(1)}, bf16[3,512,512]{2,1,0:T(8,128)(2,1)S(1)}) custom-call(f32[2,16,8,512]{3,2,1,0:T(8,128)S(1)} %copy-done.1, f32[2,16,8,512]{3,2,1,0:T(8,128)S(1)} %copy-done.4, f32[3,512,512]{2,1,0:T(8,128)S(1)} %copy-done.6, s32[96]{0:T(128)S(1)} %reshape.12.code_ref, ...), custom_call_target="tpu_custom_call" | custom-call | tf_op jit(solution)/shard_map/first_pull/pallas_call | solution.py:398
  30.7 0.0 collective-permute-done.arriving_ref
  30.7 0.0 copy-done.8
  30.7 0.0 copy-done.9
  30.7 0.0 copy-done.17
  30.7 0.0 copy-done.24
  30.8 0.0 copy-done.26
  30.8 0.0 copy-start.23
  30.8 2.0 %local_average.1 = (f32[2,16,8,512]{3,2,1,0:T(8,128)S(1)}, f32[2,16,8,512]{3,2,1,0:T(8,128)S(1)}, f32[64,8,128]{2,1,0:T(8,128)S(1)}) custom-call(f32[512,512]{1,0:T(8,128)S(1)} %get-tuple-element.27.pulled_ref, f32[2,16,8,512]{3,2,1,0:T(8,128)S(1)} %copy-done.1, f32[2,16,8,512]{3,2,1,0:T(8,128)S(1)} %copy-done.4, ...), custom_call_target="tpu_custom_call" | custom-call | tf_op jit(solution)/shard_map/local_average/pallas_call | solution.py:404
  32.8 0.0 copy-start.12
  32.8 0.8 copy-done.12
  33.6 0.8 copy-done.14
  34.4 0.7 copy-done.16
  35.1 13.0 %all-to-all-start = ((f32[64,8,128]{2,1,0:T(8,128)}), f32[64,8,128]{2,1,0:T(8,128)S(1)}, u32[]{:S(2)}, u32[]{:S(2)}) async-start(f32[64,8,128]{2,1,0:T(8,128)} %copy-done.16), calls=%async_computation | async-start | bytes 524288 | tf_op jit(solution)/shard_map/all_to_all | solution.py:410
  48.2 3.4 %collective-permute-start.1 = (s32[1]{0:T(128)}, s32[1]{0:T(128)}, u32[]{:S(2)}, u32[]{:S(2)}) collective-permute-start(s32[1]{0:T(128)} %slice.10), channel_id=1, source_target_pairs={{0,1},{1,2},{2,3},{3,4},{4,5},{5,6},{6,7},{8,9},{9,10},{10,11},{11... | collective-permute-start | bytes 20 | tf_op jit(solution)/shard_map/ppermute | solution.py:28
  51.5 0.8 collective-permute-done.1.before_ref
  52.3 16.1 %all-to-all-done.got_ref = f32[64,8,128]{2,1,0:T(8,128)S(1)} async-done(((f32[64,8,128]{2,1,0:T(8,128)}), f32[64,8,128]{2,1,0:T(8,128)S(1)}, u32[]{:S(2)}, u32[]{:S(2)}) %all-to-all-start) | async-done | bytes 262176 | tf_op jit(solution)/shard_map/all_to_all | solution.py:410
  68.4 0.7 copy-done.25
  69.1 2.0 %section_average.1 = f32[64,8,128]{2,1,0:T(8,128)S(1)} custom-call(f32[64,8,128]{2,1,0:T(8,128)S(1)} %all-to-all-done.got_ref, f32[2,8192]{1,0:T(2,128)S(1)} %copy-done.9, s32[2]{0:T(128)S(1)} %copy-done.25, s32[1]{0:T(128)} %collective-permute-done.1.before_ref), custom_call_target="tpu_custom_call" | custom-call | tf_op jit(solution)/shard_map/section_average/pallas_call | solution.py:414
  71.1 25.3 %all_to_all.10.returned_ref = f32[64,8,128]{2,1,0:T(8,128)S(1)} all-to-all(f32[64,8,128]{2,1,0:T(8,128)S(1)} %section_average.1), channel_id=1, replica_groups=mesh['scen'=64,'per'=8] {'scen'}, dimensions={0} | all-to-all | bytes 524288 | tf_op jit(solution)/shard_map/all_to_all | solution.py:417
  96.4 0.0 copy-done.23
  96.4 1.0 copy-done.13
  97.4 1.0 copy-done.15
  98.5 0.7 copy-done.27
  99.1 1.6 %selected.1 = (f32[16,8,512]{2,1,0:T(8,128)S(1)}, f32[16,8,512]{2,1,0:T(8,128)S(1)}, f32[2,16,8,512]{3,2,1,0:T(8,128)S(1)}, f32[2,16,8,512]{3,2,1,0:T(8,128)S(1)}) custom-call(f32[64,8,128]{2,1,0:T(8,128)S(1)} %all_to_all.10.returned_ref, f32[2,16,8,512]{3,2,1,0:T(8,128)S(1)} %copy-done.13, f32[2,16,8,512]{3,2,1,0:T(8,128)S(1)} %copy-done.15, ...), custom_call_target="tpu_custom_call" | custom-call | tf_op jit(solution)/shard_map/selected/pallas_call | solution.py:419
  100.7 6.1 %collective-permute-start.2 = (f32[16,8,512]{2,1,0:T(8,128)S(1)}, f32[16,8,512]{2,1,0:T(8,128)S(1)}, u32[]{:S(2)}, u32[]{:S(2)}) collective-permute-start(f32[16,8,512]{2,1,0:T(8,128)S(1)} %get-tuple-element.35.late_ref), channel_id=1, source_target_pairs={{0,1},{1,2},{2,3},{3,4},{4,5},{5,6},{6,7},{8,9},{9,10},{10,11},{11... | collective-permute-start | bytes 786440 | tf_op jit(solution)/shard_map/ppermute | solution.py:28
  106.9 0.0 copy-done.20
  106.9 0.0 copy-start.28
  106.9 3.8 %push.1 = (f32[2,16,8,512]{3,2,1,0:T(8,128)S(1)}, f32[16,8,512]{2,1,0:T(8,128)S(1)}, f32[16,8,512]{2,1,0:T(8,128)S(1)}) custom-call(f32[16,8,512]{2,1,0:T(8,128)S(1)} %get-tuple-element.34.early_ref, f32[16,8,512]{2,1,0:T(8,128)S(1)} %get-tuple-element.35.late_ref, f32[2,16,8,512]{3,2,1,0:T(8,128)S(1)} %get-tuple-element.36.pushed_ref, ...), custom_call_target="tpu_custom_call" | custom-call | tf_op jit(solution)/shard_map/push/pallas_call | solution.py:425
  110.7 1.9 %collective-permute-start.3 = (f32[16,8,512]{2,1,0:T(8,128)S(1)}, f32[16,8,512]{2,1,0:T(8,128)S(1)}, u32[]{:S(2)}, u32[]{:S(2)}) collective-permute-start(f32[16,8,512]{2,1,0:T(8,128)S(1)} %get-tuple-element.42), channel_id=1, source_target_pairs={{1,0},{2,1},{3,2},{4,3},{5,4},{6,5},{7,6},{9,8},{10,9},{11,10},{12... | collective-permute-start | bytes 786440 | tf_op jit(solution)/shard_map/ppermute | solution.py:28
  112.7 2.1 %collective-permute-start.4 = (f32[1,8192]{1,0:T(1,128)S(1)}, f32[1,8192]{1,0:T(1,128)S(1)}, u32[]{:S(2)}, u32[]{:S(2)}) collective-permute-start(f32[1,8192]{1,0:T(1,128)S(1)} %copy-done.28), channel_id=1, source_target_pairs={{1,0},{2,1},{3,2},{4,3},{5,4},{6,5},{7,6},{9,8},{10,9},{11,10},{12... | collective-permute-start | bytes 98312 | tf_op jit(solution)/shard_map/ppermute | solution.py:28
  114.8 4.0 %collective-permute-done.4.square_ref = f32[1,8192]{1,0:T(1,128)S(1)} collective-permute-done((f32[1,8192]{1,0:T(1,128)S(1)}, f32[1,8192]{1,0:T(1,128)S(1)}, u32[]{:S(2)}, u32[]{:S(2)}) %collective-permute-start.4) | collective-permute-done | bytes 32800 | tf_op jit(solution)/shard_map/ppermute | solution.py:28
  118.8 0.0 collective-permute-done.2.before_ref
  118.8 0.0 collective-permute-done.3.far_ref
  118.8 2.8 %second_pull.1 = (f32[2,16,8,512]{3,2,1,0:T(8,128)S(1)}, f32[2,16,8,512]{3,2,1,0:T(8,128)S(1)}, f32[16,8,512]{2,1,0:T(8,128)S(1)}, f32[16,8,512]{2,1,0:T(8,128)S(1)}) custom-call(f32[16,8,512]{2,1,0:T(8,128)S(1)} %get-tuple-element.34.early_ref, f32[16,8,512]{2,1,0:T(8,128)S(1)} %get-tuple-element.35.late_ref, ...), custom_call_target="tpu_custom_call" | custom-call | tf_op jit(solution)/shard_map/second_pull/pallas_call | solution.py:431
  121.6 1.9 %collective-permute-start.5 = (f32[16,8,512]{2,1,0:T(8,128)S(1)}, f32[16,8,512]{2,1,0:T(8,128)S(1)}, u32[]{:S(2)}, u32[]{:S(2)}) collective-permute-start(f32[16,8,512]{2,1,0:T(8,128)S(1)} %get-tuple-element.45.late_ref), channel_id=1, source_target_pairs={{0,1},{1,2},{2,3},{3,4},{4,5},{5,6},{6,7},{8,9},{9,10},{10,11},{11... | collective-permute-start | bytes 786440 | tf_op jit(solution)/shard_map/ppermute | solution.py:28
  123.5 0.0 copy-start.2
  123.5 2.6 %second_push.1.image_ref = f32[2,16,8,512]{3,2,1,0:T(8,128)S(1)} custom-call(f32[16,8,512]{2,1,0:T(8,128)S(1)} %get-tuple-element.44.early_ref.early_probe_ref, f32[16,8,512]{2,1,0:T(8,128)S(1)} %get-tuple-element.45.late_ref, bf16[3,512,512]{2,1,0:T(8,128)(2,1)S(1)} %get-tuple-element.37.high_ref, bf16[3,512,512]{2,1,0:T(8,128)(2,1)S(1)} %get-tuple-element.38.low_ref, ...), custom_call_target="tpu_custom_call" | custom-call | tf_op jit(solution)/shard_map/second_push/pallas_call | solution.py:439
  126.1 0.7 collective-permute-done.5.before_ref
  126.8 0.0 copy-done.5
  126.8 2.1 %result.1 = (f32[8,2,8192]{2,1,0:T(2,128)}, f32[8,2,8192]{2,1,0:T(2,128)}) custom-call(f32[2,16,8,512]{3,2,1,0:T(8,128)S(1)} %second_push.1.image_ref, f32[16,8,512]{2,1,0:T(8,128)S(1)} %get-tuple-element.44.early_ref.early_probe_ref, f32[16,8,512]{2,1,0:T(8,128)S(1)} %collective-permute-done.5.before_ref, f32[2,16,8,512]{3,2,1,0:T(8,128)S(1)} %copy-done.2, ...), custom_call_target="tpu_custom_call" | custom-call | tf_op jit(solution)/shard_map/result/pallas_call | solution.py:443
  (25 shorter events, 0.0 us)
Async XLA Ops:
  1.4 0.8 copy-start.7
  2.2 1.0 copy-start.10
  3.3 1.0 copy-start.11
  4.3 0.7 copy-start.18
  5.0 0.7 copy-start.21
  7.3 0.8 copy-start
  8.1 0.8 copy-start.3
  8.9 21.8 %collective-permute-start = (f32[16,16,512]{2,1,0:T(8,128)}, f32[16,16,512]{2,1,0:T(8,128)}, u32[]{:S(2)}, u32[]{:S(2)}) collective-permute-start(f32[16,16,512]{2,1,0:T(8,128)} %get-tuple-element.28), channel_id=1, source_target_pairs={{1,0},{2,1},{3,2},{4,3},{5,4},{6,5},{7,6},{9,8},{10,9},{11,10},{12... | collective-permute-start | bytes 1572872 | tf_op jit(solution)/shard_map/ppermute | solution.py:28
  21.5 1.0 copy-start.1
  22.5 1.0 copy-start.4
  23.6 1.9 %copy-start.6 = (f32[3,512,512]{2,1,0:T(8,128)S(1)}, f32[3,512,512]{2,1,0:T(8,128)}, u32[]{:S(2)}) copy-start(f32[3,512,512]{2,1,0:T(8,128)} %pool_ref.1) | copy-start | bytes 9437188
  25.5 0.7 copy-start.19
  26.2 0.7 copy-start.22
  26.8 3.9 %copy-start.8 = (f32[2,8192]{1,0:T(2,128)S(1)}, f32[2,8192]{1,0:T(2,128)}, u32[]{:S(2)}) copy-start(f32[2,8192]{1,0:T(2,128)} %carry_ref.9) | copy-start | bytes 196612
  26.8 3.9 %copy-start.9 = (f32[2,8192]{1,0:T(2,128)S(1)}, f32[2,8192]{1,0:T(2,128)}, u32[]{:S(2)}) copy-start(f32[2,8192]{1,0:T(2,128)} %upper_ref.5) | copy-start | bytes 196612
  26.8 3.9 %copy-start.17 = (f32[2,8192]{1,0:T(2,128)S(1)}, f32[2,8192]{1,0:T(2,128)}, u32[]{:S(2)}) copy-start(f32[2,8192]{1,0:T(2,128)} %cost_ref.1) | copy-start | bytes 196612
  26.8 3.9 %copy-start.24 = (s32[2]{0:T(128)S(1)}, s32[2]{0:T(128)}, u32[]{:S(2)}) copy-start(s32[2]{0:T(128)} %section_ref.5) | copy-start | bytes 28
  26.8 3.9 %copy-start.26 = (f32[8]{0:T(128)S(1)}, f32[8]{0:T(128)}, u32[]{:S(2)}) copy-start(f32[8]{0:T(128)} %prob_ref.3) | copy-start | bytes 100
  30.8 65.6 %copy-start.23 = (s32[8]{0:T(128)S(1)}, s32[8]{0:T(128)}, u32[]{:S(2)}) copy-start(s32[8]{0:T(128)} %subtree_ref.9) | copy-start | bytes 100
  32.8 0.8 copy-start.12
  33.6 0.8 copy-start.14
  34.4 0.7 copy-start.16
  35.1 71.8 %copy-start.20 = (s32[2,2]{1,0:T(2,128)S(1)}, s32[2,2]{1,0:T(2,128)}, u32[]{:S(2)}) copy-start(s32[2,2]{1,0:T(2,128)} %restart_ref.11) | copy-start | bytes 52
  35.1 33.3 %all-to-all-start = ((f32[64,8,128]{2,1,0:T(8,128)}), f32[64,8,128]{2,1,0:T(8,128)S(1)}, u32[]{:S(2)}, u32[]{:S(2)}) async-start(f32[64,8,128]{2,1,0:T(8,128)} %copy-done.16), calls=%async_computation | async-start | bytes 524288 | tf_op jit(solution)/shard_map/all_to_all | solution.py:410
  48.2 4.1 %collective-permute-start.1 = (s32[1]{0:T(128)}, s32[1]{0:T(128)}, u32[]{:S(2)}, u32[]{:S(2)}) collective-permute-start(s32[1]{0:T(128)} %slice.10), channel_id=1, source_target_pairs={{0,1},{1,2},{2,3},{3,4},{4,5},{5,6},{6,7},{8,9},{9,10},{10,11},{11... | collective-permute-start | bytes 20 | tf_op jit(solution)/shard_map/ppermute | solution.py:28
  68.4 0.7 copy-start.25
  96.4 1.0 copy-start.13
  97.4 1.0 copy-start.15
  98.5 0.7 copy-start.27
  100.7 18.0 %collective-permute-start.2 = (f32[16,8,512]{2,1,0:T(8,128)S(1)}, f32[16,8,512]{2,1,0:T(8,128)S(1)}, u32[]{:S(2)}, u32[]{:S(2)}) collective-permute-start(f32[16,8,512]{2,1,0:T(8,128)S(1)} %get-tuple-element.35.late_ref), channel_id=1, source_target_pairs={{0,1},{1,2},{2,3},{3,4},{4,5},{5,6},{6,7},{8,9},{9,10},{10,11},{11... | collective-permute-start | bytes 786440 | tf_op jit(solution)/shard_map/ppermute | solution.py:28
  106.9 5.8 %copy-start.28 = (f32[1,8192]{1,0:T(1,128)S(1)}, f32[1,8192]{1,0:T(1,128)}, u32[]{:S(2)}) copy-start(f32[1,8192]{1,0:T(1,128)} %multiply_multiply_fusion) | copy-start | bytes 98308
  110.7 8.0 %collective-permute-start.3 = (f32[16,8,512]{2,1,0:T(8,128)S(1)}, f32[16,8,512]{2,1,0:T(8,128)S(1)}, u32[]{:S(2)}, u32[]{:S(2)}) collective-permute-start(f32[16,8,512]{2,1,0:T(8,128)S(1)} %get-tuple-element.42), channel_id=1, source_target_pairs={{1,0},{2,1},{3,2},{4,3},{5,4},{6,5},{7,6},{9,8},{10,9},{11,10},{12... | collective-permute-start | bytes 786440 | tf_op jit(solution)/shard_map/ppermute | solution.py:28
  112.7 6.1 %collective-permute-start.4 = (f32[1,8192]{1,0:T(1,128)S(1)}, f32[1,8192]{1,0:T(1,128)S(1)}, u32[]{:S(2)}, u32[]{:S(2)}) collective-permute-start(f32[1,8192]{1,0:T(1,128)S(1)} %copy-done.28), channel_id=1, source_target_pairs={{1,0},{2,1},{3,2},{4,3},{5,4},{6,5},{7,6},{9,8},{10,9},{11,10},{12... | collective-permute-start | bytes 98312 | tf_op jit(solution)/shard_map/ppermute | solution.py:28
  121.6 5.2 %collective-permute-start.5 = (f32[16,8,512]{2,1,0:T(8,128)S(1)}, f32[16,8,512]{2,1,0:T(8,128)S(1)}, u32[]{:S(2)}, u32[]{:S(2)}) collective-permute-start(f32[16,8,512]{2,1,0:T(8,128)S(1)} %get-tuple-element.45.late_ref), channel_id=1, source_target_pairs={{0,1},{1,2},{2,3},{3,4},{4,5},{5,6},{6,7},{8,9},{9,10},{10,11},{11... | collective-permute-start | bytes 786440 | tf_op jit(solution)/shard_map/ppermute | solution.py:28
  123.5 3.3 %copy-start.2 = (f32[2,16,8,512]{3,2,1,0:T(8,128)S(1)}, f32[2,16,8,512]{3,2,1,0:T(8,128)}, u32[]{:S(2)}) copy-start(f32[2,16,8,512]{3,2,1,0:T(8,128)} %copy-done) | copy-start | bytes 1572868
  123.5 3.3 %copy-start.5 = (f32[2,16,8,512]{3,2,1,0:T(8,128)S(1)}, f32[2,16,8,512]{3,2,1,0:T(8,128)}, u32[]{:S(2)}) copy-start(f32[2,16,8,512]{3,2,1,0:T(8,128)} %copy-done.3) | copy-start | bytes 1572868

commit v3 on v2

v3 whole, which is shorter than its diff:
```python
import jax
import jax.numpy as jnp
from jax import lax
from jax.experimental import pallas as pl
from jax.experimental.pallas import tpu as pltpu
from jax.sharding import PartitionSpec as P

TILE = 512
NPOOL = 3
NB = 3
SUBTREES = 8
RB = 16
LANES = 128
ROWS = 8
PER = 2
QUARTERS = TILE // LANES
MIB = 1 << 20
F32 = jnp.float32
BF16 = jnp.bfloat16

VM = pl.BlockSpec(memory_space=pltpu.VMEM)
SM = pl.BlockSpec(memory_space=pltpu.SMEM)
FAR = pl.BlockSpec(memory_space=pltpu.HBM)
PROB, RATE, DUAL_RATE, DAMP, FLAG, SECTION, PRODUCTS, TABLE = 0, 1, 2, 3, 5, 7, 9, 17


def shifted(block, axis, distance):
    devices = range(lax.axis_size(axis))
    route = [(i - distance, i) for i in devices if i - distance in devices]
    return lax.ppermute(block, axis, route)


def call(body, specs, outs, scratch=(), limit=4, aliases={}, places=None):
    return pl.pallas_call(
        body,
        input_output_aliases=aliases,
        out_shape=[jax.ShapeDtypeStruct(shape, dtype) for shape, dtype in outs],
        in_specs=specs,
        out_specs=places or [VM] * len(outs),
        scratch_shapes=list(scratch),
        compiler_params=pltpu.CompilerParams(vmem_limit_bytes=limit * MIB),
    )


def lanes_of(ref, row, block):
    return ref[row : row + 1, block * TILE : (block + 1) * TILE]


def widened(column):
    return jnp.concatenate([column] * QUARTERS, axis=1)


def entry_of(table_ref, index):
    return widened(table_ref[index])


def group_sum(values, inside):
    row = lax.broadcasted_iota(jnp.int32, values.shape, 0)
    for step in (1, 2, 4):
        partner = jnp.where(
            (row & step) != 0,
            pltpu.roll(values, step, 0),
            pltpu.roll(values, ROWS - step, 0),
        )
        values = jnp.where(inside > step, values + partner, values)
    return values


def halves(values):
    high = values.astype(BF16)
    return high, (values - high.astype(F32)).astype(BF16)


def product_images(lhs_ref, high_ref, low_ref, image_ref, transposed, ready=None):
    rows = lhs_ref.shape[0]
    high, low = halves(lhs_ref[...])
    both = jnp.concatenate([high, low], axis=0)
    dims = (((1,), (0,)), ((), ())) if transposed else (((1,), (1,)), ((), ()))

    def dot(a, b):
        return lax.dot_general(a, b, dims, preferred_element_type=F32)

    for j in range(NPOOL):
        if ready is not None:
            ready(j)
        main = dot(both, high_ref[j])
        image_ref[j] = main[:rows] + main[rows:] + dot(high, low_ref[j])


def gathered_blocks(image_ref, code_ref, period, block, height):
    total = None
    for k in range(NB):
        code = code_ref[(period * RB + block) * NB + k]
        first = pl.multiple_of((period * RB + code % RB) * height, height)
        part = image_ref[code // RB, pl.ds(first, height), :]
        total = part if total is None else total + part
    return total


def scattered_blocks(image_ref, code_ref, out_ref, height):
    out_ref[...] = jnp.zeros_like(out_ref)
    for period in range(PER):
        for block in range(RB):
            first = (period * RB + block) * height
            for k in range(NB):
                code = code_ref[(period * RB + block) * NB + k]
                part = image_ref[code // RB, first : first + height, :]
                place = pl.multiple_of((period * RB + code % RB) * height, height)
                out_ref[pl.ds(place, height), :] += part


def fetch(pairs, sems):
    copies = [
        pltpu.make_async_copy(source, place, sems.at[i]) for i, (source, place) in enumerate(pairs)
    ]
    for copy in copies:
        copy.start()
    return copies


def carried_kernel(dual_hbm, demand_hbm, carry_hbm, prob_hbm, section_hbm, steps_hbm, subtree_hbm,
                   restart_hbm, carried_ref, square_ref, table_ref,
                   dual_ref, demand_ref, carry_ref, prob_ref, section_ref, steps_ref, subtree_ref,
                   restart_ref, first_ref, other_ref, sems):
    copies = fetch(
        [(prob_hbm, prob_ref), (section_hbm, section_ref), (steps_hbm, steps_ref),
         (subtree_hbm, subtree_ref), (restart_hbm, restart_ref), (carry_hbm, carry_ref),
         (dual_hbm, dual_ref), (demand_hbm, demand_ref)], sems)
    for copy in copies[:6]:
        copy.wait()
    device = lax.axis_index("scen")
    share = lax.axis_size("scen") // SUBTREES
    shape = (ROWS, LANES)
    row = lax.broadcasted_iota(jnp.int32, shape, 0)
    column = jnp.zeros(shape, F32)
    for s in range(ROWS):
        column = jnp.where(row == s, prob_ref[s], column)
    entry = subtree_ref[device // share]
    rate, dual_rate = steps_ref[0, entry], steps_ref[1, entry]
    table_ref[PROB] = column
    table_ref[RATE] = jnp.full(shape, rate)
    table_ref[DUAL_RATE] = jnp.full(shape, dual_rate)
    damps = []
    for period in range(PER):
        damps.append(jnp.where(restart_ref[0, period] == 1, 0.5, 1.0).astype(F32))
        table_ref[DAMP + period] = jnp.full(shape, damps[period])
        table_ref[FLAG + period] = jnp.full(shape, restart_ref[1, period].astype(F32))
        table_ref[SECTION + period] = jnp.full(shape, section_ref[period].astype(F32))
    assert share == ROWS
    for subtree in range(SUBTREES):
        other = subtree_ref[subtree]
        value = steps_ref[0, other] * steps_ref[1, other]
        table_ref[PRODUCTS + subtree] = jnp.full(shape, value)
    carry = carry_ref[0:1, :]
    square_ref[...] = damps[0] * carry * carry
    for copy in copies[6:]:
        copy.wait()
    for s in range(ROWS):
        a, b = dual_ref[s, 0:1, :], demand_ref[s, 0:1, :]
        for block in range(RB):
            lanes = slice(block * TILE, (block + 1) * TILE)
            first_ref[block, s : s + 1, :] = a[:, lanes]
            other_ref[block, s : s + 1, :] = b[:, lanes]
    factor = damps[0] * dual_rate
    for block in range(RB):
        weight = lanes_of(carry_ref, 0, block)
        a = first_ref[block]
        carried_ref[block, 0:ROWS, :] = weight * a
        carried_ref[block, ROWS : 2 * ROWS, :] = weight * (a + factor * other_ref[block])


def pull_kernel(dual_hbm, demand_hbm, pool_hbm, carry_hbm, cost_hbm, table_ref, code_ref,
                raw_ref, high_ref, low_ref,
                dual_ref, demand_ref, pool_ref, carry_ref, cost_ref, lhs_ref, image_ref, sems):
    copies = fetch(
        [(dual_hbm, dual_ref), (demand_hbm, demand_ref)]
        + [(pool_hbm.at[j], pool_ref.at[j]) for j in range(NPOOL)]
        + [(carry_hbm, carry_ref), (cost_hbm, cost_ref)], sems)
    copies[0].wait()
    copies[1].wait()
    for period in range(PER):
        factor = table_ref[DAMP + period, 0:1, 0:1] * table_ref[DUAL_RATE, 0:1, 0:1]
        for s in range(ROWS):
            a = dual_ref[s, period : period + 1, :]
            moved = a + factor * demand_ref[s, period : period + 1, :]
            for block in range(RB):
                lanes = slice(block * TILE, (block + 1) * TILE)
                first = (period * RB + block) * 2 * ROWS + s
                lhs_ref[first : first + 1, :] = a[:, lanes]
                lhs_ref[first + ROWS : first + ROWS + 1, :] = moved[:, lanes]

    def ready(j):
        copies[2 + j].wait()
        high, low = halves(pool_ref[j])
        high_ref[j] = high
        low_ref[j] = low

    product_images(lhs_ref, high_ref, low_ref, image_ref, True, ready)
    scattered_blocks(image_ref, code_ref, raw_ref, 2 * ROWS)
    copies[5].wait()
    copies[6].wait()
    rate = jnp.concatenate([entry_of(table_ref, RATE)] * 2, axis=0)
    for period in range(PER):
        for block in range(RB):
            first = (period * RB + block) * 2 * ROWS
            here = slice(first, first + 2 * ROWS)
            value = raw_ref[here, :] - lanes_of(cost_ref, period, block)
            if period == 0:
                later = (RB + block) * 2 * ROWS
                value -= lanes_of(carry_ref, 1, block) * lhs_ref[later : later + 2 * ROWS, :]
            raw_ref[here, :] = rate * value


def local_kernel(raw_ref, arriving_ref, upper_ref, table_ref,
                 new_hbm, second_hbm, message_ref, chunk_ref, new_ref, second_ref, sems):
    place = pl.multiple_of(lax.axis_index("scen") * LANES, LANES)
    copies = []
    rate = entry_of(table_ref, RATE)
    product = rate * entry_of(table_ref, DUAL_RATE)
    weight = entry_of(table_ref, PROB)
    mass = jnp.sum(weight, axis=0, keepdims=True)
    for period in range(PER):
        section = entry_of(table_ref, SECTION + period)
        inverse = 1.0 / group_sum(weight, section)
        wide = section[0:1] > ROWS
        for block in range(RB):
            first = (period * RB + block) * 2 * ROWS
            raw = raw_ref[first : first + ROWS, :]
            other = raw_ref[first + ROWS : first + 2 * ROWS, :]
            if period == 1:
                raw -= rate * arriving_ref[block, 0:ROWS, :]
                other -= rate * arriving_ref[block, ROWS : 2 * ROWS, :]
            averaged = group_sum(weight * raw, section) * inverse
            second = group_sum(weight * other, section) * inverse
            new = jnp.minimum(jnp.maximum(averaged, 0.0), lanes_of(upper_ref, period, block))
            new_ref[period, block] = new
            second_ref[period, block] = second
            pushed = jnp.sum(product * weight * new, axis=0, keepdims=True)
            sums = jnp.where(wide, mass * averaged[0:1], pushed)
            second_sums = mass * second[0:1]
            for quarter in range(QUARTERS):
                lanes = slice(quarter * LANES, (quarter + 1) * LANES)
                chunk = block * QUARTERS + quarter
                message_ref[chunk, period : period + 1, :] = sums[:, lanes]
                message_ref[chunk, 2 + period : 3 + period, :] = second_sums[:, lanes]
        chunk_ref[period] = jnp.broadcast_to(
            upper_ref[period : period + 1, pl.ds(place, LANES)], (ROWS, LANES)
        )
        for i, (source, out) in enumerate(((new_ref, new_hbm), (second_ref, second_hbm))):
            copy = pltpu.make_async_copy(
                source.at[period], out.at[period], sems.at[2 * period + i]
            )
            copy.start()
            copies.append(copy)
    for chunk in range(RB * QUARTERS):
        message_ref[chunk, 4:5, :] = mass[:, :LANES]
    for copy in copies:
        copy.wait()


def reduce_kernel(got_ref, upper_ref, table_ref, before_ref, back_ref, mean_ref, moment_ref):
    devices = got_ref.shape[0]
    row = lax.broadcasted_iota(jnp.int32, (devices, devices), 0)
    column = lax.broadcasted_iota(jnp.int32, (devices, devices), 1)

    def member(section):
        span = jnp.maximum(section[0:1, 0:devices].astype(jnp.int32) // ROWS, 1)
        return ((row & -span) == (column & -span)).astype(F32)

    def dot(a, b):
        return jnp.dot(a, b, precision=lax.Precision.HIGHEST, preferred_element_type=F32)

    device = lax.axis_index("scen")
    mass = got_ref[:, 4, :]
    moment = mass * table_ref[PRODUCTS:TABLE].reshape(devices, LANES)
    befores = (before_ref[...], table_ref[SECTION])
    for period in range(PER):
        section = table_ref[SECTION + period]
        same = member(section)
        inverse = 1.0 / dot(same, mass)
        sums = got_ref[:, period, :]
        upper = upper_ref[period, 0:1, :]
        new = jnp.minimum(jnp.maximum(dot(same, sums) * inverse, 0.0), upper)
        back_ref[:, period, :] = new
        back_ref[:, 2 + period, :] = dot(same, got_ref[:, 2 + period, :]) * inverse
        moment_ref[...] = dot(same, moment) * inverse
        mean_ref[period] = jnp.broadcast_to(moment_ref[pl.ds(device, 1), :], (ROWS, LANES))
        source = jnp.where(section[0:1] > ROWS, moment * new, sums)
        same = member(befores[period])
        back_ref[:, 4 + period, :] = dot(same, source) / dot(same, mass)


def row_of(returned_ref, index, block):
    parts = [
        returned_ref[block * QUARTERS + quarter, index : index + 1, :] for quarter in range(QUARTERS)
    ]
    return jnp.concatenate(parts, axis=1)


def select_kernel(returned_ref, local_hbm, local_second_hbm, table_ref, before_ref,
                  early_ref, late_ref, second_ref, pushed_ref, local_ref, local_second_ref, sems):
    copies = fetch([(local_hbm, local_ref), (local_second_hbm, local_second_ref)], sems)
    for copy in copies:
        copy.wait()
    product = entry_of(table_ref, RATE) * entry_of(table_ref, DUAL_RATE)
    weight = entry_of(table_ref, PROB)
    befores = (widened(before_ref[...]), entry_of(table_ref, SECTION))
    for period in range(PER):
        out_ref = (early_ref, late_ref)[period]
        wide = entry_of(table_ref, SECTION + period) > ROWS
        wide_before = befores[period] > ROWS
        scale = product / group_sum(weight, befores[period])
        for block in range(RB):
            shape = (ROWS, TILE)
            row = jnp.broadcast_to(row_of(returned_ref, period, block), shape)
            new = jnp.where(wide, row, local_ref[period, block])
            out_ref[block] = new
            row = jnp.broadcast_to(row_of(returned_ref, 2 + period, block), shape)
            second_ref[period, block] = jnp.where(wide, row, local_second_ref[period, block])
            row = jnp.broadcast_to(row_of(returned_ref, 4 + period, block), shape)
            averaged = scale * group_sum(weight * new, befores[period])
            pushed_ref[period, block] = jnp.where(wide_before, row, averaged)


def push_kernel(early_ref, late_ref, pushed_ref, high_ref, low_ref, carry_ref, table_ref, code_ref,
                image_out_ref, first_ref, next_ref, lhs_ref, image_ref):
    for period in range(PER):
        new_ref = (early_ref, late_ref)[period]
        for block in range(RB):
            first = (period * RB + block) * 2 * ROWS
            lhs_ref[first : first + ROWS, :] = new_ref[block]
            lhs_ref[first + ROWS : first + 2 * ROWS, :] = pushed_ref[period, block]
    product_images(lhs_ref, high_ref, low_ref, image_ref, False)
    for period in range(PER):
        out_ref = (first_ref, next_ref)[period]
        factor = 2.0 * entry_of(table_ref, DAMP + period)
        for block in range(RB):
            both = gathered_blocks(image_ref, code_ref, period, block, 2 * ROWS)
            image_out_ref[period, block] = both[:ROWS]
            out_ref[block] = factor * lanes_of(carry_ref, period, block) * both[ROWS:]


def second_kernel(early_ref, late_ref, before_ref, images_ref, second_ref, near_ref, far_ref,
                  mean_ref, square_ref, upper_ref, carry_ref, high_ref, low_ref, table_ref, code_ref,
                  net_ref, primal_ref, early_probe_ref, late_probe_ref,
                  lhs_ref, image_ref, pulled_ref):
    for period in range(PER):
        previous_ref = (before_ref, early_ref)[period]
        factor = entry_of(table_ref, DAMP + period) * widened(mean_ref[period])
        for block in range(RB):
            carry = lanes_of(carry_ref, period, block)
            net = 2.0 * (images_ref[period, block] - carry * previous_ref[block])
            net_ref[period, block] = net
            first = (period * RB + block) * ROWS
            lhs_ref[first : first + ROWS, :] = factor * net
    product_images(lhs_ref, high_ref, low_ref, image_ref, True)
    scattered_blocks(image_ref, code_ref, pulled_ref, ROWS)
    for period in range(PER):
        new_ref = (early_ref, late_ref)[period]
        next_ref = (near_ref, far_ref)[period]
        probe_ref = (early_probe_ref, late_probe_ref)[period]
        damp = entry_of(table_ref, DAMP + period)
        mean = 2.0 * widened(mean_ref[period])
        if period == 0:
            mean *= entry_of(table_ref, DAMP + 1)
        for block in range(RB):
            if period == 0:
                carry = lanes_of(carry_ref, 1, block)
                square = carry * carry
            else:
                square = lanes_of(square_ref, 0, block)
            first = (period * RB + block) * ROWS
            new = new_ref[block]
            primal = damp * new
            averaged = (
                primal + second_ref[period, block] - pulled_ref[first : first + ROWS, :]
                + next_ref[block] - square * mean * new
            )
            primal_new = jnp.minimum(jnp.maximum(averaged, 0.0), lanes_of(upper_ref, period, block))
            primal_ref[period, block] = primal_new
            probe_ref[block] = 2.0 * primal_new - primal


def result_kernel(early_probe_ref, late_probe_ref, high_ref, low_ref, dual_ref, demand_ref, net_ref,
                  early_ref, late_ref, new_ref, carry_ref, table_ref, code_ref,
                  primal_ref, out_ref, lhs_ref, image_ref, start_ref, target_ref):
    for period in range(PER):
        probe_ref = (early_probe_ref, late_probe_ref)[period]
        for block in range(RB):
            first = (period * RB + block) * ROWS
            lhs_ref[first : first + ROWS, :] = probe_ref[block]
        for s in range(ROWS):
            a = dual_ref[s, period : period + 1, :]
            b = demand_ref[s, period : period + 1, :]
            for block in range(RB):
                lanes = slice(block * TILE, (block + 1) * TILE)
                start_ref[period, block, s : s + 1, :] = a[:, lanes]
                target_ref[period, block, s : s + 1, :] = b[:, lanes]
    product_images(lhs_ref, high_ref, low_ref, image_ref, False)
    dual_rate = entry_of(table_ref, DUAL_RATE)
    for period in range(PER):
        first_ref = (early_ref, late_ref)[period]
        damp = entry_of(table_ref, DAMP + period)
        count = 2.0 * damp
        flagged = entry_of(table_ref, FLAG + period) == 1.0
        share = 1.0 / (count + 1.0)
        for block in range(RB):
            start, target = start_ref[period, block], target_ref[period, block]
            change = dual_rate * (target - net_ref[period, block])
            image = gathered_blocks(image_ref, code_ref, period, block, ROWS)
            if period == 1:
                image -= lanes_of(carry_ref, 1, block) * early_probe_ref[block]
            dual_new = start + damp * change + dual_rate * (target - image)
            dual_mean = (count * (start + 0.5 * change) + dual_new) * share
            primal_new = new_ref[period, block]
            primal_mean = (count * (0.5 * first_ref[block]) + primal_new) * share
            primal = jnp.where(flagged, primal_mean, primal_new)
            dual = jnp.where(flagged, dual_mean, dual_new)
            lanes = slice(block * TILE, (block + 1) * TILE)
            for s in range(ROWS):
                primal_ref[s, period : period + 1, lanes] = primal[s : s + 1]
                out_ref[s, period : period + 1, lanes] = dual[s : s + 1]


def correct_kernel(partial_ref, before_ref, carry_ref, table_ref, out_ref):
    share = 1.0 / (2.0 * entry_of(table_ref, DAMP) + 1.0)
    factor = entry_of(table_ref, DUAL_RATE) * jnp.where(
        entry_of(table_ref, FLAG) == 1.0, share, 1.0
    )
    for block in range(RB):
        added = factor * lanes_of(carry_ref, 0, block) * before_ref[block]
        lanes = slice(block * TILE, (block + 1) * TILE)
        for s in range(ROWS):
            out_ref[s, 0:1, lanes] = partial_ref[s, 0:1, lanes] + added[s : s + 1]
            out_ref[s, 1:2, lanes] = partial_ref[s, 1:2, lanes]


def per_device(
    dual_start,
    demand,
    cost,
    upper,
    carry,
    prob,
    section_size,
    block_cols,
    block_pool,
    pool_tiles,
    step_table,
    subtree_step,
    restart,
):
    rows, periods, feature = dual_start.shape
    devices = lax.axis_size("scen")
    field = (PER, RB, ROWS, TILE)
    slab = (RB, ROWS, TILE)
    tiles = (NPOOL, TILE, TILE)
    packed = (PER, feature)
    code = (block_pool * RB + block_cols).reshape(PER * RB * NB)

    def scratch(height):
        count = PER * RB * height
        return [pltpu.VMEM((count, TILE), F32), pltpu.VMEM((NPOOL, count, TILE), F32)]

    with jax.named_scope("carried"):
        carried, square, table = call(
            carried_kernel, [FAR] * 8,
            [((RB, 2 * ROWS, TILE), F32), ((1, feature), F32), ((TABLE, ROWS, LANES), F32)],
            [pltpu.VMEM(dual_start.shape, F32), pltpu.VMEM(dual_start.shape, F32),
             pltpu.VMEM(packed, F32), pltpu.SMEM((ROWS,), F32), pltpu.SMEM((PER,), jnp.int32),
             pltpu.SMEM(step_table.shape[::-1], F32), pltpu.SMEM((SUBTREES,), jnp.int32),
             pltpu.SMEM(restart.shape, jnp.int32), pltpu.VMEM(slab, F32), pltpu.VMEM(slab, F32),
             pltpu.SemaphoreType.DMA((8,))], 60,
        )(dual_start, demand, carry, prob, section_size, step_table.T, subtree_step, restart)
    arriving = shifted(carried, "per", -1)
    with jax.named_scope("first_pull"):
        raw, high, low = call(
            pull_kernel, [FAR] * 5 + [VM, SM],
            [((PER * RB * 2 * ROWS, TILE), F32), (tiles, BF16), (tiles, BF16)],
            [pltpu.VMEM(dual_start.shape, F32), pltpu.VMEM(dual_start.shape, F32),
             pltpu.VMEM(tiles, F32), pltpu.VMEM(packed, F32), pltpu.VMEM(packed, F32)]
            + scratch(2 * ROWS) + [pltpu.SemaphoreType.DMA((7,))], 60,
        )(dual_start, demand, pool_tiles, carry, cost, table, code)
    with jax.named_scope("local_average"):
        local, local_second, message, upper_chunk = call(
            local_kernel, [VM] * 4,
            [(field, F32), (field, F32), ((devices, 5, LANES), F32), ((PER, ROWS, LANES), F32)],
            [pltpu.VMEM(field, F32), pltpu.VMEM(field, F32), pltpu.SemaphoreType.DMA((4,))],
            places=[FAR, FAR, VM, VM],
        )(raw, arriving, upper, table)
    late_section, late_square, message = lax.optimization_barrier(
        (table[SECTION + 1], square, message)
    )
    got = lax.all_to_all(message, "scen", 0, 0, tiled=True)
    before = shifted(late_section, "per", 1)
    square_next = shifted(late_square, "per", -1)
    before, square_next, got = lax.optimization_barrier((before, square_next, got))
    with jax.named_scope("section_average"):
        back, mean = call(
            reduce_kernel, [VM] * 4, [((devices, 6, LANES), F32), ((PER, ROWS, LANES), F32)],
            [pltpu.VMEM((devices, LANES), F32)],
        )(got, upper_chunk, table, before)
    returned = lax.all_to_all(back, "scen", 0, 0, tiled=True)
    with jax.named_scope("selected"):
        early, late, second, pushed = call(
            select_kernel, [VM, FAR, FAR, VM, VM],
            [(slab, F32), (slab, F32), (field, F32), (field, F32)],
            [pltpu.VMEM(field, F32), pltpu.VMEM(field, F32), pltpu.SemaphoreType.DMA((2,))],
        )(returned, local, local_second, table, before)
    new_before = shifted(late, "per", 1)
    with jax.named_scope("push"):
        images, first, near = call(
            push_kernel, [VM] * 7 + [SM], [(field, F32), (slab, F32), (slab, F32)],
            scratch(2 * ROWS), 12,
        )(early, late, pushed, high, low, carry, table, code)
    far = shifted(first, "per", -1)
    with jax.named_scope("second_pull"):
        net, primal_new, early_probe, late_probe = call(
            second_kernel, [VM] * 14 + [SM],
            [(field, F32), (field, F32), (slab, F32), (slab, F32)],
            scratch(ROWS) + [pltpu.VMEM((PER * RB * ROWS, TILE), F32)], 8,
        )(early, late, new_before, images, second, near, far, mean, square_next, upper, carry,
          high, low, table, code)
    probe_before = shifted(late_probe, "per", 1)
    with jax.named_scope("second_push"):
        primal, partial = call(
            result_kernel, [VM] * 12 + [SM], [(dual_start.shape, F32), (dual_start.shape, F32)],
            scratch(ROWS) + [pltpu.VMEM(field, F32), pltpu.VMEM(field, F32)], 8,
        )(early_probe, late_probe, high, low, dual_start, demand, net, early, late, primal_new,
          carry, table, code)
    with jax.named_scope("correction"):
        (dual,) = call(correct_kernel, [VM] * 4, [(dual_start.shape, F32)], aliases={0: 0})(
            partial, probe_before, carry, table
        )
    return primal, dual


def solution(mesh):
    return jax.shard_map(
        per_device,
        mesh=mesh,
        in_specs=(
            P("scen", "per", None),
            P("scen", "per", None),
            P("per", None),
            P("per", None),
            P("per", None),
            P("scen"),
            P("per"),
            P("per", None, None),
            P("per", None, None),
            P(),
            P(),
            P(),
            P(None, "per"),
        ),
        out_specs=(P("scen", "per", None), P("scen", "per", None)),
        check_vma=False,
    )
```

time: 131 us -> 119 us (0.908)
  local copies, waits for them, and re-layouts: 19.5 us -> 8.24 us
  Pallas kernels: 22.4 us -> 25.5 us
  waiting for transfers between devices: 21.6 us -> 19.7 us
    unnamed x59 -> x38, local copies, waits for them, and re-layouts: 17.7 us -> 7.52 us
    pallas_call x9, Pallas kernels: 22.4 us -> 25.5 us  [the longest x1 8.64 us: per_device(): call(pull_kernel, [FAR] * 5 + [VM, SM], [((PER * RB * 2 * ROWS, TILE), F3...]
    all_to_all x1, waiting for transfers between devices: 16.1 us -> 13.4 us  [per_device(): got = lax.all_to_all(message, 'scen', 0, 0, tiled=True)]
    slice x2 -> x0, local copies, waits for them, and re-layouts: 1.69 us -> none  [the longest x1 1.2 us: per_device(): section_size[1:]]
  transfers between devices with their start and end apart: 7 -> 7, of which waited for: 4 -> 3; matrix products, arithmetic and copies ran while one was open for 3% -> 1% of each run, Pallas kernels for 8% -> 14%
where the time goes in v3:
time: 119 us; the launch traced here: 118 us
  starting transfers between devices  37.5 us (32%)
  Pallas kernels  25.5 us (21%)
  blocking collectives  25.3 us (21%)
  waiting for transfers between devices  19.7 us (17%)
  local copies, waits for them, and re-layouts  8.24 us (7%)
    all_to_all x1, blocking collectives, per_device(): returned = lax.all_to_all(back, 'scen', 0, 0, tiled=True)  25.3 us
    ppermute x6, starting transfers between devices, shifted(): return lax.ppermute(block, axis, route)  24.5 us
    all_to_all x1, waiting for transfers between devices, per_device(): got = lax.all_to_all(message, 'scen', 0, 0, tiled=True)  13.4 us
    all_to_all x1, starting transfers between devices, per_device(): got = lax.all_to_all(message, 'scen', 0, 0, tiled=True)  13 us
    pallas_call x1, Pallas kernels, per_device(): call(pull_kernel, [FAR] * 5 + [VM, SM], [((PER * RB * 2 * ROWS, TILE), F3...  8.64 us
    unnamed x38, local copies, waits for them, and re-layouts  7.52 us
    ppermute x6, waiting for transfers between devices, shifted(): return lax.ppermute(block, axis, route)  6.31 us
    pallas_call x1, Pallas kernels, per_device(): call(result_kernel, [VM] * 12 + [SM], [(dual_start.shape, F32), (dual_sta...  3.92 us
  transfers between devices with their start and end apart: 7, of which 3 were waited for; matrix products, arithmetic and copies ran while one was open for 1% of the time, Pallas kernels for 14%

profile of v3, /device:TPU:1, one launch (start us, length us, event | category | flops | bytes accessed | tf_op | source)
XLA Modules:
  0.0 117.9 jit_solution(11061778221445307157)
XLA Ops:
  0.6 2.3 %carried.1 = (f32[16,16,512]{2,1,0:T(8,128)}, f32[1,8192]{1,0:T(1,128)}, f32[17,8,128]{2,1,0:T(8,128)}) custom-call(f32[8,2,8192]{2,1,0:T(2,128)} %dual_ref.1, f32[8,2,8192]{2,1,0:T(2,128)} %demand_ref.1, f32[2,8192]{1,0:T(2,128)} %carry_ref.7, f32[8]{0:T(128)} %prob_hbm.1, s32[2]{0:T(128)} %section_hbm.1, f32[2,4]{1,0:T(2,128)} %bitcast.3, s32[8]{0:T(128)} %subtree_hbm.1, ...), custom_call_target="tpu_custom_call" | custom-call | tf_op jit(solution)/shard_map/carried/pallas_call | solution.py:466
  2.9 8.8 %collective-permute-start = (f32[16,16,512]{2,1,0:T(8,128)}, f32[16,16,512]{2,1,0:T(8,128)S(1)}, u32[]{:S(2)}, u32[]{:S(2)}) collective-permute-start(f32[16,16,512]{2,1,0:T(8,128)} %get-tuple-element.36), channel_id=1, source_target_pairs={{1,0},{2,1},{3,2},{4,3},{5,4},{6,5},{7,6},{9,8},{10,9},{11,10},{12... | collective-permute-start | bytes 1572872 | tf_op jit(solution)/shard_map/ppermute | solution.py:30
  11.7 0.7 multiply_add_fusion
  12.4 0.1 copy.17
  12.5 0.6 reshape.7.code_ref
  13.2 0.0 copy-start.4
  13.2 0.0 copy-start.11
  13.2 8.6 %first_pull.1 = (f32[512,512]{1,0:T(8,128)}, bf16[3,512,512]{2,1,0:T(8,128)(2,1)}, bf16[3,512,512]{2,1,0:T(8,128)(2,1)}) custom-call(f32[8,2,8192]{2,1,0:T(2,128)} %dual_ref.1, f32[8,2,8192]{2,1,0:T(2,128)} %demand_ref.1, f32[3,512,512]{2,1,0:T(8,128)} %pool_hbm.1, f32[2,8192]{1,0:T(2,128)} %carry_ref.7, f32[2,8192]{1,0:T(2,128)} %cost_hbm.1, ...), custom_call_target="tpu_custom_call" | custom-call | tf_op jit(solution)/shard_map/first_pull/pallas_call | solution.py:477
  21.8 0.0 copy-done.4
  21.8 0.0 collective-permute-done.arriving_ref
  21.8 0.0 copy-done.11
  21.8 0.0 copy-start.6
  21.9 1.2 %copy-done.6 = f32[512,512]{1,0:T(8,128)S(1)} copy-done((f32[512,512]{1,0:T(8,128)S(1)}, f32[512,512]{1,0:T(8,128)}, u32[]{:S(2)}) %copy-start.6) | copy-done | bytes 1048600
  23.1 0.0 copy-start.1
  23.1 0.0 copy-start.16
  23.1 0.9 local_average.1
  24.0 0.0 copy-start.7
  24.0 0.8 copy-done.7
  24.8 0.0 copy-start.9
  24.8 0.8 copy-done.9
  25.6 0.0 copy-start.13
  25.6 0.7 copy-done.13
  26.3 0.0 copy-start.17
  26.3 0.6 copy-done.17
  26.9 0.0 copy-start.5
  26.9 13.0 %all-to-all-start = ((f32[64,5,128]{2,1,0:T(8,128)}), f32[64,5,128]{2,1,0:T(8,128)S(1)}, u32[]{:S(2)}, u32[]{:S(2)}) async-start(f32[64,5,128]{2,1,0:T(8,128)} %copy-done.13), calls=%async_computation | async-start | bytes 524288 | tf_op jit(solution)/shard_map/all_to_all | solution.py:494
  39.9 1.9 %collective-permute-start.2 = (f32[1,8192]{1,0:T(1,128)}, f32[1,8192]{1,0:T(1,128)S(1)}, u32[]{:S(2)}, u32[]{:S(2)}) collective-permute-start(f32[1,8192]{1,0:T(1,128)} %get-tuple-element.39), channel_id=1, source_target_pairs={{1,0},{2,1},{3,2},{4,3},{5,4},{6,5},{7,6},{9,8},{10,9},{11,10},{12... | collective-permute-start | bytes 98312 | tf_op jit(solution)/shard_map/ppermute | solution.py:30
  41.8 3.6 %collective-permute-start.1 = (f32[8,128]{1,0:T(8,128)S(1)}, f32[8,128]{1,0:T(8,128)S(1)}, u32[]{:S(2)}, u32[]{:S(2)}) collective-permute-start(f32[8,128]{1,0:T(8,128)S(1)} %slice_bitcast_fusion), channel_id=1, source_target_pairs={{0,1},{1,2},{2,3},{3,4},{4,5},{5,6},{6,7},{8,9},{9,10},{10,11},{11... | collective-permute-start | bytes 12296 | tf_op jit(solution)/shard_map/ppermute | solution.py:30
  45.5 0.7 collective-permute-done.1.before_ref
  46.2 0.0 collective-permute-done.2.square_ref
  46.2 0.0 copy-start.14
  46.2 0.6 copy-done.14
  46.8 13.4 %all-to-all-done.got_ref = f32[64,5,128]{2,1,0:T(8,128)S(1)} async-done(((f32[64,5,128]{2,1,0:T(8,128)}), f32[64,5,128]{2,1,0:T(8,128)S(1)}, u32[]{:S(2)}, u32[]{:S(2)}) %all-to-all-start) | async-done | bytes 163872 | tf_op jit(solution)/shard_map/all_to_all | solution.py:494
  60.2 0.0 copy-start.18
  60.2 0.7 copy-done.18
  60.9 0.7 section_average.1
  61.6 25.3 %all_to_all.10.returned_ref = f32[64,6,128]{2,1,0:T(8,128)S(1)} all-to-all(f32[64,6,128]{2,1,0:T(8,128)S(1)} %get-tuple-element.44), channel_id=1, replica_groups=mesh['scen'=64,'per'=8] {'scen'}, dimensions={0} | all-to-all | bytes 393216 | tf_op jit(solution)/shard_map/all_to_all | solution.py:503
  87.0 0.0 copy-start.8
  87.0 1.0 copy-done.8
  88.0 0.0 copy-start.10
  88.0 1.0 copy-done.10
  89.0 0.4 selected.1
  89.5 6.1 %collective-permute-start.3 = (f32[16,8,512]{2,1,0:T(8,128)S(1)}, f32[16,8,512]{2,1,0:T(8,128)S(1)}, u32[]{:S(2)}, u32[]{:S(2)}) collective-permute-start(f32[16,8,512]{2,1,0:T(8,128)S(1)} %get-tuple-element.48.late_ref), channel_id=1, source_target_pairs={{0,1},{1,2},{2,3},{3,4},{4,5},{5,6},{6,7},{8,9},{9,10},{10,11},{11... | collective-permute-start | bytes 786440 | tf_op jit(solution)/shard_map/ppermute | solution.py:30
  95.6 0.0 copy-done.1
  95.6 0.0 copy-done.16
  95.6 0.0 copy-done
  95.6 0.0 copy-done.5
  95.6 0.0 copy-start.12
  95.7 0.0 copy-start.15
  95.7 3.8 %push.1 = (f32[2,16,8,512]{3,2,1,0:T(8,128)S(1)}, f32[16,8,512]{2,1,0:T(8,128)S(1)}, f32[16,8,512]{2,1,0:T(8,128)S(1)}) custom-call(f32[16,8,512]{2,1,0:T(8,128)S(1)} %get-tuple-element.47.early_ref, f32[16,8,512]{2,1,0:T(8,128)S(1)} %get-tuple-element.48.late_ref, f32[2,16,8,512]{3,2,1,0:T(8,128)S(1)} %get-tuple-element.49.pushed_ref, ...), custom_call_target="tpu_custom_call" | custom-call | tf_op jit(solution)/shard_map/push/pallas_call | solution.py:512
  99.5 2.1 %collective-permute-start.4 = (f32[16,8,512]{2,1,0:T(8,128)S(1)}, f32[16,8,512]{2,1,0:T(8,128)S(1)}, u32[]{:S(2)}, u32[]{:S(2)}) collective-permute-start(f32[16,8,512]{2,1,0:T(8,128)S(1)} %get-tuple-element.55), channel_id=1, source_target_pairs={{1,0},{2,1},{3,2},{4,3},{5,4},{6,5},{7,6},{9,8},{10,9},{11,10},{12... | collective-permute-start | bytes 786440 | tf_op jit(solution)/shard_map/ppermute | solution.py:30
  101.6 0.0 collective-permute-done.3.before_ref
  101.6 5.6 %collective-permute-done.4.far_ref = f32[16,8,512]{2,1,0:T(8,128)S(1)} collective-permute-done((f32[16,8,512]{2,1,0:T(8,128)S(1)}, f32[16,8,512]{2,1,0:T(8,128)S(1)}, u32[]{:S(2)}, u32[]{:S(2)}) %collective-permute-start.4) | collective-permute-done | bytes 262176 | tf_op jit(solution)/shard_map/ppermute | solution.py:30
  107.2 0.0 copy-done.12
  107.2 0.0 copy-done.15
  107.2 0.0 copy-start.2
  107.2 0.0 copy-start.3
  107.2 2.8 %second_pull.1 = (f32[2,16,8,512]{3,2,1,0:T(8,128)S(1)}, f32[2,16,8,512]{3,2,1,0:T(8,128)S(1)}, f32[16,8,512]{2,1,0:T(8,128)S(1)}, f32[16,8,512]{2,1,0:T(8,128)S(1)}) custom-call(f32[16,8,512]{2,1,0:T(8,128)S(1)} %get-tuple-element.47.early_ref, f32[16,8,512]{2,1,0:T(8,128)S(1)} %get-tuple-element.48.late_ref, ...), custom_call_target="tpu_custom_call" | custom-call | tf_op jit(solution)/shard_map/second_pull/pallas_call | solution.py:518
  110.0 1.9 %collective-permute-start.5 = (f32[16,8,512]{2,1,0:T(8,128)S(1)}, f32[16,8,512]{2,1,0:T(8,128)S(1)}, u32[]{:S(2)}, u32[]{:S(2)}) collective-permute-start(f32[16,8,512]{2,1,0:T(8,128)S(1)} %get-tuple-element.59.late_probe_ref), channel_id=1, source_target_pairs={{0,1},{1,2},{2,3},{3,4},{4,5},{5,6},{6,7},{8,9},{9,10},{10,11},{11... | collective-permute-start | bytes 786440 | tf_op jit(solution)/shard_map/ppermute | solution.py:30
  111.9 0.0 copy-done.2
  111.9 0.0 copy-done.3
  112.0 3.9 %second_push.1 = (f32[8,2,8192]{2,1,0:T(2,128)}, f32[8,2,8192]{2,1,0:T(2,128)}) custom-call(f32[16,8,512]{2,1,0:T(8,128)S(1)} %get-tuple-element.58.early_probe_ref, f32[16,8,512]{2,1,0:T(8,128)S(1)} %get-tuple-element.59.late_probe_ref, bf16[3,512,512]{2,1,0:T(8,128)(2,1)S(1)} %copy-done, bf16[3,512,512]{2,1,0:T(8,128)(2,1)S(1)} %copy-done.1, ...), custom_call_target="tpu_custom_call" | custom-call | tf_op jit(solution)/shard_map/second_push/pallas_call | solution.py:526
  115.9 0.0 collective-permute-done.5.before_ref
  115.9 2.0 %correction.1 = f32[8,2,8192]{2,1,0:T(2,128)} custom-call(f32[8,2,8192]{2,1,0:T(2,128)} %get-tuple-element.63.partial_ref, f32[16,8,512]{2,1,0:T(8,128)S(1)} %collective-permute-done.5.before_ref, f32[2,8192]{1,0:T(2,128)S(1)} %copy-done.5, f32[17,8,128]{2,1,0:T(8,128)S(1)} %copy-done.4), custom_call_target="tpu_custom_call", output_to_operand_aliasing={{}: (0, {})} | custom-call | tf_op jit(solution)/shard_map/correction/pallas_call | solution.py:532
  (2 shorter events, 0.0 us)
Async XLA Ops:
  2.9 18.9 %collective-permute-start = (f32[16,16,512]{2,1,0:T(8,128)}, f32[16,16,512]{2,1,0:T(8,128)S(1)}, u32[]{:S(2)}, u32[]{:S(2)}) collective-permute-start(f32[16,16,512]{2,1,0:T(8,128)} %get-tuple-element.36), channel_id=1, source_target_pairs={{1,0},{2,1},{3,2},{4,3},{5,4},{6,5},{7,6},{9,8},{10,9},{11,10},{12... | collective-permute-start | bytes 1572872 | tf_op jit(solution)/shard_map/ppermute | solution.py:30
  13.2 8.7 %copy-start.4 = (f32[17,8,128]{2,1,0:T(8,128)S(1)}, f32[17,8,128]{2,1,0:T(8,128)}, u32[]{:S(2)}) copy-start(f32[17,8,128]{2,1,0:T(8,128)} %get-tuple-element.33.table_ref) | copy-start | bytes 208900
  13.2 8.7 %copy-start.11 = (f32[2,8192]{1,0:T(2,128)S(1)}, f32[2,8192]{1,0:T(2,128)}, u32[]{:S(2)}) copy-start(f32[2,8192]{1,0:T(2,128)} %upper_ref.3) | copy-start | bytes 196612
  21.8 1.2 %copy-start.6 = (f32[512,512]{1,0:T(8,128)S(1)}, f32[512,512]{1,0:T(8,128)}, u32[]{:S(2)}) copy-start(f32[512,512]{1,0:T(8,128)} %get-tuple-element.35.raw_ref) | copy-start | bytes 3145732
  23.1 72.5 %copy-start.1 = (bf16[3,512,512]{2,1,0:T(8,128)(2,1)S(1)}, bf16[3,512,512]{2,1,0:T(8,128)(2,1)}, u32[]{:S(2)}) copy-start(bf16[3,512,512]{2,1,0:T(8,128)(2,1)} %get-tuple-element.51.low_ref) | copy-start | bytes 4718596
  23.1 72.5 %copy-start.16 = (s32[96]{0:T(128)S(1)}, s32[96]{0:T(128)}, u32[]{:S(2)}) copy-start(s32[96]{0:T(128)} %reshape.7.code_ref) | copy-start | bytes 1156
  24.0 0.8 copy-start.7
  24.8 0.8 copy-start.9
  25.6 0.7 copy-start.13
  26.3 0.6 copy-start.17
  26.9 68.8 %copy-start = (bf16[3,512,512]{2,1,0:T(8,128)(2,1)S(1)}, bf16[3,512,512]{2,1,0:T(8,128)(2,1)}, u32[]{:S(2)}) copy-start(bf16[3,512,512]{2,1,0:T(8,128)(2,1)} %get-tuple-element.50.high_ref) | copy-start | bytes 4718596
  26.9 68.8 %copy-start.5 = (f32[2,8192]{1,0:T(2,128)S(1)}, f32[2,8192]{1,0:T(2,128)}, u32[]{:S(2)}) copy-start(f32[2,8192]{1,0:T(2,128)} %carry_ref.7) | copy-start | bytes 196612
  26.9 33.3 %all-to-all-start = ((f32[64,5,128]{2,1,0:T(8,128)}), f32[64,5,128]{2,1,0:T(8,128)S(1)}, u32[]{:S(2)}, u32[]{:S(2)}) async-start(f32[64,5,128]{2,1,0:T(8,128)} %copy-done.13), calls=%async_computation | async-start | bytes 524288 | tf_op jit(solution)/shard_map/all_to_all | solution.py:494
  39.9 6.3 %collective-permute-start.2 = (f32[1,8192]{1,0:T(1,128)}, f32[1,8192]{1,0:T(1,128)S(1)}, u32[]{:S(2)}, u32[]{:S(2)}) collective-permute-start(f32[1,8192]{1,0:T(1,128)} %get-tuple-element.39), channel_id=1, source_target_pairs={{1,0},{2,1},{3,2},{4,3},{5,4},{6,5},{7,6},{9,8},{10,9},{11,10},{12... | collective-permute-start | bytes 98312 | tf_op jit(solution)/shard_map/ppermute | solution.py:30
  41.8 4.4 %collective-permute-start.1 = (f32[8,128]{1,0:T(8,128)S(1)}, f32[8,128]{1,0:T(8,128)S(1)}, u32[]{:S(2)}, u32[]{:S(2)}) collective-permute-start(f32[8,128]{1,0:T(8,128)S(1)} %slice_bitcast_fusion), channel_id=1, source_target_pairs={{0,1},{1,2},{2,3},{3,4},{4,5},{5,6},{6,7},{8,9},{9,10},{10,11},{11... | collective-permute-start | bytes 12296 | tf_op jit(solution)/shard_map/ppermute | solution.py:30
  46.2 0.6 copy-start.14
  60.2 0.7 copy-start.18
  87.0 1.0 copy-start.8
  88.0 1.0 copy-start.10
  89.5 12.1 %collective-permute-start.3 = (f32[16,8,512]{2,1,0:T(8,128)S(1)}, f32[16,8,512]{2,1,0:T(8,128)S(1)}, u32[]{:S(2)}, u32[]{:S(2)}) collective-permute-start(f32[16,8,512]{2,1,0:T(8,128)S(1)} %get-tuple-element.48.late_ref), channel_id=1, source_target_pairs={{0,1},{1,2},{2,3},{3,4},{4,5},{5,6},{6,7},{8,9},{9,10},{10,11},{11... | collective-permute-start | bytes 786440 | tf_op jit(solution)/shard_map/ppermute | solution.py:30
  95.6 11.5 %copy-start.12 = (f32[2,8192]{1,0:T(2,128)S(1)}, f32[2,8192]{1,0:T(2,128)}, u32[]{:S(2)}) copy-start(f32[2,8192]{1,0:T(2,128)} %upper_ref.3) | copy-start | bytes 196612
  95.7 11.5 %copy-start.15 = (f32[1,8192]{1,0:T(1,128)S(1)}, f32[1,8192]{1,0:T(1,128)}, u32[]{:S(2)}) copy-start(f32[1,8192]{1,0:T(1,128)} %copy-done.14) | copy-start | bytes 98308
  99.5 7.7 %collective-permute-start.4 = (f32[16,8,512]{2,1,0:T(8,128)S(1)}, f32[16,8,512]{2,1,0:T(8,128)S(1)}, u32[]{:S(2)}, u32[]{:S(2)}) collective-permute-start(f32[16,8,512]{2,1,0:T(8,128)S(1)} %get-tuple-element.55), channel_id=1, source_target_pairs={{1,0},{2,1},{3,2},{4,3},{5,4},{6,5},{7,6},{9,8},{10,9},{11,10},{12... | collective-permute-start | bytes 786440 | tf_op jit(solution)/shard_map/ppermute | solution.py:30
  107.2 4.8 %copy-start.2 = (f32[8,2,8192]{2,1,0:T(2,128)S(1)}, f32[8,2,8192]{2,1,0:T(2,128)}, u32[]{:S(2)}) copy-start(f32[8,2,8192]{2,1,0:T(2,128)} %dual_ref.1) | copy-start | bytes 1572868
  107.2 4.8 %copy-start.3 = (f32[8,2,8192]{2,1,0:T(2,128)S(1)}, f32[8,2,8192]{2,1,0:T(2,128)}, u32[]{:S(2)}) copy-start(f32[8,2,8192]{2,1,0:T(2,128)} %demand_ref.1) | copy-start | bytes 1572868
  110.0 5.9 %collective-permute-start.5 = (f32[16,8,512]{2,1,0:T(8,128)S(1)}, f32[16,8,512]{2,1,0:T(8,128)S(1)}, u32[]{:S(2)}, u32[]{:S(2)}) collective-permute-start(f32[16,8,512]{2,1,0:T(8,128)S(1)} %get-tuple-element.59.late_probe_ref), channel_id=1, source_target_pairs={{0,1},{1,2},{2,3},{3,4},{4,5},{5,6},{6,7},{8,9},{9,10},{10,11},{11... | collective-permute-start | bytes 786440 | tf_op jit(solution)/shard_map/ppermute | solution.py:30

commit v4 on v3

--- a/solution.py
+++ b/solution.py
@@ -30,14 +30,16 @@
     return lax.ppermute(block, axis, route)
 
 
-def call(body, specs, outs, scratch=(), limit=4, aliases={}, places=None):
+def call(body, specs, outs, scratch=(), limit=4, places=None, work=0):
     return pl.pallas_call(
         body,
-        input_output_aliases=aliases,
         out_shape=[jax.ShapeDtypeStruct(shape, dtype) for shape, dtype in outs],
         in_specs=specs,
         out_specs=places or [VM] * len(outs),
         scratch_shapes=list(scratch),
+        cost_estimate=pl.CostEstimate(
+            flops=work, bytes_accessed=work // 256, transcendentals=0
+        ) if work else None,
         compiler_params=pltpu.CompilerParams(vmem_limit_bytes=limit * MIB),
     )
 
@@ -87,25 +89,29 @@
         image_ref[j] = main[:rows] + main[rows:] + dot(high, low_ref[j])
 
 
-def gathered_blocks(image_ref, code_ref, period, block, height):
+def code_of(code_refs, period, block, k):
+    return tuple(ref[k, period, block] for ref in code_refs)
+
+
+def gathered_blocks(image_ref, code_refs, period, block, height):
     total = None
     for k in range(NB):
-        code = code_ref[(period * RB + block) * NB + k]
-        first = pl.multiple_of((period * RB + code % RB) * height, height)
-        part = image_ref[code // RB, pl.ds(first, height), :]
+        which, place = code_of(code_refs, period, block, k)
+        first = pl.multiple_of((period * RB + place) * height, height)
+        part = image_ref[which, pl.ds(first, height), :]
         total = part if total is None else total + part
     return total
 
 
-def scattered_blocks(image_ref, code_ref, out_ref, height):
+def scattered_blocks(image_ref, code_refs, out_ref, height):
     out_ref[...] = jnp.zeros_like(out_ref)
     for period in range(PER):
         for block in range(RB):
             first = (period * RB + block) * height
             for k in range(NB):
-                code = code_ref[(period * RB + block) * NB + k]
-                part = image_ref[code // RB, first : first + height, :]
-                place = pl.multiple_of((period * RB + code % RB) * height, height)
+                which, column = code_of(code_refs, period, block, k)
+                part = image_ref[which, first : first + height, :]
+                place = pl.multiple_of((period * RB + column) * height, height)
                 out_ref[pl.ds(place, height), :] += part
 
 
@@ -119,7 +125,7 @@
 
 
 def carried_kernel(dual_hbm, demand_hbm, carry_hbm, prob_hbm, section_hbm, steps_hbm, subtree_hbm,
-                   restart_hbm, carried_ref, square_ref, table_ref,
+                   restart_hbm, carried_ref, late_ref, table_ref,
                    dual_ref, demand_ref, carry_ref, prob_ref, section_ref, steps_ref, subtree_ref,
                    restart_ref, first_ref, other_ref, sems):
     copies = fetch(
@@ -151,8 +157,7 @@
         other = subtree_ref[subtree]
         value = steps_ref[0, other] * steps_ref[1, other]
         table_ref[PRODUCTS + subtree] = jnp.full(shape, value)
-    carry = carry_ref[0:1, :]
-    square_ref[...] = damps[0] * carry * carry
+    late_ref[...] = table_ref[SECTION + 1]
     for copy in copies[6:]:
         copy.wait()
     for s in range(ROWS):
@@ -169,13 +174,15 @@
         carried_ref[block, ROWS : 2 * ROWS, :] = weight * (a + factor * other_ref[block])
 
 
-def pull_kernel(dual_hbm, demand_hbm, pool_hbm, carry_hbm, cost_hbm, table_ref, code_ref,
-                raw_ref, high_ref, low_ref,
-                dual_ref, demand_ref, pool_ref, carry_ref, cost_ref, lhs_ref, image_ref, sems):
+def pull_kernel(dual_hbm, demand_hbm, pool_hbm, carry_hbm, cost_hbm, cols_hbm, which_hbm, table_ref,
+                raw_ref, high_hbm, low_hbm, dual_ref, demand_ref, pool_ref, carry_ref, cost_ref,
+                cols_ref, which_ref, high_ref, low_ref, lhs_ref, image_ref, sems, out_sems):
     copies = fetch(
         [(dual_hbm, dual_ref), (demand_hbm, demand_ref)]
         + [(pool_hbm.at[j], pool_ref.at[j]) for j in range(NPOOL)]
-        + [(carry_hbm, carry_ref), (cost_hbm, cost_ref)], sems)
+        + [(carry_hbm, carry_ref), (cost_hbm, cost_ref), (cols_hbm, cols_ref),
+           (which_hbm, which_ref)], sems)
+    written = []
     copies[0].wait()
     copies[1].wait()
     for period in range(PER):
@@ -194,11 +201,15 @@
         high, low = halves(pool_ref[j])
         high_ref[j] = high
         low_ref[j] = low
+        for i, (source, out) in enumerate(((high_ref, high_hbm), (low_ref, low_hbm))):
+            copy = pltpu.make_async_copy(source.at[j], out.at[j], out_sems.at[2 * j + i])
+            copy.start()
+            written.append(copy)
 
     product_images(lhs_ref, high_ref, low_ref, image_ref, True, ready)
-    scattered_blocks(image_ref, code_ref, raw_ref, 2 * ROWS)
-    copies[5].wait()
-    copies[6].wait()
+    for copy in copies[5:]:
+        copy.wait()
+    scattered_blocks(image_ref, (which_ref, cols_ref), raw_ref, 2 * ROWS)
     rate = jnp.concatenate([entry_of(table_ref, RATE)] * 2, axis=0)
     for period in range(PER):
         for block in range(RB):
@@ -209,12 +220,14 @@
                 later = (RB + block) * 2 * ROWS
                 value -= lanes_of(carry_ref, 1, block) * lhs_ref[later : later + 2 * ROWS, :]
             raw_ref[here, :] = rate * value
-
-
-def local_kernel(raw_ref, arriving_ref, upper_ref, table_ref,
-                 new_hbm, second_hbm, message_ref, chunk_ref, new_ref, second_ref, sems):
+    for copy in written:
+        copy.wait()
+
+
+def local_kernel(raw_ref, arriving_ref, upper_ref, table_ref, before_ref,
+                 kept_ref, message_ref, chunk_ref):
     place = pl.multiple_of(lax.axis_index("scen") * LANES, LANES)
-    copies = []
+    chunk_ref[PER] = before_ref[...]
     rate = entry_of(table_ref, RATE)
     product = rate * entry_of(table_ref, DUAL_RATE)
     weight = entry_of(table_ref, PROB)
@@ -233,8 +246,8 @@
             averaged = group_sum(weight * raw, section) * inverse
             second = group_sum(weight * other, section) * inverse
             new = jnp.minimum(jnp.maximum(averaged, 0.0), lanes_of(upper_ref, period, block))
-            new_ref[period, block] = new
-            second_ref[period, block] = second
+            kept_ref[0, period, block] = new
+            kept_ref[1, period, block] = second
             pushed = jnp.sum(product * weight * new, axis=0, keepdims=True)
             sums = jnp.where(wide, mass * averaged[0:1], pushed)
             second_sums = mass * second[0:1]
@@ -246,19 +259,11 @@
         chunk_ref[period] = jnp.broadcast_to(
             upper_ref[period : period + 1, pl.ds(place, LANES)], (ROWS, LANES)
         )
-        for i, (source, out) in enumerate(((new_ref, new_hbm), (second_ref, second_hbm))):
-            copy = pltpu.make_async_copy(
-                source.at[period], out.at[period], sems.at[2 * period + i]
-            )
-            copy.start()
-            copies.append(copy)
     for chunk in range(RB * QUARTERS):
         message_ref[chunk, 4:5, :] = mass[:, :LANES]
-    for copy in copies:
-        copy.wait()
-
-
-def reduce_kernel(got_ref, upper_ref, table_ref, before_ref, back_ref, mean_ref, moment_ref):
+
+
+def reduce_kernel(got_ref, chunk_ref, table_ref, back_ref, mean_ref, moment_ref):
     devices = got_ref.shape[0]
     row = lax.broadcasted_iota(jnp.int32, (devices, devices), 0)
     column = lax.broadcasted_iota(jnp.int32, (devices, devices), 1)
@@ -273,13 +278,13 @@
     device = lax.axis_index("scen")
     mass = got_ref[:, 4, :]
     moment = mass * table_ref[PRODUCTS:TABLE].reshape(devices, LANES)
-    befores = (before_ref[...], table_ref[SECTION])
+    befores = (chunk_ref[PER], table_ref[SECTION])
     for period in range(PER):
         section = table_ref[SECTION + period]
         same = member(section)
         inverse = 1.0 / dot(same, mass)
         sums = got_ref[:, period, :]
-        upper = upper_ref[period, 0:1, :]
+        upper = chunk_ref[period, 0:1, :]
         new = jnp.minimum(jnp.maximum(dot(same, sums) * inverse, 0.0), upper)
         back_ref[:, period, :] = new
         back_ref[:, 2 + period, :] = dot(same, got_ref[:, 2 + period, :]) * inverse
@@ -297,14 +302,11 @@
     return jnp.concatenate(parts, axis=1)
 
 
-def select_kernel(returned_ref, local_hbm, local_second_hbm, table_ref, before_ref,
-                  early_ref, late_ref, second_ref, pushed_ref, local_ref, local_second_ref, sems):
-    copies = fetch([(local_hbm, local_ref), (local_second_hbm, local_second_ref)], sems)
-    for copy in copies:
-        copy.wait()
+def select_kernel(returned_ref, kept_ref, table_ref, chunk_ref,
+                  early_ref, late_ref, second_ref, pushed_ref):
     product = entry_of(table_ref, RATE) * entry_of(table_ref, DUAL_RATE)
     weight = entry_of(table_ref, PROB)
-    befores = (widened(before_ref[...]), entry_of(table_ref, SECTION))
+    befores = (entry_of(chunk_ref, PER), entry_of(table_ref, SECTION))
     for period in range(PER):
         out_ref = (early_ref, late_ref)[period]
         wide = entry_of(table_ref, SECTION + period) > ROWS
@@ -313,17 +315,20 @@
         for block in range(RB):
             shape = (ROWS, TILE)
             row = jnp.broadcast_to(row_of(returned_ref, period, block), shape)
-            new = jnp.where(wide, row, local_ref[period, block])
+            new = jnp.where(wide, row, kept_ref[0, period, block])
             out_ref[block] = new
             row = jnp.broadcast_to(row_of(returned_ref, 2 + period, block), shape)
-            second_ref[period, block] = jnp.where(wide, row, local_second_ref[period, block])
+            second_ref[period, block] = jnp.where(wide, row, kept_ref[1, period, block])
             row = jnp.broadcast_to(row_of(returned_ref, 4 + period, block), shape)
             averaged = scale * group_sum(weight * new, befores[period])
             pushed_ref[period, block] = jnp.where(wide_before, row, averaged)
 
 
-def push_kernel(early_ref, late_ref, pushed_ref, high_ref, low_ref, carry_ref, table_ref, code_ref,
-                image_out_ref, first_ref, next_ref, lhs_ref, image_ref):
+def push_kernel(early_ref, late_ref, pushed_ref, high_ref, low_ref, carry_ref, table_ref,
+                cols_hbm, which_hbm, image_out_ref, first_ref, next_ref, lhs_ref, image_ref,
+                cols_ref, which_ref, sems):
+    copies = fetch([(cols_hbm, cols_ref), (which_hbm, which_ref)], sems)
+    code_refs = which_ref, cols_ref
     for period in range(PER):
         new_ref = (early_ref, late_ref)[period]
         for block in range(RB):
@@ -331,19 +336,27 @@
             lhs_ref[first : first + ROWS, :] = new_ref[block]
             lhs_ref[first + ROWS : first + 2 * ROWS, :] = pushed_ref[period, block]
     product_images(lhs_ref, high_ref, low_ref, image_ref, False)
+    for copy in copies:
+        copy.wait()
     for period in range(PER):
         out_ref = (first_ref, next_ref)[period]
         factor = 2.0 * entry_of(table_ref, DAMP + period)
         for block in range(RB):
-            both = gathered_blocks(image_ref, code_ref, period, block, 2 * ROWS)
+            both = gathered_blocks(image_ref, code_refs, period, block, 2 * ROWS)
             image_out_ref[period, block] = both[:ROWS]
-            out_ref[block] = factor * lanes_of(carry_ref, period, block) * both[ROWS:]
+            carry = lanes_of(carry_ref, period, block)
+            out_ref[block] = factor * carry * both[ROWS:]
+            if period == 0:
+                row = block % ROWS
+                out_ref[RB + block // ROWS, row : row + 1, :] = 0.5 * factor[0:1] * carry * carry
 
 
 def second_kernel(early_ref, late_ref, before_ref, images_ref, second_ref, near_ref, far_ref,
-                  mean_ref, square_ref, upper_ref, carry_ref, high_ref, low_ref, table_ref, code_ref,
+                  mean_ref, upper_ref, carry_ref, high_ref, low_ref, table_ref, cols_hbm, which_hbm,
                   net_ref, primal_ref, early_probe_ref, late_probe_ref,
-                  lhs_ref, image_ref, pulled_ref):
+                  pulled_ref, lhs_ref, image_ref, cols_ref, which_ref, sems):
+    copies = fetch([(cols_hbm, cols_ref), (which_hbm, which_ref)], sems)
+    code_refs = which_ref, cols_ref
     for period in range(PER):
         previous_ref = (before_ref, early_ref)[period]
         factor = entry_of(table_ref, DAMP + period) * widened(mean_ref[period])
@@ -354,7 +367,9 @@
             first = (period * RB + block) * ROWS
             lhs_ref[first : first + ROWS, :] = factor * net
     product_images(lhs_ref, high_ref, low_ref, image_ref, True)
-    scattered_blocks(image_ref, code_ref, pulled_ref, ROWS)
+    for copy in copies:
+        copy.wait()
+    scattered_blocks(image_ref, code_refs, pulled_ref, ROWS)
     for period in range(PER):
         new_ref = (early_ref, late_ref)[period]
         next_ref = (near_ref, far_ref)[period]
@@ -368,7 +383,8 @@
                 carry = lanes_of(carry_ref, 1, block)
                 square = carry * carry
             else:
-                square = lanes_of(square_ref, 0, block)
+                row = block % ROWS
+                square = far_ref[RB + block // ROWS, row : row + 1, :]
             first = (period * RB + block) * ROWS
             new = new_ref[block]
             primal = damp * new
@@ -382,8 +398,11 @@
 
 
 def result_kernel(early_probe_ref, late_probe_ref, high_ref, low_ref, dual_ref, demand_ref, net_ref,
-                  early_ref, late_ref, new_ref, carry_ref, table_ref, code_ref,
-                  primal_ref, out_ref, lhs_ref, image_ref, start_ref, target_ref):
+                  early_ref, late_ref, new_ref, carry_ref, table_ref, cols_hbm, which_hbm,
+                  primal_ref, out_ref, start_ref, target_ref, lhs_ref, image_ref,
+                  cols_ref, which_ref, sems):
+    copies = fetch([(cols_hbm, cols_ref), (which_hbm, which_ref)], sems)
+    code_refs = which_ref, cols_ref
     for period in range(PER):
         probe_ref = (early_probe_ref, late_probe_ref)[period]
         for block in range(RB):
@@ -397,6 +416,8 @@
                 start_ref[period, block, s : s + 1, :] = a[:, lanes]
                 target_ref[period, block, s : s + 1, :] = b[:, lanes]
     product_images(lhs_ref, high_ref, low_ref, image_ref, False)
+    for copy in copies:
+        copy.wait()
     dual_rate = entry_of(table_ref, DUAL_RATE)
     for period in range(PER):
         first_ref = (early_ref, late_ref)[period]
@@ -407,7 +428,7 @@
         for block in range(RB):
             start, target = start_ref[period, block], target_ref[period, block]
             change = dual_rate * (target - net_ref[period, block])
-            image = gathered_blocks(image_ref, code_ref, period, block, ROWS)
+            image = gathered_blocks(image_ref, code_refs, period, block, ROWS)
             if period == 1:
                 image -= lanes_of(carry_ref, 1, block) * early_probe_ref[block]
             dual_new = start + damp * change + dual_rate * (target - image)
@@ -422,17 +443,24 @@
                 out_ref[s, period : period + 1, lanes] = dual[s : s + 1]
 
 
-def correct_kernel(partial_ref, before_ref, carry_ref, table_ref, out_ref):
+def correct_kernel(partial_ref, before_ref, carry_ref, table_ref, out_hbm, out_ref, added_ref, sems):
     share = 1.0 / (2.0 * entry_of(table_ref, DAMP) + 1.0)
     factor = entry_of(table_ref, DUAL_RATE) * jnp.where(
         entry_of(table_ref, FLAG) == 1.0, share, 1.0
     )
     for block in range(RB):
-        added = factor * lanes_of(carry_ref, 0, block) * before_ref[block]
-        lanes = slice(block * TILE, (block + 1) * TILE)
-        for s in range(ROWS):
-            out_ref[s, 0:1, lanes] = partial_ref[s, 0:1, lanes] + added[s : s + 1]
-            out_ref[s, 1:2, lanes] = partial_ref[s, 1:2, lanes]
+        added_ref[:, block * TILE : (block + 1) * TILE] = (
+            factor * lanes_of(carry_ref, 0, block) * before_ref[block]
+        )
+    copies = []
+    for s in range(ROWS):
+        out_ref[s, 0:1, :] = partial_ref[s, 0:1, :] + added_ref[s : s + 1, :]
+        out_ref[s, 1:2, :] = partial_ref[s, 1:2, :]
+        copy = pltpu.make_async_copy(out_ref.at[s], out_hbm.at[s], sems.at[s])
+        copy.start()
+        copies.append(copy)
+    for copy in copies:
+        copy.wait()
 
 
 def per_device(
@@ -456,16 +484,22 @@
     slab = (RB, ROWS, TILE)
     tiles = (NPOOL, TILE, TILE)
     packed = (PER, feature)
-    code = (block_pool * RB + block_cols).reshape(PER * RB * NB)
 
     def scratch(height):
         count = PER * RB * height
         return [pltpu.VMEM((count, TILE), F32), pltpu.VMEM((NPOOL, count, TILE), F32)]
 
+    codes = (block_cols.transpose(2, 0, 1), block_pool.transpose(2, 0, 1))
+    code_scratch = [
+        pltpu.SMEM((NB, PER, RB), jnp.int32), pltpu.SMEM((NB, PER, RB), jnp.int32),
+        pltpu.SemaphoreType.DMA((2,)),
+    ]
+    heavy = 2 * 3 * NPOOL * TILE * TILE * PER * RB * ROWS
+
     with jax.named_scope("carried"):
-        carried, square, table = call(
+        carried, late_section, table = call(
             carried_kernel, [FAR] * 8,
-            [((RB, 2 * ROWS, TILE), F32), ((1, feature), F32), ((TABLE, ROWS, LANES), F32)],
+            [((RB, 2 * ROWS, TILE), F32), ((ROWS, LANES), F32), ((TABLE, ROWS, LANES), F32)],
             [pltpu.VMEM(dual_start.shape, F32), pltpu.VMEM(dual_start.shape, F32),
              pltpu.VMEM(packed, F32), pltpu.SMEM((ROWS,), F32), pltpu.SMEM((PER,), jnp.int32),
              pltpu.SMEM(step_table.shape[::-1], F32), pltpu.SMEM((SUBTREES,), jnp.int32),
@@ -473,65 +507,64 @@
              pltpu.SemaphoreType.DMA((8,))], 60,
         )(dual_start, demand, carry, prob, section_size, step_table.T, subtree_step, restart)
     arriving = shifted(carried, "per", -1)
+    before = shifted(late_section, "per", 1)
     with jax.named_scope("first_pull"):
         raw, high, low = call(
-            pull_kernel, [FAR] * 5 + [VM, SM],
+            pull_kernel, [FAR] * 7 + [VM],
             [((PER * RB * 2 * ROWS, TILE), F32), (tiles, BF16), (tiles, BF16)],
             [pltpu.VMEM(dual_start.shape, F32), pltpu.VMEM(dual_start.shape, F32),
-             pltpu.VMEM(tiles, F32), pltpu.VMEM(packed, F32), pltpu.VMEM(packed, F32)]
-            + scratch(2 * ROWS) + [pltpu.SemaphoreType.DMA((7,))], 60,
-        )(dual_start, demand, pool_tiles, carry, cost, table, code)
+             pltpu.VMEM(tiles, F32), pltpu.VMEM(packed, F32), pltpu.VMEM(packed, F32),
+             pltpu.SMEM((NB, PER, RB), jnp.int32), pltpu.SMEM((NB, PER, RB), jnp.int32),
+             pltpu.VMEM(tiles, BF16), pltpu.VMEM(tiles, BF16)]
+            + scratch(2 * ROWS) + [pltpu.SemaphoreType.DMA((9,)), pltpu.SemaphoreType.DMA((6,))],
+            60, [VM, FAR, FAR], 2 * heavy,
+        )(dual_start, demand, pool_tiles, carry, cost, *codes, table)
     with jax.named_scope("local_average"):
-        local, local_second, message, upper_chunk = call(
-            local_kernel, [VM] * 4,
-            [(field, F32), (field, F32), ((devices, 5, LANES), F32), ((PER, ROWS, LANES), F32)],
-            [pltpu.VMEM(field, F32), pltpu.VMEM(field, F32), pltpu.SemaphoreType.DMA((4,))],
-            places=[FAR, FAR, VM, VM],
-        )(raw, arriving, upper, table)
-    late_section, late_square, message = lax.optimization_barrier(
-        (table[SECTION + 1], square, message)
-    )
+        kept, message, chunk = call(
+            local_kernel, [VM] * 5,
+            [((2,) + field, F32), ((devices, 5, LANES), F32), ((PER + 1, ROWS, LANES), F32)],
+        )(raw, arriving, upper, table, before)
     got = lax.all_to_all(message, "scen", 0, 0, tiled=True)
-    before = shifted(late_section, "per", 1)
-    square_next = shifted(late_square, "per", -1)
-    before, square_next, got = lax.optimization_barrier((before, square_next, got))
     with jax.named_scope("section_average"):
         back, mean = call(
-            reduce_kernel, [VM] * 4, [((devices, 6, LANES), F32), ((PER, ROWS, LANES), F32)],
+            reduce_kernel, [VM] * 3, [((devices, 6, LANES), F32), ((PER, ROWS, LANES), F32)],
             [pltpu.VMEM((devices, LANES), F32)],
-        )(got, upper_chunk, table, before)
+        )(got, chunk, table)
     returned = lax.all_to_all(back, "scen", 0, 0, tiled=True)
     with jax.named_scope("selected"):
         early, late, second, pushed = call(
-            select_kernel, [VM, FAR, FAR, VM, VM],
-            [(slab, F32), (slab, F32), (field, F32), (field, F32)],
-            [pltpu.VMEM(field, F32), pltpu.VMEM(field, F32), pltpu.SemaphoreType.DMA((2,))],
-        )(returned, local, local_second, table, before)
+            select_kernel, [VM] * 4, [(slab, F32), (slab, F32), (field, F32), (field, F32)],
+        )(returned, kept, table, chunk)
     new_before = shifted(late, "per", 1)
     with jax.named_scope("push"):
         images, first, near = call(
-            push_kernel, [VM] * 7 + [SM], [(field, F32), (slab, F32), (slab, F32)],
-            scratch(2 * ROWS), 12,
-        )(early, late, pushed, high, low, carry, table, code)
+            push_kernel, [VM] * 7 + [FAR] * 2,
+            [(field, F32), ((RB + RB // ROWS, ROWS, TILE), F32), (slab, F32)],
+            scratch(2 * ROWS) + code_scratch, 12, work=2 * heavy,
+        )(early, late, pushed, high, low, carry, table, *codes)
+    new_before, first = lax.optimization_barrier((new_before, first))
     far = shifted(first, "per", -1)
     with jax.named_scope("second_pull"):
         net, primal_new, early_probe, late_probe = call(
-            second_kernel, [VM] * 14 + [SM],
+            second_kernel, [VM] * 13 + [FAR] * 2,
             [(field, F32), (field, F32), (slab, F32), (slab, F32)],
-            scratch(ROWS) + [pltpu.VMEM((PER * RB * ROWS, TILE), F32)], 8,
-        )(early, late, new_before, images, second, near, far, mean, square_next, upper, carry,
-          high, low, table, code)
+            [pltpu.VMEM((PER * RB * ROWS, TILE), F32)] + scratch(ROWS) + code_scratch, 8, work=heavy,
+        )(early, late, new_before, images, second, near, far, mean, upper, carry,
+          high, low, table, *codes)
     probe_before = shifted(late_probe, "per", 1)
     with jax.named_scope("second_push"):
         primal, partial = call(
-            result_kernel, [VM] * 12 + [SM], [(dual_start.shape, F32), (dual_start.shape, F32)],
-            scratch(ROWS) + [pltpu.VMEM(field, F32), pltpu.VMEM(field, F32)], 8,
+            result_kernel, [VM] * 12 + [FAR] * 2, [(dual_start.shape, F32), (dual_start.shape, F32)],
+            [pltpu.VMEM(field, F32), pltpu.VMEM(field, F32)] + scratch(ROWS) + code_scratch, 8,
+            work=heavy,
         )(early_probe, late_probe, high, low, dual_start, demand, net, early, late, primal_new,
-          carry, table, code)
+          carry, table, *codes)
     with jax.named_scope("correction"):
-        (dual,) = call(correct_kernel, [VM] * 4, [(dual_start.shape, F32)], aliases={0: 0})(
-            partial, probe_before, carry, table
-        )
+        (dual,) = call(
+            correct_kernel, [VM] * 4, [(dual_start.shape, F32)],
+            [pltpu.VMEM(dual_start.shape, F32), pltpu.VMEM((ROWS, feature), F32),
+             pltpu.SemaphoreType.DMA((ROWS,))], places=[FAR],
+        )(partial, probe_before, carry, table)
     return primal, dual
 
 

time: 119 us -> 112 us (0.941)
  blocking collectives: 25.3 us -> 60.5 us
  starting transfers between devices: 37.5 us -> 20.4 us
  waiting for transfers between devices: 19.7 us -> 7.39 us
  local copies, waits for them, and re-layouts: 8.24 us -> 1.26 us
  Pallas kernels: 25.5 us -> 21.1 us
    all_to_all x0 -> x1, blocking collectives: none -> 35 us  [per_device(): got = lax.all_to_all(message, 'scen', 0, 0, tiled=True)]
    all_to_all x1 -> x0, waiting for transfers between devices: 13.4 us -> none  [per_device(): got = lax.all_to_all(message, 'scen', 0, 0, tiled=True)]
    all_to_all x1 -> x0, starting transfers between devices: 13 us -> none  [per_device(): got = lax.all_to_all(message, 'scen', 0, 0, tiled=True)]
    unnamed x38 -> x20, local copies, waits for them, and re-layouts: 7.52 us -> 1.26 us
    pallas_call x9, Pallas kernels: 25.5 us -> 21.1 us  [the longest x1 7.82 us: per_device(): call(pull_kernel, [FAR] * 7 + [VM], [((PER * RB * 2 * ROWS, TILE), F32),...]
    ppermute x6 -> x5, starting transfers between devices: 24.5 us -> 20.4 us  [shifted(): return lax.ppermute(block, axis, route)]
    ppermute x6 -> x5, waiting for transfers between devices: 6.31 us -> 7.39 us  [shifted(): return lax.ppermute(block, axis, route)]
  transfers between devices with their start and end apart: 7 -> 5, of which waited for: 3 -> 3; matrix products, arithmetic and copies ran while one was open for 1% -> 0% of each run, Pallas kernels for 14% -> 12%
where the time goes in v4:
time: 112 us; the launch traced here: 111 us
  blocking collectives  60.5 us (54%)
  Pallas kernels  21.1 us (19%)
  starting transfers between devices  20.4 us (18%)
  waiting for transfers between devices  7.39 us (7%)
  local copies, waits for them, and re-layouts  1.26 us (1%)
    all_to_all x1, blocking collectives, per_device(): got = lax.all_to_all(message, 'scen', 0, 0, tiled=True)  35 us
    all_to_all x1, blocking collectives, per_device(): returned = lax.all_to_all(back, 'scen', 0, 0, tiled=True)  25.4 us
    ppermute x5, starting transfers between devices, shifted(): return lax.ppermute(block, axis, route)  20.4 us
    pallas_call x1, Pallas kernels, per_device(): call(pull_kernel, [FAR] * 7 + [VM], [((PER * RB * 2 * ROWS, TILE), F32),...  7.82 us
    ppermute x5, waiting for transfers between devices, shifted(): return lax.ppermute(block, axis, route)  7.39 us
    pallas_call x1, Pallas kernels, per_device(): call(result_kernel, [VM] * 12 + [FAR] * 2, [(dual_start.shape, F32), (dua...  3.04 us
    pallas_call x1, Pallas kernels, per_device(): call(push_kernel, [VM] * 7 + [FAR] * 2, [(field, F32), ((RB + RB // ROWS,...  2.94 us
    pallas_call x1, Pallas kernels, per_device(): call(carried_kernel, [FAR] * 8, [((RB, 2 * ROWS, TILE), F32), ((ROWS, LAN...  2.29 us
  transfers between devices with their start and end apart: 5, of which 3 were waited for; matrix products, arithmetic and copies ran while one was open for 0% of the time, Pallas kernels for 12%

profile of v4, /device:TPU:1, one launch (start us, length us, event | category | flops | bytes accessed | tf_op | source)
XLA Modules:
  0.0 111.5 jit_solution(14937330538987643737)
XLA Ops:
  0.6 2.3 %carried.1 = (f32[16,16,512]{2,1,0:T(8,128)}, f32[8,128]{1,0:T(8,128)}, f32[17,8,128]{2,1,0:T(8,128)}) custom-call(f32[8,2,8192]{2,1,0:T(2,128)} %dual_ref.1, f32[8,2,8192]{2,1,0:T(2,128)} %demand_ref.1, f32[2,8192]{1,0:T(2,128)} %carry_ref.7, f32[8]{0:T(128)} %prob_hbm.1, s32[2]{0:T(128)} %section_hbm.1, f32[2,4]{1,0:T(2,128)} %bitcast.11, s32[8]{0:T(128)} %subtree_hbm.1, ...), custom_call_target="tpu_custom_call" | custom-call | tf_op jit(solution)/shard_map/carried/pallas_call | solution.py:500
  2.9 8.8 %collective-permute-start = (f32[16,16,512]{2,1,0:T(8,128)}, f32[16,16,512]{2,1,0:T(8,128)S(1)}, u32[]{:S(2)}, u32[]{:S(2)}) collective-permute-start(f32[16,16,512]{2,1,0:T(8,128)} %get-tuple-element.30), channel_id=1, source_target_pairs={{1,0},{2,1},{3,2},{4,3},{5,4},{6,5},{7,6},{9,8},{10,9},{11,10},{12... | collective-permute-start | bytes 1572872 | tf_op jit(solution)/shard_map/ppermute | solution.py:30
  11.7 1.9 %collective-permute-start.1 = (f32[8,128]{1,0:T(8,128)}, f32[8,128]{1,0:T(8,128)S(1)}, u32[]{:S(2)}, u32[]{:S(2)}) collective-permute-start(f32[8,128]{1,0:T(8,128)} %get-tuple-element.31), channel_id=1, source_target_pairs={{0,1},{1,2},{2,3},{3,4},{4,5},{5,6},{6,7},{8,9},{9,10},{10,11},{11... | collective-permute-start | bytes 12296 | tf_op jit(solution)/shard_map/ppermute | solution.py:30
  13.7 0.0 copy-start.2
  13.7 0.0 copy-start.7
  13.7 7.8 %first_pull.1 = (f32[512,512]{1,0:T(8,128)}, bf16[3,512,512]{2,1,0:T(8,128)(2,1)}, bf16[3,512,512]{2,1,0:T(8,128)(2,1)}) custom-call(f32[8,2,8192]{2,1,0:T(2,128)} %dual_ref.1, f32[8,2,8192]{2,1,0:T(2,128)} %demand_ref.1, f32[3,512,512]{2,1,0:T(8,128)} %pool_hbm.1, f32[2,8192]{1,0:T(2,128)} %carry_ref.7, f32[2,8192]{1,0:T(2,128)} %cost_hbm.1, ...), custom_call_target="tpu_custom_call" | custom-call | flops 2415919104 | bytes 9437184 | tf_op jit(solution)/shard_map/first_pull/pallas_call | solution.py:512
  21.5 0.0 collective-permute-done.1.before_ref
  21.5 0.0 collective-permute-done.arriving_ref
  21.5 0.0 copy-done.2
  21.5 0.0 copy-done.7
  21.5 0.0 copy-start.6
  21.6 1.2 %copy-done.6 = f32[512,512]{1,0:T(8,128)S(1)} copy-done((f32[512,512]{1,0:T(8,128)S(1)}, f32[512,512]{1,0:T(8,128)}, u32[]{:S(2)}) %copy-start.6) | copy-done | bytes 1048600
  22.8 0.0 copy-start.1
  22.8 0.8 local_average.1
  23.5 0.0 copy-start
  23.6 0.0 copy-start.5
  23.6 0.0 copy-start.8
  23.6 0.0 copy-start.9
  23.6 35.0 %all_to_all.10.got_ref = f32[64,5,128]{2,1,0:T(8,128)S(1)} all-to-all(f32[64,5,128]{2,1,0:T(8,128)S(1)} %get-tuple-element.32), channel_id=1, replica_groups=mesh['scen'=64,'per'=8] {'scen'}, dimensions={0} | all-to-all | bytes 327680 | tf_op jit(solution)/shard_map/all_to_all | solution.py:527
  58.6 0.7 section_average.1
  59.4 25.4 %all_to_all.11.returned_ref = f32[64,6,128]{2,1,0:T(8,128)S(1)} all-to-all(f32[64,6,128]{2,1,0:T(8,128)S(1)} %get-tuple-element.34), channel_id=1, replica_groups=mesh['scen'=64,'per'=8] {'scen'}, dimensions={0} | all-to-all | bytes 393216 | tf_op jit(solution)/shard_map/all_to_all | solution.py:533
  84.8 0.3 selected.1
  85.2 5.9 %collective-permute-start.2 = (f32[16,8,512]{2,1,0:T(8,128)S(1)}, f32[16,8,512]{2,1,0:T(8,128)S(1)}, u32[]{:S(2)}, u32[]{:S(2)}) collective-permute-start(f32[16,8,512]{2,1,0:T(8,128)S(1)} %get-tuple-element.37.late_ref), channel_id=1, source_target_pairs={{0,1},{1,2},{2,3},{3,4},{4,5},{5,6},{6,7},{8,9},{9,10},{10,11},{11... | collective-permute-start | bytes 786440 | tf_op jit(solution)/shard_map/ppermute | solution.py:30
  91.1 0.0 copy-done.1
  91.1 0.0 copy-done
  91.1 0.0 copy-done.5
  91.1 0.0 copy-done.8
  91.1 0.0 copy-done.9
  91.1 2.9 %push.1 = (f32[2,16,8,512]{3,2,1,0:T(8,128)S(1)}, f32[18,8,512]{2,1,0:T(8,128)S(1)}, f32[16,8,512]{2,1,0:T(8,128)S(1)}) custom-call(f32[16,8,512]{2,1,0:T(8,128)S(1)} %get-tuple-element.36.early_ref, f32[16,8,512]{2,1,0:T(8,128)S(1)} %get-tuple-element.37.late_ref, f32[2,16,8,512]{3,2,1,0:T(8,128)S(1)} %get-tuple-element.38.pushed_ref, ...), custom_call_target="tpu_custom_call" | custom-call | flops 2415919104 | bytes 9437184 | tf_op jit(solution)/shard_map/push/pallas_call | solution.py:540
  94.1 0.3 collective-permute-done.2.before_ref
  94.4 1.9 %collective-permute-start.3 = (f32[18,8,512]{2,1,0:T(8,128)S(1)}, f32[18,8,512]{2,1,0:T(8,128)S(1)}, u32[]{:S(2)}, u32[]{:S(2)}) collective-permute-start(f32[18,8,512]{2,1,0:T(8,128)S(1)} %get-tuple-element.46), channel_id=1, source_target_pairs={{1,0},{2,1},{3,2},{4,3},{5,4},{6,5},{7,6},{9,8},{10,9},{11,10},{12... | collective-permute-start | bytes 884744 | tf_op jit(solution)/shard_map/ppermute | solution.py:30
  96.3 6.9 %collective-permute-done.3.far_ref = f32[18,8,512]{2,1,0:T(8,128)S(1)} collective-permute-done((f32[18,8,512]{2,1,0:T(8,128)S(1)}, f32[18,8,512]{2,1,0:T(8,128)S(1)}, u32[]{:S(2)}, u32[]{:S(2)}) %collective-permute-start.3) | collective-permute-done | bytes 294944 | tf_op jit(solution)/shard_map/ppermute | solution.py:30
  103.2 0.0 copy-start.3
  103.2 0.0 copy-start.4
  103.2 2.2 %second_pull.1 = (f32[2,16,8,512]{3,2,1,0:T(8,128)S(1)}, f32[2,16,8,512]{3,2,1,0:T(8,128)S(1)}, f32[16,8,512]{2,1,0:T(8,128)S(1)}, f32[16,8,512]{2,1,0:T(8,128)S(1)}) custom-call(f32[16,8,512]{2,1,0:T(8,128)S(1)} %get-tuple-element.36.early_ref, f32[16,8,512]{2,1,0:T(8,128)S(1)} %get-tuple-element.37.late_ref, ...), custom_call_target="tpu_custom_call" | custom-call | flops 1207959552 | bytes 4718592 | tf_op jit(solution)/shard_map/second_pull/pallas_call | solution.py:548
  105.4 1.9 %collective-permute-start.4 = (f32[16,8,512]{2,1,0:T(8,128)S(1)}, f32[16,8,512]{2,1,0:T(8,128)S(1)}, u32[]{:S(2)}, u32[]{:S(2)}) collective-permute-start(f32[16,8,512]{2,1,0:T(8,128)S(1)} %get-tuple-element.49.late_probe_ref), channel_id=1, source_target_pairs={{0,1},{1,2},{2,3},{3,4},{4,5},{5,6},{6,7},{8,9},{9,10},{10,11},{11... | collective-permute-start | bytes 786440 | tf_op jit(solution)/shard_map/ppermute | solution.py:30
  107.3 0.0 copy-done.3
  107.3 0.0 copy-done.4
  107.3 3.0 %second_push.1 = (f32[8,2,8192]{2,1,0:T(2,128)}, f32[8,2,8192]{2,1,0:T(2,128)S(1)}) custom-call(f32[16,8,512]{2,1,0:T(8,128)S(1)} %get-tuple-element.48.early_probe_ref, f32[16,8,512]{2,1,0:T(8,128)S(1)} %get-tuple-element.49.late_probe_ref, bf16[3,512,512]{2,1,0:T(8,128)(2,1)S(1)} %copy-done, bf16[3,512,512]{2,1,0:T(8,128)(2,1)S(1)} %copy-done.1, ...), custom_call_target="tpu_custom_call" | custom-call | flops 1207959552 | bytes 4718592 | tf_op jit(solution)/shard_map/second_push/pallas_call | solution.py:556
  110.4 0.2 collective-permute-done.4.before_ref
  110.6 0.9 correction.1
Async XLA Ops:
  2.9 18.6 %collective-permute-start = (f32[16,16,512]{2,1,0:T(8,128)}, f32[16,16,512]{2,1,0:T(8,128)S(1)}, u32[]{:S(2)}, u32[]{:S(2)}) collective-permute-start(f32[16,16,512]{2,1,0:T(8,128)} %get-tuple-element.30), channel_id=1, source_target_pairs={{1,0},{2,1},{3,2},{4,3},{5,4},{6,5},{7,6},{9,8},{10,9},{11,10},{12... | collective-permute-start | bytes 1572872 | tf_op jit(solution)/shard_map/ppermute | solution.py:30
  11.7 9.8 %collective-permute-start.1 = (f32[8,128]{1,0:T(8,128)}, f32[8,128]{1,0:T(8,128)S(1)}, u32[]{:S(2)}, u32[]{:S(2)}) collective-permute-start(f32[8,128]{1,0:T(8,128)} %get-tuple-element.31), channel_id=1, source_target_pairs={{0,1},{1,2},{2,3},{3,4},{4,5},{5,6},{6,7},{8,9},{9,10},{10,11},{11... | collective-permute-start | bytes 12296 | tf_op jit(solution)/shard_map/ppermute | solution.py:30
  13.7 7.9 %copy-start.2 = (f32[17,8,128]{2,1,0:T(8,128)S(1)}, f32[17,8,128]{2,1,0:T(8,128)}, u32[]{:S(2)}) copy-start(f32[17,8,128]{2,1,0:T(8,128)} %get-tuple-element.28.table_ref) | copy-start | bytes 208900
  13.7 7.9 %copy-start.7 = (f32[2,8192]{1,0:T(2,128)S(1)}, f32[2,8192]{1,0:T(2,128)}, u32[]{:S(2)}) copy-start(f32[2,8192]{1,0:T(2,128)} %upper_ref.3) | copy-start | bytes 196612
  21.5 1.2 %copy-start.6 = (f32[512,512]{1,0:T(8,128)S(1)}, f32[512,512]{1,0:T(8,128)}, u32[]{:S(2)}) copy-start(f32[512,512]{1,0:T(8,128)} %get-tuple-element.29.raw_ref) | copy-start | bytes 3145732
  22.8 68.3 %copy-start.1 = (bf16[3,512,512]{2,1,0:T(8,128)(2,1)S(1)}, bf16[3,512,512]{2,1,0:T(8,128)(2,1)}, u32[]{:S(2)}) copy-start(bf16[3,512,512]{2,1,0:T(8,128)(2,1)} %get-tuple-element.40.low_ref) | copy-start | bytes 4718596
  23.5 67.5 %copy-start = (bf16[3,512,512]{2,1,0:T(8,128)(2,1)S(1)}, bf16[3,512,512]{2,1,0:T(8,128)(2,1)}, u32[]{:S(2)}) copy-start(bf16[3,512,512]{2,1,0:T(8,128)(2,1)} %get-tuple-element.39.high_ref) | copy-start | bytes 4718596
  23.6 67.5 %copy-start.5 = (f32[2,8192]{1,0:T(2,128)S(1)}, f32[2,8192]{1,0:T(2,128)}, u32[]{:S(2)}) copy-start(f32[2,8192]{1,0:T(2,128)} %carry_ref.7) | copy-start | bytes 196612
  23.6 67.5 %copy-start.8 = (s32[2,16,3]{1,0,2:T(2,128)S(1)}, s32[2,16,3]{1,0,2:T(2,128)}, u32[]{:S(2)}) copy-start(s32[2,16,3]{1,0,2:T(2,128)} %param.20) | copy-start | bytes 1156
  23.6 67.5 %copy-start.9 = (s32[2,16,3]{1,0,2:T(2,128)S(1)}, s32[2,16,3]{1,0,2:T(2,128)}, u32[]{:S(2)}) copy-start(s32[2,16,3]{1,0,2:T(2,128)} %param.21) | copy-start | bytes 1156
  85.2 9.2 %collective-permute-start.2 = (f32[16,8,512]{2,1,0:T(8,128)S(1)}, f32[16,8,512]{2,1,0:T(8,128)S(1)}, u32[]{:S(2)}, u32[]{:S(2)}) collective-permute-start(f32[16,8,512]{2,1,0:T(8,128)S(1)} %get-tuple-element.37.late_ref), channel_id=1, source_target_pairs={{0,1},{1,2},{2,3},{3,4},{4,5},{5,6},{6,7},{8,9},{9,10},{10,11},{11... | collective-permute-start | bytes 786440 | tf_op jit(solution)/shard_map/ppermute | solution.py:30
  94.4 8.8 %collective-permute-start.3 = (f32[18,8,512]{2,1,0:T(8,128)S(1)}, f32[18,8,512]{2,1,0:T(8,128)S(1)}, u32[]{:S(2)}, u32[]{:S(2)}) collective-permute-start(f32[18,8,512]{2,1,0:T(8,128)S(1)} %get-tuple-element.46), channel_id=1, source_target_pairs={{1,0},{2,1},{3,2},{4,3},{5,4},{6,5},{7,6},{9,8},{10,9},{11,10},{12... | collective-permute-start | bytes 884744 | tf_op jit(solution)/shard_map/ppermute | solution.py:30
  103.2 4.2 %copy-start.3 = (f32[8,2,8192]{2,1,0:T(2,128)S(1)}, f32[8,2,8192]{2,1,0:T(2,128)}, u32[]{:S(2)}) copy-start(f32[8,2,8192]{2,1,0:T(2,128)} %dual_ref.1) | copy-start | bytes 1572868
  103.2 4.2 %copy-start.4 = (f32[8,2,8192]{2,1,0:T(2,128)S(1)}, f32[8,2,8192]{2,1,0:T(2,128)}, u32[]{:S(2)}) copy-start(f32[8,2,8192]{2,1,0:T(2,128)} %demand_ref.1) | copy-start | bytes 1572868
  105.4 5.2 %collective-permute-start.4 = (f32[16,8,512]{2,1,0:T(8,128)S(1)}, f32[16,8,512]{2,1,0:T(8,128)S(1)}, u32[]{:S(2)}, u32[]{:S(2)}) collective-permute-start(f32[16,8,512]{2,1,0:T(8,128)S(1)} %get-tuple-element.49.late_probe_ref), channel_id=1, source_target_pairs={{0,1},{1,2},{2,3},{3,4},{4,5},{5,6},{6,7},{8,9},{9,10},{10,11},{11... | collective-permute-start | bytes 786440 | tf_op jit(solution)/shard_map/ppermute | solution.py:30

commit v5 on v4

--- a/solution.py
+++ b/solution.py
@@ -93,11 +93,11 @@
     return tuple(ref[k, period, block] for ref in code_refs)
 
 
-def gathered_blocks(image_ref, code_refs, period, block, height):
+def gathered_blocks(image_ref, code_refs, period, block, height, slot):
     total = None
     for k in range(NB):
         which, place = code_of(code_refs, period, block, k)
-        first = pl.multiple_of((period * RB + place) * height, height)
+        first = pl.multiple_of((slot * RB + place) * height, height)
         part = image_ref[which, pl.ds(first, height), :]
         total = part if total is None else total + part
     return total
@@ -254,13 +254,17 @@
             for quarter in range(QUARTERS):
                 lanes = slice(quarter * LANES, (quarter + 1) * LANES)
                 chunk = block * QUARTERS + quarter
-                message_ref[chunk, period : period + 1, :] = sums[:, lanes]
-                message_ref[chunk, 2 + period : 3 + period, :] = second_sums[:, lanes]
+                message_ref[chunk, :, part_of(period)] = sums[:, lanes]
+                message_ref[chunk, :, part_of(2 + period)] = second_sums[:, lanes]
         chunk_ref[period] = jnp.broadcast_to(
             upper_ref[period : period + 1, pl.ds(place, LANES)], (ROWS, LANES)
         )
     for chunk in range(RB * QUARTERS):
-        message_ref[chunk, 4:5, :] = mass[:, :LANES]
+        message_ref[chunk, :, part_of(4)] = mass[:, :LANES]
+
+
+def part_of(index):
+    return slice(index * LANES, (index + 1) * LANES)
 
 
 def reduce_kernel(got_ref, chunk_ref, table_ref, back_ref, mean_ref, moment_ref):
@@ -276,39 +280,40 @@
         return jnp.dot(a, b, precision=lax.Precision.HIGHEST, preferred_element_type=F32)
 
     device = lax.axis_index("scen")
-    mass = got_ref[:, 4, :]
+    mass = got_ref[:, 0, part_of(4)]
     moment = mass * table_ref[PRODUCTS:TABLE].reshape(devices, LANES)
     befores = (chunk_ref[PER], table_ref[SECTION])
     for period in range(PER):
         section = table_ref[SECTION + period]
         same = member(section)
         inverse = 1.0 / dot(same, mass)
-        sums = got_ref[:, period, :]
+        sums = got_ref[:, 0, part_of(period)]
         upper = chunk_ref[period, 0:1, :]
         new = jnp.minimum(jnp.maximum(dot(same, sums) * inverse, 0.0), upper)
-        back_ref[:, period, :] = new
-        back_ref[:, 2 + period, :] = dot(same, got_ref[:, 2 + period, :]) * inverse
+        back_ref[:, 0, part_of(period)] = new
+        back_ref[:, 0, part_of(2 + period)] = dot(same, got_ref[:, 0, part_of(2 + period)]) * inverse
         moment_ref[...] = dot(same, moment) * inverse
         mean_ref[period] = jnp.broadcast_to(moment_ref[pl.ds(device, 1), :], (ROWS, LANES))
         source = jnp.where(section[0:1] > ROWS, moment * new, sums)
         same = member(befores[period])
-        back_ref[:, 4 + period, :] = dot(same, source) / dot(same, mass)
+        back_ref[:, 0, part_of(4 + period)] = dot(same, source) / dot(same, mass)
 
 
 def row_of(returned_ref, index, block):
     parts = [
-        returned_ref[block * QUARTERS + quarter, index : index + 1, :] for quarter in range(QUARTERS)
+        returned_ref[block * QUARTERS + quarter, :, part_of(index)] for quarter in range(QUARTERS)
     ]
     return jnp.concatenate(parts, axis=1)
 
 
 def select_kernel(returned_ref, kept_ref, table_ref, chunk_ref,
-                  early_ref, late_ref, second_ref, pushed_ref):
+                  early_ref, late_ref, second_ref, pushed_first_ref, pushed_next_ref):
     product = entry_of(table_ref, RATE) * entry_of(table_ref, DUAL_RATE)
     weight = entry_of(table_ref, PROB)
     befores = (entry_of(chunk_ref, PER), entry_of(table_ref, SECTION))
     for period in range(PER):
         out_ref = (early_ref, late_ref)[period]
+        pushed_ref = (pushed_first_ref, pushed_next_ref)[period]
         wide = entry_of(table_ref, SECTION + period) > ROWS
         wide_before = befores[period] > ROWS
         scale = product / group_sum(weight, befores[period])
@@ -321,40 +326,52 @@
             second_ref[period, block] = jnp.where(wide, row, kept_ref[1, period, block])
             row = jnp.broadcast_to(row_of(returned_ref, 4 + period, block), shape)
             averaged = scale * group_sum(weight * new, befores[period])
-            pushed_ref[period, block] = jnp.where(wide_before, row, averaged)
+            pushed_ref[block] = jnp.where(wide_before, row, averaged)
+
+
+def push_first_kernel(pushed_ref, high_ref, low_ref, carry_ref, table_ref, cols_hbm, which_hbm,
+                      first_ref, lhs_ref, image_ref, cols_ref, which_ref, sems):
+    copies = fetch([(cols_hbm, cols_ref), (which_hbm, which_ref)], sems)
+    code_refs = which_ref, cols_ref
+    for block in range(RB):
+        lhs_ref[block * ROWS : (block + 1) * ROWS, :] = pushed_ref[block]
+    product_images(lhs_ref, high_ref, low_ref, image_ref, False)
+    for copy in copies:
+        copy.wait()
+    factor = 2.0 * entry_of(table_ref, DAMP)
+    for block in range(RB):
+        carry = lanes_of(carry_ref, 0, block)
+        image = gathered_blocks(image_ref, code_refs, 0, block, ROWS, 0)
+        first_ref[block] = factor * carry * image
+        row = block % ROWS
+        first_ref[RB + block // ROWS, row : row + 1, :] = 0.5 * factor[0:1] * carry * carry
 
 
 def push_kernel(early_ref, late_ref, pushed_ref, high_ref, low_ref, carry_ref, table_ref,
-                cols_hbm, which_hbm, image_out_ref, first_ref, next_ref, lhs_ref, image_ref,
+                cols_hbm, which_hbm, image_out_ref, next_ref, lhs_ref, image_ref,
                 cols_ref, which_ref, sems):
     copies = fetch([(cols_hbm, cols_ref), (which_hbm, which_ref)], sems)
     code_refs = which_ref, cols_ref
-    for period in range(PER):
-        new_ref = (early_ref, late_ref)[period]
-        for block in range(RB):
-            first = (period * RB + block) * 2 * ROWS
-            lhs_ref[first : first + ROWS, :] = new_ref[block]
-            lhs_ref[first + ROWS : first + 2 * ROWS, :] = pushed_ref[period, block]
+    for slot, field_ref in enumerate((early_ref, late_ref, pushed_ref)):
+        for block in range(RB):
+            first = (slot * RB + block) * ROWS
+            lhs_ref[first : first + ROWS, :] = field_ref[block]
     product_images(lhs_ref, high_ref, low_ref, image_ref, False)
     for copy in copies:
         copy.wait()
-    for period in range(PER):
-        out_ref = (first_ref, next_ref)[period]
-        factor = 2.0 * entry_of(table_ref, DAMP + period)
-        for block in range(RB):
-            both = gathered_blocks(image_ref, code_refs, period, block, 2 * ROWS)
-            image_out_ref[period, block] = both[:ROWS]
-            carry = lanes_of(carry_ref, period, block)
-            out_ref[block] = factor * carry * both[ROWS:]
-            if period == 0:
-                row = block % ROWS
-                out_ref[RB + block // ROWS, row : row + 1, :] = 0.5 * factor[0:1] * carry * carry
-
-
-def second_kernel(early_ref, late_ref, before_ref, images_ref, second_ref, near_ref, far_ref,
-                  mean_ref, upper_ref, carry_ref, high_ref, low_ref, table_ref, cols_hbm, which_hbm,
-                  net_ref, primal_ref, early_probe_ref, late_probe_ref,
-                  pulled_ref, lhs_ref, image_ref, cols_ref, which_ref, sems):
+    factor = 2.0 * entry_of(table_ref, DAMP + 1)
+    for block in range(RB):
+        for period in range(PER):
+            image_out_ref[period, block] = gathered_blocks(
+                image_ref, code_refs, period, block, ROWS, period
+            )
+        image = gathered_blocks(image_ref, code_refs, 1, block, ROWS, 2)
+        next_ref[block] = factor * lanes_of(carry_ref, 1, block) * image
+
+
+def net_kernel(early_ref, before_ref, images_ref, mean_ref, carry_ref, high_ref, low_ref, table_ref,
+               cols_hbm, which_hbm, net_ref, pulled_ref, lhs_ref, image_ref,
+               cols_ref, which_ref, sems):
     copies = fetch([(cols_hbm, cols_ref), (which_hbm, which_ref)], sems)
     code_refs = which_ref, cols_ref
     for period in range(PER):
@@ -370,6 +387,10 @@
     for copy in copies:
         copy.wait()
     scattered_blocks(image_ref, code_refs, pulled_ref, ROWS)
+
+
+def primal_kernel(early_ref, late_ref, pulled_ref, second_ref, near_ref, far_ref, mean_ref,
+                  upper_ref, carry_ref, table_ref, primal_ref, early_probe_ref, late_probe_ref):
     for period in range(PER):
         new_ref = (early_ref, late_ref)[period]
         next_ref = (near_ref, far_ref)[period]
@@ -428,7 +449,7 @@
         for block in range(RB):
             start, target = start_ref[period, block], target_ref[period, block]
             change = dual_rate * (target - net_ref[period, block])
-            image = gathered_blocks(image_ref, code_refs, period, block, ROWS)
+            image = gathered_blocks(image_ref, code_refs, period, block, ROWS, period)
             if period == 1:
                 image -= lanes_of(carry_ref, 1, block) * early_probe_ref[block]
             dual_new = start + damp * change + dual_rate * (target - image)
@@ -485,8 +506,8 @@
     tiles = (NPOOL, TILE, TILE)
     packed = (PER, feature)
 
-    def scratch(height):
-        count = PER * RB * height
+    def scratch(height, slots=PER):
+        count = slots * RB * height
         return [pltpu.VMEM((count, TILE), F32), pltpu.VMEM((NPOOL, count, TILE), F32)]
 
     codes = (block_cols.transpose(2, 0, 1), block_pool.transpose(2, 0, 1))
@@ -522,35 +543,43 @@
     with jax.named_scope("local_average"):
         kept, message, chunk = call(
             local_kernel, [VM] * 5,
-            [((2,) + field, F32), ((devices, 5, LANES), F32), ((PER + 1, ROWS, LANES), F32)],
+            [((2,) + field, F32), ((devices, 1, 5 * LANES), F32), ((PER + 1, ROWS, LANES), F32)],
         )(raw, arriving, upper, table, before)
     got = lax.all_to_all(message, "scen", 0, 0, tiled=True)
     with jax.named_scope("section_average"):
         back, mean = call(
-            reduce_kernel, [VM] * 3, [((devices, 6, LANES), F32), ((PER, ROWS, LANES), F32)],
+            reduce_kernel, [VM] * 3, [((devices, 1, 6 * LANES), F32), ((PER, ROWS, LANES), F32)],
             [pltpu.VMEM((devices, LANES), F32)],
         )(got, chunk, table)
     returned = lax.all_to_all(back, "scen", 0, 0, tiled=True)
     with jax.named_scope("selected"):
-        early, late, second, pushed = call(
-            select_kernel, [VM] * 4, [(slab, F32), (slab, F32), (field, F32), (field, F32)],
+        early, late, second, pushed_first, pushed_next = call(
+            select_kernel, [VM] * 4,
+            [(slab, F32), (slab, F32), (field, F32), (slab, F32), (slab, F32)],
         )(returned, kept, table, chunk)
     new_before = shifted(late, "per", 1)
+    with jax.named_scope("push_first"):
+        (first,) = call(
+            push_first_kernel, [VM] * 5 + [FAR] * 2, [((RB + RB // ROWS, ROWS, TILE), F32)],
+            scratch(ROWS, 1) + code_scratch, 6, work=heavy // 2,
+        )(pushed_first, high, low, carry, table, *codes)
+    far = shifted(first, "per", -1)
+    early, late, pushed_next, first = lax.optimization_barrier((early, late, pushed_next, first))
     with jax.named_scope("push"):
-        images, first, near = call(
-            push_kernel, [VM] * 7 + [FAR] * 2,
-            [(field, F32), ((RB + RB // ROWS, ROWS, TILE), F32), (slab, F32)],
-            scratch(2 * ROWS) + code_scratch, 12, work=2 * heavy,
-        )(early, late, pushed, high, low, carry, table, *codes)
-    new_before, first = lax.optimization_barrier((new_before, first))
-    far = shifted(first, "per", -1)
+        images, near = call(
+            push_kernel, [VM] * 7 + [FAR] * 2, [(field, F32), (slab, F32)],
+            scratch(ROWS, 3) + code_scratch, 10, work=2 * heavy,
+        )(early, late, pushed_next, high, low, carry, table, *codes)
     with jax.named_scope("second_pull"):
-        net, primal_new, early_probe, late_probe = call(
-            second_kernel, [VM] * 13 + [FAR] * 2,
-            [(field, F32), (field, F32), (slab, F32), (slab, F32)],
-            [pltpu.VMEM((PER * RB * ROWS, TILE), F32)] + scratch(ROWS) + code_scratch, 8, work=heavy,
-        )(early, late, new_before, images, second, near, far, mean, upper, carry,
-          high, low, table, *codes)
+        net, pulled = call(
+            net_kernel, [VM] * 8 + [FAR] * 2, [(field, F32), ((PER * RB * ROWS, TILE), F32)],
+            scratch(ROWS) + code_scratch, 8, work=heavy,
+        )(early, new_before, images, mean, carry, high, low, table, *codes)
+    far, pulled = lax.optimization_barrier((far, pulled))
+    with jax.named_scope("second_primal"):
+        primal_new, early_probe, late_probe = call(
+            primal_kernel, [VM] * 10, [(field, F32), (slab, F32), (slab, F32)],
+        )(early, late, pulled, second, near, far, mean, upper, carry, table)
     probe_before = shifted(late_probe, "per", 1)
     with jax.named_scope("second_push"):
         primal, partial = call(

time: 112 us -> 100 us (0.89)
  blocking collectives: 60.5 us -> 53.2 us
  waiting for transfers between devices: 7.39 us -> 1.93 us
    ppermute x5, waiting for transfers between devices: 7.39 us -> 1.93 us  [shifted(): return lax.ppermute(block, axis, route)]
    all_to_all x1, blocking collectives: 35 us -> 31.2 us  [per_device(): got = lax.all_to_all(message, 'scen', 0, 0, tiled=True)]
    all_to_all x1, blocking collectives: 25.4 us -> 22.1 us  [per_device(): returned = lax.all_to_all(back, 'scen', 0, 0, tiled=True)]
    pallas_call x5 -> x7, Pallas kernels: 7.02 us -> 7.65 us  [the longest x1 2.41 us: per_device(): call(push_kernel, [VM] * 7 + [FAR] * 2, [(field, F32), (slab, F32)], scra...]
  transfers between devices with their start and end apart: 5 -> 5, of which waited for: 3 -> 2; matrix products, arithmetic and copies ran while one was open for 0% -> 0% of each run, Pallas kernels for 12% -> 16%
where the time goes in v5:
time: 100 us; the launch traced here: 99.8 us
  blocking collectives  53.2 us (53%)
  Pallas kernels  21.7 us (22%)
  starting transfers between devices  20.8 us (21%)
  waiting for transfers between devices  1.93 us (2%)
  local copies, waits for them, and re-layouts  1.27 us (1%)
    all_to_all x1, blocking collectives, per_device(): got = lax.all_to_all(message, 'scen', 0, 0, tiled=True)  31.2 us
    all_to_all x1, blocking collectives, per_device(): returned = lax.all_to_all(back, 'scen', 0, 0, tiled=True)  22.1 us
    ppermute x5, starting transfers between devices, shifted(): return lax.ppermute(block, axis, route)  20.8 us
    pallas_call x1, Pallas kernels, per_device(): call(pull_kernel, [FAR] * 7 + [VM], [((PER * RB * 2 * ROWS, TILE), F32),...  7.81 us
    pallas_call x1, Pallas kernels, per_device(): call(result_kernel, [VM] * 12 + [FAR] * 2, [(dual_start.shape, F32), (dua...  3.05 us
    pallas_call x1, Pallas kernels, per_device(): call(push_kernel, [VM] * 7 + [FAR] * 2, [(field, F32), (slab, F32)], scra...  2.41 us
    pallas_call x1, Pallas kernels, per_device(): call(carried_kernel, [FAR] * 8, [((RB, 2 * ROWS, TILE), F32), ((ROWS, LAN...  2.29 us
  transfers between devices with their start and end apart: 5, of which 2 were waited for; matrix products, arithmetic and copies ran while one was open for 0% of the time, Pallas kernels for 16%

profile of v5, /device:TPU:1, one launch (start us, length us, event | category | flops | bytes accessed | tf_op | source)
XLA Modules:
  0.0 99.8 jit_solution(2015674484961445823)
XLA Ops:
  0.6 2.3 %carried.1 = (f32[16,16,512]{2,1,0:T(8,128)}, f32[8,128]{1,0:T(8,128)}, f32[17,8,128]{2,1,0:T(8,128)}) custom-call(f32[8,2,8192]{2,1,0:T(2,128)} %dual_ref.1, f32[8,2,8192]{2,1,0:T(2,128)} %demand_ref.1, f32[2,8192]{1,0:T(2,128)} %carry_ref.11, f32[8]{0:T(128)} %prob_hbm.1, s32[2]{0:T(128)} %section_hbm.1, f32[2,4]{1,0:T(2,128)} %bitcast.13, s32[8]{0:T(128)} %subtree_hbm.1, ...), custom_call_target="tpu_custom_call" | custom-call | tf_op jit(solution)/shard_map/carried/pallas_call | solution.py:521
  2.9 8.8 %collective-permute-start = (f32[16,16,512]{2,1,0:T(8,128)}, f32[16,16,512]{2,1,0:T(8,128)S(1)}, u32[]{:S(2)}, u32[]{:S(2)}) collective-permute-start(f32[16,16,512]{2,1,0:T(8,128)} %get-tuple-element.34), channel_id=1, source_target_pairs={{1,0},{2,1},{3,2},{4,3},{5,4},{6,5},{7,6},{9,8},{10,9},{11,10},{12... | collective-permute-start | bytes 1572872 | tf_op jit(solution)/shard_map/ppermute | solution.py:30
  11.7 1.9 %collective-permute-start.1 = (f32[8,128]{1,0:T(8,128)}, f32[8,128]{1,0:T(8,128)S(1)}, u32[]{:S(2)}, u32[]{:S(2)}) collective-permute-start(f32[8,128]{1,0:T(8,128)} %get-tuple-element.35), channel_id=1, source_target_pairs={{0,1},{1,2},{2,3},{3,4},{4,5},{5,6},{6,7},{8,9},{9,10},{10,11},{11... | collective-permute-start | bytes 12296 | tf_op jit(solution)/shard_map/ppermute | solution.py:30
  13.7 0.0 copy-start.2
  13.7 0.0 copy-start.7
  13.7 7.8 %first_pull.1 = (f32[512,512]{1,0:T(8,128)}, bf16[3,512,512]{2,1,0:T(8,128)(2,1)}, bf16[3,512,512]{2,1,0:T(8,128)(2,1)}) custom-call(f32[8,2,8192]{2,1,0:T(2,128)} %dual_ref.1, f32[8,2,8192]{2,1,0:T(2,128)} %demand_ref.1, f32[3,512,512]{2,1,0:T(8,128)} %pool_hbm.1, f32[2,8192]{1,0:T(2,128)} %carry_ref.11, f32[2,8192]{1,0:T(2,128)} %cost_hbm.1, ...), custom_call_target="tpu_custom_call" | custom-call | flops 2415919104 | bytes 9437184 | tf_op jit(solution)/shard_map/first_pull/pallas_call | solution.py:533
  21.5 0.0 collective-permute-done.1.before_ref
  21.5 0.0 collective-permute-done.arriving_ref
  21.5 0.0 copy-done.2
  21.5 0.0 copy-done.7
  21.5 0.0 copy-start.6
  21.5 1.2 %copy-done.6 = f32[512,512]{1,0:T(8,128)S(1)} copy-done((f32[512,512]{1,0:T(8,128)S(1)}, f32[512,512]{1,0:T(8,128)}, u32[]{:S(2)}) %copy-start.6) | copy-done | bytes 1048600
  22.8 0.0 copy-start.1
  22.8 0.8 local_average.1
  23.5 0.0 copy-start
  23.5 0.0 copy-start.5
  23.6 0.0 copy-start.8
  23.6 0.0 copy-start.9
  23.6 31.2 %all_to_all.10.got_ref = f32[64,1,640]{2,1,0:T(1,128)S(1)} all-to-all(f32[64,1,640]{2,1,0:T(1,128)S(1)} %get-tuple-element.36), channel_id=1, replica_groups=mesh['scen'=64,'per'=8] {'scen'}, dimensions={0} | all-to-all | bytes 327680 | tf_op jit(solution)/shard_map/all_to_all | solution.py:548
  54.8 0.7 section_average.1
  55.5 22.1 %all_to_all.11.returned_ref = f32[64,1,768]{2,1,0:T(1,128)S(1)} all-to-all(f32[64,1,768]{2,1,0:T(1,128)S(1)} %get-tuple-element.38), channel_id=1, replica_groups=mesh['scen'=64,'per'=8] {'scen'}, dimensions={0} | all-to-all | bytes 393216 | tf_op jit(solution)/shard_map/all_to_all | solution.py:554
  77.6 0.3 selected.1
  77.9 6.1 %collective-permute-start.3 = (f32[16,8,512]{2,1,0:T(8,128)S(1)}, f32[16,8,512]{2,1,0:T(8,128)S(1)}, u32[]{:S(2)}, u32[]{:S(2)}) collective-permute-start(f32[16,8,512]{2,1,0:T(8,128)S(1)} %get-tuple-element.47.late_ref), channel_id=1, source_target_pairs={{0,1},{1,2},{2,3},{3,4},{4,5},{5,6},{6,7},{8,9},{9,10},{10,11},{11... | collective-permute-start | bytes 786440 | tf_op jit(solution)/shard_map/ppermute | solution.py:30
  84.0 0.0 copy-done.1
  84.0 0.0 copy-done
  84.0 0.0 copy-done.5
  84.0 0.0 copy-done.8
  84.0 0.0 copy-done.9
  84.0 1.2 %push_first.1 = f32[18,8,512]{2,1,0:T(8,128)S(1)} custom-call(f32[16,8,512]{2,1,0:T(8,128)S(1)} %get-tuple-element.43.pushed_ref, bf16[3,512,512]{2,1,0:T(8,128)(2,1)S(1)} %copy-done, bf16[3,512,512]{2,1,0:T(8,128)(2,1)S(1)} %copy-done.1, f32[2,8192]{1,0:T(2,128)S(1)} %copy-done.5, f32[17,8,128]{2,1,0:T(8,128)S(1)} %copy-done.2, s32[3,2,16]{2,1,0:T(2,128)S(1)} %bitcast.4, ...), custom_call_target="tpu_custom_call" | custom-call | flops 603979776 | bytes 2359296 | tf_op jit(solution)/shard_map/push_first/pallas_call | solution.py:562
  85.2 1.9 %collective-permute-start.2 = (f32[18,8,512]{2,1,0:T(8,128)S(1)}, f32[18,8,512]{2,1,0:T(8,128)S(1)}, u32[]{:S(2)}, u32[]{:S(2)}) collective-permute-start(f32[18,8,512]{2,1,0:T(8,128)S(1)} %push_first.1), channel_id=1, source_target_pairs={{1,0},{2,1},{3,2},{4,3},{5,4},{6,5},{7,6},{9,8},{10,9},{11,10},{12... | collective-permute-start | bytes 884744 | tf_op jit(solution)/shard_map/ppermute | solution.py:30
  87.2 2.4 %push.1 = (f32[2,16,8,512]{3,2,1,0:T(8,128)S(1)}, f32[16,8,512]{2,1,0:T(8,128)S(1)}) custom-call(f32[16,8,512]{2,1,0:T(8,128)S(1)} %get-tuple-element.46.early_ref, f32[16,8,512]{2,1,0:T(8,128)S(1)} %get-tuple-element.47.late_ref, f32[16,8,512]{2,1,0:T(8,128)S(1)} %get-tuple-element.48.pushed_ref, bf16[3,512,512]{2,1,0:T(8,128)(2,1)S(1)} %copy-done, ...), custom_call_target="tpu_custom_call" | custom-call | flops 2415919104 | bytes 9437184 | tf_op jit(solution)/shard_map/push/pallas_call | solution.py:569
  89.6 0.0 collective-permute-done.3.before_ref
  89.6 2.0 %second_pull.1 = (f32[2,16,8,512]{3,2,1,0:T(8,128)S(1)}, f32[256,512]{1,0:T(8,128)S(1)}) custom-call(f32[16,8,512]{2,1,0:T(8,128)S(1)} %get-tuple-element.46.early_ref, f32[16,8,512]{2,1,0:T(8,128)S(1)} %collective-permute-done.3.before_ref, f32[2,16,8,512]{3,2,1,0:T(8,128)S(1)} %get-tuple-element.49.images_ref, ...), custom_call_target="tpu_custom_call" | custom-call | flops 1207959552 | bytes 4718592 | tf_op jit(solution)/shard_map/second_pull/pallas_call | solution.py:574
  91.6 0.0 copy-start.3
  91.6 0.0 copy-start.4
  91.6 1.7 %collective-permute-done.2.far_ref = f32[18,8,512]{2,1,0:T(8,128)S(1)} collective-permute-done((f32[18,8,512]{2,1,0:T(8,128)S(1)}, f32[18,8,512]{2,1,0:T(8,128)S(1)}, u32[]{:S(2)}, u32[]{:S(2)}) %collective-permute-start.2) | collective-permute-done | bytes 294944 | tf_op jit(solution)/shard_map/ppermute | solution.py:30
  93.3 0.2 second_primal.1
  93.5 2.1 %collective-permute-start.4 = (f32[16,8,512]{2,1,0:T(8,128)S(1)}, f32[16,8,512]{2,1,0:T(8,128)S(1)}, u32[]{:S(2)}, u32[]{:S(2)}) collective-permute-start(f32[16,8,512]{2,1,0:T(8,128)S(1)} %get-tuple-element.57.late_probe_ref), channel_id=1, source_target_pairs={{0,1},{1,2},{2,3},{3,4},{4,5},{5,6},{6,7},{8,9},{9,10},{10,11},{11... | collective-permute-start | bytes 786440 | tf_op jit(solution)/shard_map/ppermute | solution.py:30
  95.6 0.0 copy-done.3
  95.6 0.0 copy-done.4
  95.7 3.1 %second_push.1 = (f32[8,2,8192]{2,1,0:T(2,128)}, f32[8,2,8192]{2,1,0:T(2,128)S(1)}) custom-call(f32[16,8,512]{2,1,0:T(8,128)S(1)} %get-tuple-element.56.early_probe_ref, f32[16,8,512]{2,1,0:T(8,128)S(1)} %get-tuple-element.57.late_probe_ref, bf16[3,512,512]{2,1,0:T(8,128)(2,1)S(1)} %copy-done, bf16[3,512,512]{2,1,0:T(8,128)(2,1)S(1)} %copy-done.1, ...), custom_call_target="tpu_custom_call" | custom-call | flops 1207959552 | bytes 4718592 | tf_op jit(solution)/shard_map/second_push/pallas_call | solution.py:585
  98.7 0.2 collective-permute-done.4.before_ref
  98.9 0.9 correction.1
Async XLA Ops:
  2.9 18.6 %collective-permute-start = (f32[16,16,512]{2,1,0:T(8,128)}, f32[16,16,512]{2,1,0:T(8,128)S(1)}, u32[]{:S(2)}, u32[]{:S(2)}) collective-permute-start(f32[16,16,512]{2,1,0:T(8,128)} %get-tuple-element.34), channel_id=1, source_target_pairs={{1,0},{2,1},{3,2},{4,3},{5,4},{6,5},{7,6},{9,8},{10,9},{11,10},{12... | collective-permute-start | bytes 1572872 | tf_op jit(solution)/shard_map/ppermute | solution.py:30
  11.7 9.8 %collective-permute-start.1 = (f32[8,128]{1,0:T(8,128)}, f32[8,128]{1,0:T(8,128)S(1)}, u32[]{:S(2)}, u32[]{:S(2)}) collective-permute-start(f32[8,128]{1,0:T(8,128)} %get-tuple-element.35), channel_id=1, source_target_pairs={{0,1},{1,2},{2,3},{3,4},{4,5},{5,6},{6,7},{8,9},{9,10},{10,11},{11... | collective-permute-start | bytes 12296 | tf_op jit(solution)/shard_map/ppermute | solution.py:30
  13.7 7.9 %copy-start.2 = (f32[17,8,128]{2,1,0:T(8,128)S(1)}, f32[17,8,128]{2,1,0:T(8,128)}, u32[]{:S(2)}) copy-start(f32[17,8,128]{2,1,0:T(8,128)} %get-tuple-element.32.table_ref) | copy-start | bytes 208900
  13.7 7.9 %copy-start.7 = (f32[2,8192]{1,0:T(2,128)S(1)}, f32[2,8192]{1,0:T(2,128)}, u32[]{:S(2)}) copy-start(f32[2,8192]{1,0:T(2,128)} %upper_ref.3) | copy-start | bytes 196612
  21.5 1.2 %copy-start.6 = (f32[512,512]{1,0:T(8,128)S(1)}, f32[512,512]{1,0:T(8,128)}, u32[]{:S(2)}) copy-start(f32[512,512]{1,0:T(8,128)} %get-tuple-element.33.raw_ref) | copy-start | bytes 3145732
  22.8 61.2 %copy-start.1 = (bf16[3,512,512]{2,1,0:T(8,128)(2,1)S(1)}, bf16[3,512,512]{2,1,0:T(8,128)(2,1)}, u32[]{:S(2)}) copy-start(bf16[3,512,512]{2,1,0:T(8,128)(2,1)} %get-tuple-element.45.low_ref) | copy-start | bytes 4718596
  23.5 60.5 %copy-start = (bf16[3,512,512]{2,1,0:T(8,128)(2,1)S(1)}, bf16[3,512,512]{2,1,0:T(8,128)(2,1)}, u32[]{:S(2)}) copy-start(bf16[3,512,512]{2,1,0:T(8,128)(2,1)} %get-tuple-element.44.high_ref) | copy-start | bytes 4718596
  23.5 60.5 %copy-start.5 = (f32[2,8192]{1,0:T(2,128)S(1)}, f32[2,8192]{1,0:T(2,128)}, u32[]{:S(2)}) copy-start(f32[2,8192]{1,0:T(2,128)} %carry_ref.11) | copy-start | bytes 196612
  23.6 60.5 %copy-start.8 = (s32[2,16,3]{1,0,2:T(2,128)S(1)}, s32[2,16,3]{1,0,2:T(2,128)}, u32[]{:S(2)}) copy-start(s32[2,16,3]{1,0,2:T(2,128)} %param.20) | copy-start | bytes 1156
  23.6 60.5 %copy-start.9 = (s32[2,16,3]{1,0,2:T(2,128)S(1)}, s32[2,16,3]{1,0,2:T(2,128)}, u32[]{:S(2)}) copy-start(s32[2,16,3]{1,0,2:T(2,128)} %param.21) | copy-start | bytes 1156
  77.9 11.7 %collective-permute-start.3 = (f32[16,8,512]{2,1,0:T(8,128)S(1)}, f32[16,8,512]{2,1,0:T(8,128)S(1)}, u32[]{:S(2)}, u32[]{:S(2)}) collective-permute-start(f32[16,8,512]{2,1,0:T(8,128)S(1)} %get-tuple-element.47.late_ref), channel_id=1, source_target_pairs={{0,1},{1,2},{2,3},{3,4},{4,5},{5,6},{6,7},{8,9},{9,10},{10,11},{11... | collective-permute-start | bytes 786440 | tf_op jit(solution)/shard_map/ppermute | solution.py:30
  85.2 8.0 %collective-permute-start.2 = (f32[18,8,512]{2,1,0:T(8,128)S(1)}, f32[18,8,512]{2,1,0:T(8,128)S(1)}, u32[]{:S(2)}, u32[]{:S(2)}) collective-permute-start(f32[18,8,512]{2,1,0:T(8,128)S(1)} %push_first.1), channel_id=1, source_target_pairs={{1,0},{2,1},{3,2},{4,3},{5,4},{6,5},{7,6},{9,8},{10,9},{11,10},{12... | collective-permute-start | bytes 884744 | tf_op jit(solution)/shard_map/ppermute | solution.py:30
  91.6 4.1 %copy-start.3 = (f32[8,2,8192]{2,1,0:T(2,128)S(1)}, f32[8,2,8192]{2,1,0:T(2,128)}, u32[]{:S(2)}) copy-start(f32[8,2,8192]{2,1,0:T(2,128)} %dual_ref.1) | copy-start | bytes 1572868
  91.6 4.1 %copy-start.4 = (f32[8,2,8192]{2,1,0:T(2,128)S(1)}, f32[8,2,8192]{2,1,0:T(2,128)}, u32[]{:S(2)}) copy-start(f32[8,2,8192]{2,1,0:T(2,128)} %demand_ref.1) | copy-start | bytes 1572868
  93.5 5.4 %collective-permute-start.4 = (f32[16,8,512]{2,1,0:T(8,128)S(1)}, f32[16,8,512]{2,1,0:T(8,128)S(1)}, u32[]{:S(2)}, u32[]{:S(2)}) collective-permute-start(f32[16,8,512]{2,1,0:T(8,128)S(1)} %get-tuple-element.57.late_probe_ref), channel_id=1, source_target_pairs={{0,1},{1,2},{2,3},{3,4},{4,5},{5,6},{6,7},{8,9},{9,10},{10,11},{11... | collective-permute-start | bytes 786440 | tf_op jit(solution)/shard_map/ppermute | solution.py:30

commit v6 on v5

--- a/solution.py
+++ b/solution.py
@@ -103,16 +103,16 @@
     return total
 
 
-def scattered_blocks(image_ref, code_refs, out_ref, height):
-    out_ref[...] = jnp.zeros_like(out_ref)
-    for period in range(PER):
-        for block in range(RB):
-            first = (period * RB + block) * height
-            for k in range(NB):
-                which, column = code_of(code_refs, period, block, k)
-                part = image_ref[which, first : first + height, :]
-                place = pl.multiple_of((period * RB + column) * height, height)
-                out_ref[pl.ds(place, height), :] += part
+def scattered_blocks(image_ref, code_refs, out_ref, height, period):
+    top = period * RB * height
+    out_ref[top : top + RB * height, :] = jnp.zeros((RB * height, TILE), F32)
+    for block in range(RB):
+        first = top + block * height
+        for k in range(NB):
+            which, column = code_of(code_refs, period, block, k)
+            part = image_ref[which, first : first + height, :]
+            place = pl.multiple_of((period * RB + column) * height, height)
+            out_ref[pl.ds(place, height), :] += part
 
 
 def fetch(pairs, sems):
@@ -127,7 +127,7 @@
 def carried_kernel(dual_hbm, demand_hbm, carry_hbm, prob_hbm, section_hbm, steps_hbm, subtree_hbm,
                    restart_hbm, carried_ref, late_ref, table_ref,
                    dual_ref, demand_ref, carry_ref, prob_ref, section_ref, steps_ref, subtree_ref,
-                   restart_ref, first_ref, other_ref, sems):
+                   restart_ref, sems):
     copies = fetch(
         [(prob_hbm, prob_ref), (section_hbm, section_ref), (steps_hbm, steps_ref),
          (subtree_hbm, subtree_ref), (restart_hbm, restart_ref), (carry_hbm, carry_ref),
@@ -160,22 +160,17 @@
     late_ref[...] = table_ref[SECTION + 1]
     for copy in copies[6:]:
         copy.wait()
-    for s in range(ROWS):
-        a, b = dual_ref[s, 0:1, :], demand_ref[s, 0:1, :]
-        for block in range(RB):
-            lanes = slice(block * TILE, (block + 1) * TILE)
-            first_ref[block, s : s + 1, :] = a[:, lanes]
-            other_ref[block, s : s + 1, :] = b[:, lanes]
     factor = damps[0] * dual_rate
     for block in range(RB):
+        lanes = slice(block * TILE, (block + 1) * TILE)
         weight = lanes_of(carry_ref, 0, block)
-        a = first_ref[block]
+        a = dual_ref[:, 0, lanes]
         carried_ref[block, 0:ROWS, :] = weight * a
-        carried_ref[block, ROWS : 2 * ROWS, :] = weight * (a + factor * other_ref[block])
+        carried_ref[block, ROWS : 2 * ROWS, :] = weight * (a + factor * demand_ref[:, 0, lanes])
 
 
 def pull_kernel(dual_hbm, demand_hbm, pool_hbm, carry_hbm, cost_hbm, cols_hbm, which_hbm, table_ref,
-                raw_ref, high_hbm, low_hbm, dual_ref, demand_ref, pool_ref, carry_ref, cost_ref,
+                raw_hbm, high_hbm, low_hbm, raw_ref, dual_ref, demand_ref, pool_ref, carry_ref, cost_ref,
                 cols_ref, which_ref, high_ref, low_ref, lhs_ref, image_ref, sems, out_sems):
     copies = fetch(
         [(dual_hbm, dual_ref), (demand_hbm, demand_ref)]
@@ -186,15 +181,13 @@
     copies[0].wait()
     copies[1].wait()
     for period in range(PER):
-        factor = table_ref[DAMP + period, 0:1, 0:1] * table_ref[DUAL_RATE, 0:1, 0:1]
-        for s in range(ROWS):
-            a = dual_ref[s, period : period + 1, :]
-            moved = a + factor * demand_ref[s, period : period + 1, :]
-            for block in range(RB):
-                lanes = slice(block * TILE, (block + 1) * TILE)
-                first = (period * RB + block) * 2 * ROWS + s
-                lhs_ref[first : first + 1, :] = a[:, lanes]
-                lhs_ref[first + ROWS : first + ROWS + 1, :] = moved[:, lanes]
+        factor = entry_of(table_ref, DAMP + period) * entry_of(table_ref, DUAL_RATE)
+        for block in range(RB):
+            lanes = slice(block * TILE, (block + 1) * TILE)
+            first = (period * RB + block) * 2 * ROWS
+            a = dual_ref[:, period, lanes]
+            lhs_ref[first : first + ROWS, :] = a
+            lhs_ref[first + ROWS : first + 2 * ROWS, :] = a + factor * demand_ref[:, period, lanes]
 
     def ready(j):
         copies[2 + j].wait()
@@ -209,9 +202,9 @@
     product_images(lhs_ref, high_ref, low_ref, image_ref, True, ready)
     for copy in copies[5:]:
         copy.wait()
-    scattered_blocks(image_ref, (which_ref, cols_ref), raw_ref, 2 * ROWS)
     rate = jnp.concatenate([entry_of(table_ref, RATE)] * 2, axis=0)
     for period in range(PER):
+        scattered_blocks(image_ref, (which_ref, cols_ref), raw_ref, 2 * ROWS, period)
         for block in range(RB):
             first = (period * RB + block) * 2 * ROWS
             here = slice(first, first + 2 * ROWS)
@@ -220,6 +213,10 @@
                 later = (RB + block) * 2 * ROWS
                 value -= lanes_of(carry_ref, 1, block) * lhs_ref[later : later + 2 * ROWS, :]
             raw_ref[here, :] = rate * value
+        half = pl.ds(period * RB * 2 * ROWS, RB * 2 * ROWS)
+        copy = pltpu.make_async_copy(raw_ref.at[half], raw_hbm.at[half], out_sems.at[6 + period])
+        copy.start()
+        written.append(copy)
     for copy in written:
         copy.wait()
 
@@ -386,7 +383,8 @@
     product_images(lhs_ref, high_ref, low_ref, image_ref, True)
     for copy in copies:
         copy.wait()
-    scattered_blocks(image_ref, code_refs, pulled_ref, ROWS)
+    for period in range(PER):
+        scattered_blocks(image_ref, code_refs, pulled_ref, ROWS, period)
 
 
 def primal_kernel(early_ref, late_ref, pulled_ref, second_ref, near_ref, far_ref, mean_ref,
@@ -420,48 +418,45 @@
 
 def result_kernel(early_probe_ref, late_probe_ref, high_ref, low_ref, dual_ref, demand_ref, net_ref,
                   early_ref, late_ref, new_ref, carry_ref, table_ref, cols_hbm, which_hbm,
-                  primal_ref, out_ref, start_ref, target_ref, lhs_ref, image_ref,
-                  cols_ref, which_ref, sems):
+                  primal_hbm, out_ref, primal_ref, lhs_ref, image_ref,
+                  cols_ref, which_ref, sems, out_sem):
     copies = fetch([(cols_hbm, cols_ref), (which_hbm, which_ref)], sems)
     code_refs = which_ref, cols_ref
     for period in range(PER):
         probe_ref = (early_probe_ref, late_probe_ref)[period]
+        first_ref = (early_ref, late_ref)[period]
+        count = 2.0 * entry_of(table_ref, DAMP + period)
+        flagged = entry_of(table_ref, FLAG + period) == 1.0
+        share = 1.0 / (count + 1.0)
         for block in range(RB):
             first = (period * RB + block) * ROWS
             lhs_ref[first : first + ROWS, :] = probe_ref[block]
-        for s in range(ROWS):
-            a = dual_ref[s, period : period + 1, :]
-            b = demand_ref[s, period : period + 1, :]
-            for block in range(RB):
-                lanes = slice(block * TILE, (block + 1) * TILE)
-                start_ref[period, block, s : s + 1, :] = a[:, lanes]
-                target_ref[period, block, s : s + 1, :] = b[:, lanes]
+            primal_new = new_ref[period, block]
+            primal_mean = (count * (0.5 * first_ref[block]) + primal_new) * share
+            lanes = slice(block * TILE, (block + 1) * TILE)
+            primal_ref[:, period, lanes] = jnp.where(flagged, primal_mean, primal_new)
+    written = pltpu.make_async_copy(primal_ref, primal_hbm, out_sem.at[0])
+    written.start()
     product_images(lhs_ref, high_ref, low_ref, image_ref, False)
     for copy in copies:
         copy.wait()
     dual_rate = entry_of(table_ref, DUAL_RATE)
     for period in range(PER):
-        first_ref = (early_ref, late_ref)[period]
         damp = entry_of(table_ref, DAMP + period)
         count = 2.0 * damp
         flagged = entry_of(table_ref, FLAG + period) == 1.0
         share = 1.0 / (count + 1.0)
         for block in range(RB):
-            start, target = start_ref[period, block], target_ref[period, block]
+            lanes = slice(block * TILE, (block + 1) * TILE)
+            start, target = dual_ref[:, period, lanes], demand_ref[:, period, lanes]
             change = dual_rate * (target - net_ref[period, block])
             image = gathered_blocks(image_ref, code_refs, period, block, ROWS, period)
             if period == 1:
                 image -= lanes_of(carry_ref, 1, block) * early_probe_ref[block]
             dual_new = start + damp * change + dual_rate * (target - image)
             dual_mean = (count * (start + 0.5 * change) + dual_new) * share
-            primal_new = new_ref[period, block]
-            primal_mean = (count * (0.5 * first_ref[block]) + primal_new) * share
-            primal = jnp.where(flagged, primal_mean, primal_new)
-            dual = jnp.where(flagged, dual_mean, dual_new)
-            lanes = slice(block * TILE, (block + 1) * TILE)
-            for s in range(ROWS):
-                primal_ref[s, period : period + 1, lanes] = primal[s : s + 1]
-                out_ref[s, period : period + 1, lanes] = dual[s : s + 1]
+            out_ref[:, period, lanes] = jnp.where(flagged, dual_mean, dual_new)
+    written.wait()
 
 
 def correct_kernel(partial_ref, before_ref, carry_ref, table_ref, out_hbm, out_ref, added_ref, sems):
@@ -524,7 +519,7 @@
             [pltpu.VMEM(dual_start.shape, F32), pltpu.VMEM(dual_start.shape, F32),
              pltpu.VMEM(packed, F32), pltpu.SMEM((ROWS,), F32), pltpu.SMEM((PER,), jnp.int32),
              pltpu.SMEM(step_table.shape[::-1], F32), pltpu.SMEM((SUBTREES,), jnp.int32),
-             pltpu.SMEM(restart.shape, jnp.int32), pltpu.VMEM(slab, F32), pltpu.VMEM(slab, F32),
+             pltpu.SMEM(restart.shape, jnp.int32),
              pltpu.SemaphoreType.DMA((8,))], 60,
         )(dual_start, demand, carry, prob, section_size, step_table.T, subtree_step, restart)
     arriving = shifted(carried, "per", -1)
@@ -533,12 +528,13 @@
         raw, high, low = call(
             pull_kernel, [FAR] * 7 + [VM],
             [((PER * RB * 2 * ROWS, TILE), F32), (tiles, BF16), (tiles, BF16)],
-            [pltpu.VMEM(dual_start.shape, F32), pltpu.VMEM(dual_start.shape, F32),
+            [pltpu.VMEM((PER * RB * 2 * ROWS, TILE), F32),
+             pltpu.VMEM(dual_start.shape, F32), pltpu.VMEM(dual_start.shape, F32),
              pltpu.VMEM(tiles, F32), pltpu.VMEM(packed, F32), pltpu.VMEM(packed, F32),
              pltpu.SMEM((NB, PER, RB), jnp.int32), pltpu.SMEM((NB, PER, RB), jnp.int32),
              pltpu.VMEM(tiles, BF16), pltpu.VMEM(tiles, BF16)]
-            + scratch(2 * ROWS) + [pltpu.SemaphoreType.DMA((9,)), pltpu.SemaphoreType.DMA((6,))],
-            60, [VM, FAR, FAR], 2 * heavy,
+            + scratch(2 * ROWS) + [pltpu.SemaphoreType.DMA((9,)), pltpu.SemaphoreType.DMA((8,))],
+            60, [FAR, FAR, FAR], 2 * heavy,
         )(dual_start, demand, pool_tiles, carry, cost, *codes, table)
     with jax.named_scope("local_average"):
         kept, message, chunk = call(
@@ -584,8 +580,8 @@
     with jax.named_scope("second_push"):
         primal, partial = call(
             result_kernel, [VM] * 12 + [FAR] * 2, [(dual_start.shape, F32), (dual_start.shape, F32)],
-            [pltpu.VMEM(field, F32), pltpu.VMEM(field, F32)] + scratch(ROWS) + code_scratch, 8,
-            work=heavy,
+            [pltpu.VMEM(dual_start.shape, F32)] + scratch(ROWS) + code_scratch
+            + [pltpu.SemaphoreType.DMA((1,))], 8, [FAR, VM], heavy,
         )(early_probe, late_probe, high, low, dual_start, demand, net, early, late, primal_new,
           carry, table, *codes)
     with jax.named_scope("correction"):

time: 100 us -> 99.5 us (level)
  Pallas kernels: 21.7 us -> 20.3 us
  transfers between devices with their start and end apart: 5 -> 5, of which waited for: 2 -> 2; matrix products, arithmetic and copies ran while one was open for 0% -> 0% of each run, Pallas kernels for 16% -> 15%
where the time goes in v6:
time: 99.5 us; the launch traced here: 99.1 us
  blocking collectives  53.2 us (53%)
  starting transfers between devices  20.7 us (21%)
  Pallas kernels  20.3 us (20%)
  waiting for transfers between devices  2.64 us (3%)
  local copies, waits for them, and re-layouts  1.27 us (1%)
    all_to_all x1, blocking collectives, per_device(): got = lax.all_to_all(message, 'scen', 0, 0, tiled=True)  31.2 us
    all_to_all x1, blocking collectives, per_device(): returned = lax.all_to_all(back, 'scen', 0, 0, tiled=True)  22 us
    ppermute x5, starting transfers between devices, shifted(): return lax.ppermute(block, axis, route)  20.7 us
    pallas_call x1, Pallas kernels, per_device(): call(pull_kernel, [FAR] * 7 + [VM], [((PER * RB * 2 * ROWS, TILE), F32),...  7.19 us
    ppermute x5, waiting for transfers between devices, shifted(): return lax.ppermute(block, axis, route)  2.64 us
    pallas_call x1, Pallas kernels, per_device(): call(push_kernel, [VM] * 7 + [FAR] * 2, [(field, F32), (slab, F32)], scra...  2.41 us
    pallas_call x1, Pallas kernels, per_device(): call(result_kernel, [VM] * 12 + [FAR] * 2, [(dual_start.shape, F32), (dua...  2.38 us
    pallas_call x1, Pallas kernels, per_device(): call(carried_kernel, [FAR] * 8, [((RB, 2 * ROWS, TILE), F32), ((ROWS, LAN...  2.26 us
  transfers between devices with their start and end apart: 5, of which 2 were waited for; matrix products, arithmetic and copies ran while one was open for 0% of the time, Pallas kernels for 15%

profile of v6, /device:TPU:1, one launch (start us, length us, event | category | flops | bytes accessed | tf_op | source)
XLA Modules:
  0.0 99.1 jit_solution(11407507329628725695)
XLA Ops:
  0.6 2.3 %carried.1 = (f32[16,16,512]{2,1,0:T(8,128)}, f32[8,128]{1,0:T(8,128)}, f32[17,8,128]{2,1,0:T(8,128)}) custom-call(f32[8,2,8192]{2,1,0:T(2,128)} %dual_ref.1, f32[8,2,8192]{2,1,0:T(2,128)} %demand_ref.1, f32[2,8192]{1,0:T(2,128)} %carry_ref.11, f32[8]{0:T(128)} %prob_hbm.1, s32[2]{0:T(128)} %section_hbm.1, f32[2,4]{1,0:T(2,128)} %bitcast.13, s32[8]{0:T(128)} %subtree_hbm.1, ...), custom_call_target="tpu_custom_call" | custom-call | tf_op jit(solution)/shard_map/carried/pallas_call | solution.py:516
  2.9 8.8 %collective-permute-start = (f32[16,16,512]{2,1,0:T(8,128)}, f32[16,16,512]{2,1,0:T(8,128)S(1)}, u32[]{:S(2)}, u32[]{:S(2)}) collective-permute-start(f32[16,16,512]{2,1,0:T(8,128)} %get-tuple-element.34), channel_id=1, source_target_pairs={{1,0},{2,1},{3,2},{4,3},{5,4},{6,5},{7,6},{9,8},{10,9},{11,10},{12... | collective-permute-start | bytes 1572872 | tf_op jit(solution)/shard_map/ppermute | solution.py:30
  11.7 1.9 %collective-permute-start.1 = (f32[8,128]{1,0:T(8,128)}, f32[8,128]{1,0:T(8,128)S(1)}, u32[]{:S(2)}, u32[]{:S(2)}) collective-permute-start(f32[8,128]{1,0:T(8,128)} %get-tuple-element.35), channel_id=1, source_target_pairs={{0,1},{1,2},{2,3},{3,4},{4,5},{5,6},{6,7},{8,9},{9,10},{10,11},{11... | collective-permute-start | bytes 12296 | tf_op jit(solution)/shard_map/ppermute | solution.py:30
  13.6 0.0 copy-start.2
  13.6 0.0 copy-start.7
  13.6 7.2 %first_pull.1 = (f32[512,512]{1,0:T(8,128)}, bf16[3,512,512]{2,1,0:T(8,128)(2,1)}, bf16[3,512,512]{2,1,0:T(8,128)(2,1)}) custom-call(f32[8,2,8192]{2,1,0:T(2,128)} %dual_ref.1, f32[8,2,8192]{2,1,0:T(2,128)} %demand_ref.1, f32[3,512,512]{2,1,0:T(8,128)} %pool_hbm.1, f32[2,8192]{1,0:T(2,128)} %carry_ref.11, f32[2,8192]{1,0:T(2,128)} %cost_hbm.1, ...), custom_call_target="tpu_custom_call" | custom-call | flops 2415919104 | bytes 9437184 | tf_op jit(solution)/shard_map/first_pull/pallas_call | solution.py:528
  20.8 0.0 collective-permute-done.1.before_ref
  20.9 0.0 collective-permute-done.arriving_ref
  20.9 0.0 copy-done.2
  20.9 0.0 copy-done.7
  20.9 0.0 copy-start.6
  20.9 1.2 %copy-done.6 = f32[512,512]{1,0:T(8,128)S(1)} copy-done((f32[512,512]{1,0:T(8,128)S(1)}, f32[512,512]{1,0:T(8,128)}, u32[]{:S(2)}) %copy-start.6) | copy-done | bytes 1048600
  22.1 0.0 copy-start.1
  22.1 0.8 local_average.1
  22.9 0.0 copy-start
  22.9 0.0 copy-start.5
  22.9 0.0 copy-start.8
  22.9 0.0 copy-start.9
  22.9 31.2 %all_to_all.10.got_ref = f32[64,1,640]{2,1,0:T(1,128)S(1)} all-to-all(f32[64,1,640]{2,1,0:T(1,128)S(1)} %get-tuple-element.36), channel_id=1, replica_groups=mesh['scen'=64,'per'=8] {'scen'}, dimensions={0} | all-to-all | bytes 327680 | tf_op jit(solution)/shard_map/all_to_all | solution.py:544
  54.1 0.7 section_average.1
  54.8 22.0 %all_to_all.11.returned_ref = f32[64,1,768]{2,1,0:T(1,128)S(1)} all-to-all(f32[64,1,768]{2,1,0:T(1,128)S(1)} %get-tuple-element.38), channel_id=1, replica_groups=mesh['scen'=64,'per'=8] {'scen'}, dimensions={0} | all-to-all | bytes 393216 | tf_op jit(solution)/shard_map/all_to_all | solution.py:550
  76.9 0.3 selected.1
  77.2 6.1 %collective-permute-start.3 = (f32[16,8,512]{2,1,0:T(8,128)S(1)}, f32[16,8,512]{2,1,0:T(8,128)S(1)}, u32[]{:S(2)}, u32[]{:S(2)}) collective-permute-start(f32[16,8,512]{2,1,0:T(8,128)S(1)} %get-tuple-element.47.late_ref), channel_id=1, source_target_pairs={{0,1},{1,2},{2,3},{3,4},{4,5},{5,6},{6,7},{8,9},{9,10},{10,11},{11... | collective-permute-start | bytes 786440 | tf_op jit(solution)/shard_map/ppermute | solution.py:30
  83.3 0.0 copy-done.1
  83.3 0.0 copy-done
  83.4 0.0 copy-done.5
  83.4 0.0 copy-done.8
  83.4 0.0 copy-done.9
  83.4 1.2 %push_first.1 = f32[18,8,512]{2,1,0:T(8,128)S(1)} custom-call(f32[16,8,512]{2,1,0:T(8,128)S(1)} %get-tuple-element.43.pushed_ref, bf16[3,512,512]{2,1,0:T(8,128)(2,1)S(1)} %copy-done, bf16[3,512,512]{2,1,0:T(8,128)(2,1)S(1)} %copy-done.1, f32[2,8192]{1,0:T(2,128)S(1)} %copy-done.5, f32[17,8,128]{2,1,0:T(8,128)S(1)} %copy-done.2, s32[3,2,16]{2,1,0:T(2,128)S(1)} %bitcast.4, ...), custom_call_target="tpu_custom_call" | custom-call | flops 603979776 | bytes 2359296 | tf_op jit(solution)/shard_map/push_first/pallas_call | solution.py:558
  84.6 1.9 %collective-permute-start.2 = (f32[18,8,512]{2,1,0:T(8,128)S(1)}, f32[18,8,512]{2,1,0:T(8,128)S(1)}, u32[]{:S(2)}, u32[]{:S(2)}) collective-permute-start(f32[18,8,512]{2,1,0:T(8,128)S(1)} %push_first.1), channel_id=1, source_target_pairs={{1,0},{2,1},{3,2},{4,3},{5,4},{6,5},{7,6},{9,8},{10,9},{11,10},{12... | collective-permute-start | bytes 884744 | tf_op jit(solution)/shard_map/ppermute | solution.py:30
  86.5 2.4 %push.1 = (f32[2,16,8,512]{3,2,1,0:T(8,128)S(1)}, f32[16,8,512]{2,1,0:T(8,128)S(1)}) custom-call(f32[16,8,512]{2,1,0:T(8,128)S(1)} %get-tuple-element.46.early_ref, f32[16,8,512]{2,1,0:T(8,128)S(1)} %get-tuple-element.47.late_ref, f32[16,8,512]{2,1,0:T(8,128)S(1)} %get-tuple-element.48.pushed_ref, bf16[3,512,512]{2,1,0:T(8,128)(2,1)S(1)} %copy-done, ...), custom_call_target="tpu_custom_call" | custom-call | flops 2415919104 | bytes 9437184 | tf_op jit(solution)/shard_map/push/pallas_call | solution.py:565
  88.9 0.0 collective-permute-done.3.before_ref
  89.0 1.9 %second_pull.1 = (f32[2,16,8,512]{3,2,1,0:T(8,128)S(1)}, f32[256,512]{1,0:T(8,128)S(1)}) custom-call(f32[16,8,512]{2,1,0:T(8,128)S(1)} %get-tuple-element.46.early_ref, f32[16,8,512]{2,1,0:T(8,128)S(1)} %collective-permute-done.3.before_ref, f32[2,16,8,512]{3,2,1,0:T(8,128)S(1)} %get-tuple-element.49.images_ref, ...), custom_call_target="tpu_custom_call" | custom-call | flops 1207959552 | bytes 4718592 | tf_op jit(solution)/shard_map/second_pull/pallas_call | solution.py:570
  90.9 0.0 copy-start.3
  90.9 0.0 copy-start.4
  90.9 1.7 %collective-permute-done.2.far_ref = f32[18,8,512]{2,1,0:T(8,128)S(1)} collective-permute-done((f32[18,8,512]{2,1,0:T(8,128)S(1)}, f32[18,8,512]{2,1,0:T(8,128)S(1)}, u32[]{:S(2)}, u32[]{:S(2)}) %collective-permute-start.2) | collective-permute-done | bytes 294944 | tf_op jit(solution)/shard_map/ppermute | solution.py:30
  92.6 0.2 second_primal.1
  92.9 2.0 %collective-permute-start.4 = (f32[16,8,512]{2,1,0:T(8,128)S(1)}, f32[16,8,512]{2,1,0:T(8,128)S(1)}, u32[]{:S(2)}, u32[]{:S(2)}) collective-permute-start(f32[16,8,512]{2,1,0:T(8,128)S(1)} %get-tuple-element.57.late_probe_ref), channel_id=1, source_target_pairs={{0,1},{1,2},{2,3},{3,4},{4,5},{5,6},{6,7},{8,9},{9,10},{10,11},{11... | collective-permute-start | bytes 786440 | tf_op jit(solution)/shard_map/ppermute | solution.py:30
  94.9 0.0 copy-done.3
  95.0 0.0 copy-done.4
  95.0 2.4 %second_push.1 = (f32[8,2,8192]{2,1,0:T(2,128)}, f32[8,2,8192]{2,1,0:T(2,128)S(1)}) custom-call(f32[16,8,512]{2,1,0:T(8,128)S(1)} %get-tuple-element.56.early_probe_ref, f32[16,8,512]{2,1,0:T(8,128)S(1)} %get-tuple-element.57.late_probe_ref, bf16[3,512,512]{2,1,0:T(8,128)(2,1)S(1)} %copy-done, bf16[3,512,512]{2,1,0:T(8,128)(2,1)S(1)} %copy-done.1, ...), custom_call_target="tpu_custom_call" | custom-call | flops 1207959552 | bytes 4718592 | tf_op jit(solution)/shard_map/second_push/pallas_call | solution.py:581
  97.3 0.9 collective-permute-done.4.before_ref
  98.2 0.9 correction.1
Async XLA Ops:
  2.9 18.0 %collective-permute-start = (f32[16,16,512]{2,1,0:T(8,128)}, f32[16,16,512]{2,1,0:T(8,128)S(1)}, u32[]{:S(2)}, u32[]{:S(2)}) collective-permute-start(f32[16,16,512]{2,1,0:T(8,128)} %get-tuple-element.34), channel_id=1, source_target_pairs={{1,0},{2,1},{3,2},{4,3},{5,4},{6,5},{7,6},{9,8},{10,9},{11,10},{12... | collective-permute-start | bytes 1572872 | tf_op jit(solution)/shard_map/ppermute | solution.py:30
  11.7 9.2 %collective-permute-start.1 = (f32[8,128]{1,0:T(8,128)}, f32[8,128]{1,0:T(8,128)S(1)}, u32[]{:S(2)}, u32[]{:S(2)}) collective-permute-start(f32[8,128]{1,0:T(8,128)} %get-tuple-element.35), channel_id=1, source_target_pairs={{0,1},{1,2},{2,3},{3,4},{4,5},{5,6},{6,7},{8,9},{9,10},{10,11},{11... | collective-permute-start | bytes 12296 | tf_op jit(solution)/shard_map/ppermute | solution.py:30
  13.6 7.2 %copy-start.2 = (f32[17,8,128]{2,1,0:T(8,128)S(1)}, f32[17,8,128]{2,1,0:T(8,128)}, u32[]{:S(2)}) copy-start(f32[17,8,128]{2,1,0:T(8,128)} %get-tuple-element.32.table_ref) | copy-start | bytes 208900
  13.6 7.2 %copy-start.7 = (f32[2,8192]{1,0:T(2,128)S(1)}, f32[2,8192]{1,0:T(2,128)}, u32[]{:S(2)}) copy-start(f32[2,8192]{1,0:T(2,128)} %upper_ref.3) | copy-start | bytes 196612
  20.9 1.2 %copy-start.6 = (f32[512,512]{1,0:T(8,128)S(1)}, f32[512,512]{1,0:T(8,128)}, u32[]{:S(2)}) copy-start(f32[512,512]{1,0:T(8,128)} %get-tuple-element.33.raw_ref) | copy-start | bytes 3145732
  22.1 61.2 %copy-start.1 = (bf16[3,512,512]{2,1,0:T(8,128)(2,1)S(1)}, bf16[3,512,512]{2,1,0:T(8,128)(2,1)}, u32[]{:S(2)}) copy-start(bf16[3,512,512]{2,1,0:T(8,128)(2,1)} %get-tuple-element.45.low_ref) | copy-start | bytes 4718596
  22.9 60.5 %copy-start = (bf16[3,512,512]{2,1,0:T(8,128)(2,1)S(1)}, bf16[3,512,512]{2,1,0:T(8,128)(2,1)}, u32[]{:S(2)}) copy-start(bf16[3,512,512]{2,1,0:T(8,128)(2,1)} %get-tuple-element.44.high_ref) | copy-start | bytes 4718596
  22.9 60.5 %copy-start.5 = (f32[2,8192]{1,0:T(2,128)S(1)}, f32[2,8192]{1,0:T(2,128)}, u32[]{:S(2)}) copy-start(f32[2,8192]{1,0:T(2,128)} %carry_ref.11) | copy-start | bytes 196612
  22.9 60.5 %copy-start.8 = (s32[2,16,3]{1,0,2:T(2,128)S(1)}, s32[2,16,3]{1,0,2:T(2,128)}, u32[]{:S(2)}) copy-start(s32[2,16,3]{1,0,2:T(2,128)} %param.20) | copy-start | bytes 1156
  22.9 60.5 %copy-start.9 = (s32[2,16,3]{1,0,2:T(2,128)S(1)}, s32[2,16,3]{1,0,2:T(2,128)}, u32[]{:S(2)}) copy-start(s32[2,16,3]{1,0,2:T(2,128)} %param.21) | copy-start | bytes 1156
  77.2 11.7 %collective-permute-start.3 = (f32[16,8,512]{2,1,0:T(8,128)S(1)}, f32[16,8,512]{2,1,0:T(8,128)S(1)}, u32[]{:S(2)}, u32[]{:S(2)}) collective-permute-start(f32[16,8,512]{2,1,0:T(8,128)S(1)} %get-tuple-element.47.late_ref), channel_id=1, source_target_pairs={{0,1},{1,2},{2,3},{3,4},{4,5},{5,6},{6,7},{8,9},{9,10},{10,11},{11... | collective-permute-start | bytes 786440 | tf_op jit(solution)/shard_map/ppermute | solution.py:30
  84.6 8.0 %collective-permute-start.2 = (f32[18,8,512]{2,1,0:T(8,128)S(1)}, f32[18,8,512]{2,1,0:T(8,128)S(1)}, u32[]{:S(2)}, u32[]{:S(2)}) collective-permute-start(f32[18,8,512]{2,1,0:T(8,128)S(1)} %push_first.1), channel_id=1, source_target_pairs={{1,0},{2,1},{3,2},{4,3},{5,4},{6,5},{7,6},{9,8},{10,9},{11,10},{12... | collective-permute-start | bytes 884744 | tf_op jit(solution)/shard_map/ppermute | solution.py:30
  90.9 4.1 %copy-start.3 = (f32[8,2,8192]{2,1,0:T(2,128)S(1)}, f32[8,2,8192]{2,1,0:T(2,128)}, u32[]{:S(2)}) copy-start(f32[8,2,8192]{2,1,0:T(2,128)} %dual_ref.1) | copy-start | bytes 1572868
  90.9 4.1 %copy-start.4 = (f32[8,2,8192]{2,1,0:T(2,128)S(1)}, f32[8,2,8192]{2,1,0:T(2,128)}, u32[]{:S(2)}) copy-start(f32[8,2,8192]{2,1,0:T(2,128)} %demand_ref.1) | copy-start | bytes 1572868
  92.9 5.3 %collective-permute-start.4 = (f32[16,8,512]{2,1,0:T(8,128)S(1)}, f32[16,8,512]{2,1,0:T(8,128)S(1)}, u32[]{:S(2)}, u32[]{:S(2)}) collective-permute-start(f32[16,8,512]{2,1,0:T(8,128)S(1)} %get-tuple-element.57.late_probe_ref), channel_id=1, source_target_pairs={{0,1},{1,2},{2,3},{3,4},{4,5},{5,6},{6,7},{8,9},{9,10},{10,11},{11... | collective-permute-start | bytes 786440 | tf_op jit(solution)/shard_map/ppermute | solution.py:30

commit v7 on v6

--- a/solution.py
+++ b/solution.py
@@ -1,3 +1,5 @@
+import functools
+
 import jax
 import jax.numpy as jnp
 from jax import lax
@@ -103,15 +105,15 @@
     return total
 
 
-def scattered_blocks(image_ref, code_refs, out_ref, height, period):
-    top = period * RB * height
+def scattered_blocks(image_ref, code_refs, out_ref, height, period, slot):
+    top = slot * RB * height
     out_ref[top : top + RB * height, :] = jnp.zeros((RB * height, TILE), F32)
     for block in range(RB):
         first = top + block * height
         for k in range(NB):
             which, column = code_of(code_refs, period, block, k)
             part = image_ref[which, first : first + height, :]
-            place = pl.multiple_of((period * RB + column) * height, height)
+            place = pl.multiple_of((slot * RB + column) * height, height)
             out_ref[pl.ds(place, height), :] += part
 
 
@@ -204,7 +206,7 @@
         copy.wait()
     rate = jnp.concatenate([entry_of(table_ref, RATE)] * 2, axis=0)
     for period in range(PER):
-        scattered_blocks(image_ref, (which_ref, cols_ref), raw_ref, 2 * ROWS, period)
+        scattered_blocks(image_ref, (which_ref, cols_ref), raw_ref, 2 * ROWS, period, period)
         for block in range(RB):
             first = (period * RB + block) * 2 * ROWS
             here = slice(first, first + 2 * ROWS)
@@ -344,80 +346,79 @@
         first_ref[RB + block // ROWS, row : row + 1, :] = 0.5 * factor[0:1] * carry * carry
 
 
-def push_kernel(early_ref, late_ref, pushed_ref, high_ref, low_ref, carry_ref, table_ref,
-                cols_hbm, which_hbm, image_out_ref, next_ref, lhs_ref, image_ref,
-                cols_ref, which_ref, sems):
+def push_late_kernel(late_ref, high_ref, low_ref, cols_hbm, which_hbm, out_ref, lhs_ref, image_ref,
+                     cols_ref, which_ref, sems):
+    copies = fetch([(cols_hbm, cols_ref), (which_hbm, which_ref)], sems)
+    for block in range(RB):
+        lhs_ref[block * ROWS : (block + 1) * ROWS, :] = late_ref[block]
+    product_images(lhs_ref, high_ref, low_ref, image_ref, False)
+    for copy in copies:
+        copy.wait()
+    for block in range(RB):
+        out_ref[block] = gathered_blocks(image_ref, (which_ref, cols_ref), 1, block, ROWS, 0)
+
+
+def push_early_kernel(early_ref, pushed_ref, high_ref, low_ref, carry_ref, table_ref,
+                      cols_hbm, which_hbm, out_ref, next_ref, lhs_ref, image_ref,
+                      cols_ref, which_ref, sems):
     copies = fetch([(cols_hbm, cols_ref), (which_hbm, which_ref)], sems)
     code_refs = which_ref, cols_ref
-    for slot, field_ref in enumerate((early_ref, late_ref, pushed_ref)):
+    for slot, slab_ref in enumerate((early_ref, pushed_ref)):
         for block in range(RB):
             first = (slot * RB + block) * ROWS
-            lhs_ref[first : first + ROWS, :] = field_ref[block]
+            lhs_ref[first : first + ROWS, :] = slab_ref[block]
     product_images(lhs_ref, high_ref, low_ref, image_ref, False)
     for copy in copies:
         copy.wait()
     factor = 2.0 * entry_of(table_ref, DAMP + 1)
     for block in range(RB):
-        for period in range(PER):
-            image_out_ref[period, block] = gathered_blocks(
-                image_ref, code_refs, period, block, ROWS, period
-            )
-        image = gathered_blocks(image_ref, code_refs, 1, block, ROWS, 2)
+        out_ref[block] = gathered_blocks(image_ref, code_refs, 0, block, ROWS, 0)
+        image = gathered_blocks(image_ref, code_refs, 1, block, ROWS, 1)
         next_ref[block] = factor * lanes_of(carry_ref, 1, block) * image
 
 
-def net_kernel(early_ref, before_ref, images_ref, mean_ref, carry_ref, high_ref, low_ref, table_ref,
+def net_kernel(period, previous_ref, images_ref, mean_ref, carry_ref, high_ref, low_ref, table_ref,
                cols_hbm, which_hbm, net_ref, pulled_ref, lhs_ref, image_ref,
                cols_ref, which_ref, sems):
     copies = fetch([(cols_hbm, cols_ref), (which_hbm, which_ref)], sems)
-    code_refs = which_ref, cols_ref
-    for period in range(PER):
-        previous_ref = (before_ref, early_ref)[period]
-        factor = entry_of(table_ref, DAMP + period) * widened(mean_ref[period])
-        for block in range(RB):
-            carry = lanes_of(carry_ref, period, block)
-            net = 2.0 * (images_ref[period, block] - carry * previous_ref[block])
-            net_ref[period, block] = net
-            first = (period * RB + block) * ROWS
-            lhs_ref[first : first + ROWS, :] = factor * net
+    factor = entry_of(table_ref, DAMP + period) * widened(mean_ref[period])
+    for block in range(RB):
+        carry = lanes_of(carry_ref, period, block)
+        net = 2.0 * (images_ref[block] - carry * previous_ref[block])
+        net_ref[block] = net
+        lhs_ref[block * ROWS : (block + 1) * ROWS, :] = factor * net
     product_images(lhs_ref, high_ref, low_ref, image_ref, True)
     for copy in copies:
         copy.wait()
-    for period in range(PER):
-        scattered_blocks(image_ref, code_refs, pulled_ref, ROWS, period)
-
-
-def primal_kernel(early_ref, late_ref, pulled_ref, second_ref, near_ref, far_ref, mean_ref,
-                  upper_ref, carry_ref, table_ref, primal_ref, early_probe_ref, late_probe_ref):
-    for period in range(PER):
-        new_ref = (early_ref, late_ref)[period]
-        next_ref = (near_ref, far_ref)[period]
-        probe_ref = (early_probe_ref, late_probe_ref)[period]
-        damp = entry_of(table_ref, DAMP + period)
-        mean = 2.0 * widened(mean_ref[period])
+    scattered_blocks(image_ref, (which_ref, cols_ref), pulled_ref, ROWS, period, 0)
+
+
+def primal_kernel(period, new_ref, pulled_ref, second_ref, next_ref, mean_ref, upper_ref, carry_ref,
+                  table_ref, primal_ref, probe_ref):
+    damp = entry_of(table_ref, DAMP + period)
+    mean = 2.0 * widened(mean_ref[period])
+    if period == 0:
+        mean *= entry_of(table_ref, DAMP + 1)
+    for block in range(RB):
         if period == 0:
-            mean *= entry_of(table_ref, DAMP + 1)
-        for block in range(RB):
-            if period == 0:
-                carry = lanes_of(carry_ref, 1, block)
-                square = carry * carry
-            else:
-                row = block % ROWS
-                square = far_ref[RB + block // ROWS, row : row + 1, :]
-            first = (period * RB + block) * ROWS
-            new = new_ref[block]
-            primal = damp * new
-            averaged = (
-                primal + second_ref[period, block] - pulled_ref[first : first + ROWS, :]
-                + next_ref[block] - square * mean * new
-            )
-            primal_new = jnp.minimum(jnp.maximum(averaged, 0.0), lanes_of(upper_ref, period, block))
-            primal_ref[period, block] = primal_new
-            probe_ref[block] = 2.0 * primal_new - primal
-
-
-def result_kernel(early_probe_ref, late_probe_ref, high_ref, low_ref, dual_ref, demand_ref, net_ref,
-                  early_ref, late_ref, new_ref, carry_ref, table_ref, cols_hbm, which_hbm,
+            carry = lanes_of(carry_ref, 1, block)
+            square = carry * carry
+        else:
+            row = block % ROWS
+            square = next_ref[RB + block // ROWS, row : row + 1, :]
+        new = new_ref[block]
+        primal = damp * new
+        averaged = (
+            primal + second_ref[period, block] - pulled_ref[block * ROWS : (block + 1) * ROWS, :]
+            + next_ref[block] - square * mean * new
+        )
+        primal_new = jnp.minimum(jnp.maximum(averaged, 0.0), lanes_of(upper_ref, period, block))
+        primal_ref[block] = primal_new
+        probe_ref[block] = 2.0 * primal_new - primal
+
+
+def result_kernel(early_probe_ref, late_probe_ref, high_ref, low_ref, dual_ref, demand_ref, early_net_ref,
+                  late_net_ref, early_ref, late_ref, early_new_ref, late_new_ref, carry_ref, table_ref, cols_hbm, which_hbm,
                   primal_hbm, out_ref, primal_ref, lhs_ref, image_ref,
                   cols_ref, which_ref, sems, out_sem):
     copies = fetch([(cols_hbm, cols_ref), (which_hbm, which_ref)], sems)
@@ -431,7 +432,7 @@
         for block in range(RB):
             first = (period * RB + block) * ROWS
             lhs_ref[first : first + ROWS, :] = probe_ref[block]
-            primal_new = new_ref[period, block]
+            primal_new = (early_new_ref, late_new_ref)[period][block]
             primal_mean = (count * (0.5 * first_ref[block]) + primal_new) * share
             lanes = slice(block * TILE, (block + 1) * TILE)
             primal_ref[:, period, lanes] = jnp.where(flagged, primal_mean, primal_new)
@@ -449,7 +450,7 @@
         for block in range(RB):
             lanes = slice(block * TILE, (block + 1) * TILE)
             start, target = dual_ref[:, period, lanes], demand_ref[:, period, lanes]
-            change = dual_rate * (target - net_ref[period, block])
+            change = dual_rate * (target - (early_net_ref, late_net_ref)[period][block])
             image = gathered_blocks(image_ref, code_refs, period, block, ROWS, period)
             if period == 1:
                 image -= lanes_of(carry_ref, 1, block) * early_probe_ref[block]
@@ -560,30 +561,44 @@
             scratch(ROWS, 1) + code_scratch, 6, work=heavy // 2,
         )(pushed_first, high, low, carry, table, *codes)
     far = shifted(first, "per", -1)
-    early, late, pushed_next, first = lax.optimization_barrier((early, late, pushed_next, first))
-    with jax.named_scope("push"):
+    late, first = lax.optimization_barrier((late, first))
+    pulled_rows = (RB * ROWS, TILE)
+
+    def pulled_of(period, previous, images):
+        return call(
+            functools.partial(net_kernel, period), [VM] * 7 + [FAR] * 2,
+            [(slab, F32), (pulled_rows, F32)], scratch(ROWS, 1) + code_scratch, 6, work=heavy // 2,
+        )(previous, images, mean, carry, high, low, table, *codes)
+
+    def primal_of(period, new, pulled, following):
+        return call(
+            functools.partial(primal_kernel, period), [VM] * 8, [(slab, F32), (slab, F32)],
+        )(new, pulled, second, following, mean, upper, carry, table)
+
+    with jax.named_scope("late_period"):
+        (images,) = call(
+            push_late_kernel, [VM] * 3 + [FAR] * 2, [(slab, F32)],
+            scratch(ROWS, 1) + code_scratch, 6, work=heavy // 2,
+        )(late, high, low, *codes)
+        late_net, pulled = pulled_of(1, early, images)
+        far, pulled = lax.optimization_barrier((far, pulled))
+        late_new, late_probe = primal_of(1, late, pulled, far)
+    probe_before = shifted(late_probe, "per", 1)
+    early, pushed_next, late_probe = lax.optimization_barrier((early, pushed_next, late_probe))
+    with jax.named_scope("early_period"):
         images, near = call(
-            push_kernel, [VM] * 7 + [FAR] * 2, [(field, F32), (slab, F32)],
-            scratch(ROWS, 3) + code_scratch, 10, work=2 * heavy,
-        )(early, late, pushed_next, high, low, carry, table, *codes)
-    with jax.named_scope("second_pull"):
-        net, pulled = call(
-            net_kernel, [VM] * 8 + [FAR] * 2, [(field, F32), ((PER * RB * ROWS, TILE), F32)],
+            push_early_kernel, [VM] * 6 + [FAR] * 2, [(slab, F32), (slab, F32)],
             scratch(ROWS) + code_scratch, 8, work=heavy,
-        )(early, new_before, images, mean, carry, high, low, table, *codes)
-    far, pulled = lax.optimization_barrier((far, pulled))
-    with jax.named_scope("second_primal"):
-        primal_new, early_probe, late_probe = call(
-            primal_kernel, [VM] * 10, [(field, F32), (slab, F32), (slab, F32)],
-        )(early, late, pulled, second, near, far, mean, upper, carry, table)
-    probe_before = shifted(late_probe, "per", 1)
+        )(early, pushed_next, high, low, carry, table, *codes)
+        early_net, pulled = pulled_of(0, new_before, images)
+        early_new, early_probe = primal_of(0, early, pulled, near)
     with jax.named_scope("second_push"):
         primal, partial = call(
-            result_kernel, [VM] * 12 + [FAR] * 2, [(dual_start.shape, F32), (dual_start.shape, F32)],
+            result_kernel, [VM] * 14 + [FAR] * 2, [(dual_start.shape, F32), (dual_start.shape, F32)],
             [pltpu.VMEM(dual_start.shape, F32)] + scratch(ROWS) + code_scratch
             + [pltpu.SemaphoreType.DMA((1,))], 8, [FAR, VM], heavy,
-        )(early_probe, late_probe, high, low, dual_start, demand, net, early, late, primal_new,
-          carry, table, *codes)
+        )(early_probe, late_probe, high, low, dual_start, demand, early_net, late_net, early, late,
+          early_new, late_new, carry, table, *codes)
     with jax.named_scope("correction"):
         (dual,) = call(
             correct_kernel, [VM] * 4, [(dual_start.shape, F32)],

time: 99.5 us -> 99.4 us (level)
  waiting for transfers between devices: 2.64 us -> 0.19 us
  local copies, waits for them, and re-layouts: 1.27 us -> 2.32 us
    ppermute x5, waiting for transfers between devices: 2.64 us -> 0.19 us  [shifted(): return lax.ppermute(block, axis, route)]
    unnamed x20, local copies, waits for them, and re-layouts: 1.27 us -> 2.32 us
    pallas_call x4 -> x7, Pallas kernels: 6.95 us -> 7.66 us  [the longest x1 2.38 us: per_device(): call(result_kernel, [VM] * 14 + [FAR] * 2, [(dual_start.shape, F32), (dua...]
  transfers between devices with their start and end apart: 5 -> 5, of which waited for: 2 -> 1; matrix products, arithmetic and copies ran while one was open for 0% -> 0% of each run, Pallas kernels for 15% -> 15%
where the time goes in v7:
time: 99.4 us; the launch traced here: 99 us
  blocking collectives  52.9 us (53%)
  starting transfers between devices  21.4 us (22%)
  Pallas kernels  21 us (21%)
  local copies, waits for them, and re-layouts  2.32 us (2%)
  between operations  1.08 us (1%)
    all_to_all x1, blocking collectives, per_device(): got = lax.all_to_all(message, 'scen', 0, 0, tiled=True)  31.2 us
    all_to_all x1, blocking collectives, per_device(): returned = lax.all_to_all(back, 'scen', 0, 0, tiled=True)  21.8 us
    ppermute x5, starting transfers between devices, shifted(): return lax.ppermute(block, axis, route)  21.4 us
    pallas_call x1, Pallas kernels, per_device(): call(pull_kernel, [FAR] * 7 + [VM], [((PER * RB * 2 * ROWS, TILE), F32),...  7.18 us
    pallas_call x1, Pallas kernels, per_device(): call(result_kernel, [VM] * 14 + [FAR] * 2, [(dual_start.shape, F32), (dua...  2.38 us
    unnamed x20, local copies, waits for them, and re-layouts  2.32 us
    pallas_call x1, Pallas kernels, per_device(): call(carried_kernel, [FAR] * 8, [((RB, 2 * ROWS, TILE), F32), ((ROWS, LAN...  2.26 us
    pallas_call x2, Pallas kernels, pulled_of(): call(functools.partial(net_kernel, period), [VM] * 7 + [FAR] * 2, [(slab,...  2.13 us
  transfers between devices with their start and end apart: 5, of which 1 were waited for; matrix products, arithmetic and copies ran while one was open for 0% of the time, Pallas kernels for 15%

profile of v7, /device:TPU:1, one launch (start us, length us, event | category | flops | bytes accessed | tf_op | source)
XLA Modules:
  0.0 99.0 jit_solution(10290005492722581713)
XLA Ops:
  0.6 2.3 %carried.1 = (f32[16,16,512]{2,1,0:T(8,128)}, f32[8,128]{1,0:T(8,128)}, f32[17,8,128]{2,1,0:T(8,128)}) custom-call(f32[8,2,8192]{2,1,0:T(2,128)} %dual_ref.1, f32[8,2,8192]{2,1,0:T(2,128)} %demand_ref.1, f32[2,8192]{1,0:T(2,128)} %carry_ref.15, f32[8]{0:T(128)} %prob_hbm.1, s32[2]{0:T(128)} %section_hbm.1, f32[2,4]{1,0:T(2,128)} %bitcast.17, s32[8]{0:T(128)} %subtree_hbm.1, ...), custom_call_target="tpu_custom_call" | custom-call | tf_op jit(solution)/shard_map/carried/pallas_call | solution.py:517
  2.9 8.8 %collective-permute-start = (f32[16,16,512]{2,1,0:T(8,128)}, f32[16,16,512]{2,1,0:T(8,128)S(1)}, u32[]{:S(2)}, u32[]{:S(2)}) collective-permute-start(f32[16,16,512]{2,1,0:T(8,128)} %get-tuple-element.38), channel_id=1, source_target_pairs={{1,0},{2,1},{3,2},{4,3},{5,4},{6,5},{7,6},{9,8},{10,9},{11,10},{12... | collective-permute-start | bytes 1572872 | tf_op jit(solution)/shard_map/ppermute | solution.py:32
  11.7 1.9 %collective-permute-start.1 = (f32[8,128]{1,0:T(8,128)}, f32[8,128]{1,0:T(8,128)S(1)}, u32[]{:S(2)}, u32[]{:S(2)}) collective-permute-start(f32[8,128]{1,0:T(8,128)} %get-tuple-element.39), channel_id=1, source_target_pairs={{0,1},{1,2},{2,3},{3,4},{4,5},{5,6},{6,7},{8,9},{9,10},{10,11},{11... | collective-permute-start | bytes 12296 | tf_op jit(solution)/shard_map/ppermute | solution.py:32
  13.6 0.0 copy-start.2
  13.6 0.0 copy-start.7
  13.6 7.2 %first_pull.1 = (f32[512,512]{1,0:T(8,128)}, bf16[3,512,512]{2,1,0:T(8,128)(2,1)}, bf16[3,512,512]{2,1,0:T(8,128)(2,1)}) custom-call(f32[8,2,8192]{2,1,0:T(2,128)} %dual_ref.1, f32[8,2,8192]{2,1,0:T(2,128)} %demand_ref.1, f32[3,512,512]{2,1,0:T(8,128)} %pool_hbm.1, f32[2,8192]{1,0:T(2,128)} %carry_ref.15, f32[2,8192]{1,0:T(2,128)} %cost_hbm.1, ...), custom_call_target="tpu_custom_call" | custom-call | flops 2415919104 | bytes 9437184 | tf_op jit(solution)/shard_map/first_pull/pallas_call | solution.py:529
  20.8 0.0 collective-permute-done.1.before_ref
  20.8 0.0 collective-permute-done.arriving_ref
  20.9 0.0 copy-done.2
  20.9 0.0 copy-done.7
  20.9 0.0 copy-start.6
  20.9 1.2 %copy-done.6 = f32[512,512]{1,0:T(8,128)S(1)} copy-done((f32[512,512]{1,0:T(8,128)S(1)}, f32[512,512]{1,0:T(8,128)}, u32[]{:S(2)}) %copy-start.6) | copy-done | bytes 1048600
  22.1 0.0 copy-start.1
  22.1 0.8 local_average.1
  22.9 0.0 copy-start
  22.9 0.0 copy-start.3
  22.9 0.0 copy-start.8
  22.9 0.0 copy-start.9
  22.9 31.2 %all_to_all.10.got_ref = f32[64,1,640]{2,1,0:T(1,128)S(1)} all-to-all(f32[64,1,640]{2,1,0:T(1,128)S(1)} %get-tuple-element.40), channel_id=1, replica_groups=mesh['scen'=64,'per'=8] {'scen'}, dimensions={0} | all-to-all | bytes 327680 | tf_op jit(solution)/shard_map/all_to_all | solution.py:545
  54.1 0.7 section_average.1
  54.8 21.8 %all_to_all.11.returned_ref = f32[64,1,768]{2,1,0:T(1,128)S(1)} all-to-all(f32[64,1,768]{2,1,0:T(1,128)S(1)} %get-tuple-element.42), channel_id=1, replica_groups=mesh['scen'=64,'per'=8] {'scen'}, dimensions={0} | all-to-all | bytes 393216 | tf_op jit(solution)/shard_map/all_to_all | solution.py:551
  76.6 0.3 selected.1
  76.9 0.0 copy-done.1
  77.0 0.0 copy-done
  77.0 0.0 copy-done.3
  77.0 0.0 copy-done.8
  77.0 0.0 copy-done.9
  77.0 1.2 %push_first.1 = f32[18,8,512]{2,1,0:T(8,128)S(1)} custom-call(f32[16,8,512]{2,1,0:T(8,128)S(1)} %get-tuple-element.47.pushed_ref, bf16[3,512,512]{2,1,0:T(8,128)(2,1)S(1)} %copy-done, bf16[3,512,512]{2,1,0:T(8,128)(2,1)S(1)} %copy-done.1, f32[2,8192]{1,0:T(2,128)S(1)} %copy-done.3, f32[17,8,128]{2,1,0:T(8,128)S(1)} %copy-done.2, s32[3,2,16]{2,1,0:T(2,128)S(1)} %bitcast.4, ...), custom_call_target="tpu_custom_call" | custom-call | flops 603979776 | bytes 2359296 | tf_op jit(solution)/shard_map/push_first/pallas_call | solution.py:559
  78.2 5.2 %collective-permute-start.2 = (f32[18,8,512]{2,1,0:T(8,128)S(1)}, f32[18,8,512]{2,1,0:T(8,128)S(1)}, u32[]{:S(2)}, u32[]{:S(2)}) collective-permute-start(f32[18,8,512]{2,1,0:T(8,128)S(1)} %push_first.1), channel_id=1, source_target_pairs={{1,0},{2,1},{3,2},{4,3},{5,4},{6,5},{7,6},{9,8},{10,9},{11,10},{12... | collective-permute-start | bytes 884744 | tf_op jit(solution)/shard_map/ppermute | solution.py:32
  83.4 3.1 %collective-permute-start.3 = (f32[16,8,512]{2,1,0:T(8,128)S(1)}, f32[16,8,512]{2,1,0:T(8,128)S(1)}, u32[]{:S(2)}, u32[]{:S(2)}) collective-permute-start(f32[16,8,512]{2,1,0:T(8,128)S(1)} %get-tuple-element.50.late_ref.new_ref), channel_id=1, source_target_pairs={{0,1},{1,2},{2,3},{3,4},{4,5},{5,6},{6,7},{8,9},{9,10},{10,11},{11... | collective-permute-start | bytes 786440 | tf_op jit(solution)/shard_map/ppermute | solution.py:32
  86.5 1.2 %late_period.3.images_ref = f32[16,8,512]{2,1,0:T(8,128)S(1)} custom-call(f32[16,8,512]{2,1,0:T(8,128)S(1)} %get-tuple-element.50.late_ref.new_ref, bf16[3,512,512]{2,1,0:T(8,128)(2,1)S(1)} %copy-done, bf16[3,512,512]{2,1,0:T(8,128)(2,1)S(1)} %copy-done.1, s32[3,2,16]{2,1,0:T(2,128)S(1)} %bitcast.5, s32[3,2,16]{2,1,0:T(2,128)S(1)} %bitcast.12), custom_call_target="tpu_custom_call" | custom-call | flops 603979776 | bytes 2359296 | tf_op jit(solution)/shard_map/late_period/pallas_call | solution.py:579
  87.7 1.1 %late_period.4 = (f32[16,8,512]{2,1,0:T(8,128)S(1)}, f32[128,512]{1,0:T(8,128)S(1)}) custom-call(f32[16,8,512]{2,1,0:T(8,128)S(1)} %get-tuple-element.57.previous_ref.early_ref.new_ref, f32[16,8,512]{2,1,0:T(8,128)S(1)} %late_period.3.images_ref, f32[2,8,128]{2,1,0:T(8,128)S(1)} %get-tuple-element.51.mean_ref, f32[2,8192]{1,0:T(2,128)S(1)} %copy-done.3, ...), custom_call_target="tpu_custom_call" | custom-call | flops 603979776 | bytes 2359296 | tf_op jit(solution)/shard_map/late_period/pallas_call | solution.py:568
  88.8 0.2 collective-permute-done.2.next_ref
  89.0 0.1 late_period.5
  89.1 2.4 %collective-permute-start.4 = (f32[16,8,512]{2,1,0:T(8,128)S(1)}, f32[16,8,512]{2,1,0:T(8,128)S(1)}, u32[]{:S(2)}, u32[]{:S(2)}) collective-permute-start(f32[16,8,512]{2,1,0:T(8,128)S(1)} %get-tuple-element.63.late_probe_ref), channel_id=1, source_target_pairs={{0,1},{1,2},{2,3},{3,4},{4,5},{5,6},{6,7},{8,9},{9,10},{10,11},{11... | collective-permute-start | bytes 786440 | tf_op jit(solution)/shard_map/ppermute | solution.py:32
  91.5 1.7 %early_period.3 = (f32[16,8,512]{2,1,0:T(8,128)S(1)}, f32[16,8,512]{2,1,0:T(8,128)S(1)}) custom-call(f32[16,8,512]{2,1,0:T(8,128)S(1)} %get-tuple-element.57.previous_ref.early_ref.new_ref, f32[16,8,512]{2,1,0:T(8,128)S(1)} %get-tuple-element.58.pushed_ref, bf16[3,512,512]{2,1,0:T(8,128)(2,1)S(1)} %copy-done, bf16[3,512,512]{2,1,0:T(8,128)(2,1)S(1)} %copy-done.1, ...), custom_call_target="tpu_custom_call" | custom-call | flops 1207959552 | bytes 4718592 | tf_op jit(solution)/shard_map/early_period/pallas_call | solution.py:589
  93.3 0.0 collective-permute-done.3.previous_ref
  93.3 1.1 %early_period.4 = (f32[16,8,512]{2,1,0:T(8,128)S(1)}, f32[128,512]{1,0:T(8,128)S(1)}) custom-call(f32[16,8,512]{2,1,0:T(8,128)S(1)} %collective-permute-done.3.previous_ref, f32[16,8,512]{2,1,0:T(8,128)S(1)} %get-tuple-element.59.images_ref, f32[2,8,128]{2,1,0:T(8,128)S(1)} %get-tuple-element.51.mean_ref, f32[2,8192]{1,0:T(2,128)S(1)} %copy-done.3, ...), custom_call_target="tpu_custom_call" | custom-call | flops 603979776 | bytes 2359296 | tf_op jit(solution)/shard_map/early_period/pallas_call | solution.py:568
  94.3 0.0 copy-start.4
  94.4 0.0 copy-start.5
  94.4 0.1 early_period.5
  94.5 0.9 copy-done.4
  95.4 0.2 copy-done.5
  95.6 2.4 %second_push.1 = (f32[8,2,8192]{2,1,0:T(2,128)}, f32[8,2,8192]{2,1,0:T(2,128)S(1)}) custom-call(f32[16,8,512]{2,1,0:T(8,128)S(1)} %get-tuple-element.62.early_probe_ref, f32[16,8,512]{2,1,0:T(8,128)S(1)} %get-tuple-element.63.late_probe_ref, bf16[3,512,512]{2,1,0:T(8,128)(2,1)S(1)} %copy-done, bf16[3,512,512]{2,1,0:T(8,128)(2,1)S(1)} %copy-done.1, ...), custom_call_target="tpu_custom_call" | custom-call | flops 1207959552 | bytes 4718592 | tf_op jit(solution)/shard_map/second_push/pallas_call | solution.py:596
  97.9 0.0 collective-permute-done.4.before_ref
  97.9 0.9 correction.1
Async XLA Ops:
  2.9 17.9 %collective-permute-start = (f32[16,16,512]{2,1,0:T(8,128)}, f32[16,16,512]{2,1,0:T(8,128)S(1)}, u32[]{:S(2)}, u32[]{:S(2)}) collective-permute-start(f32[16,16,512]{2,1,0:T(8,128)} %get-tuple-element.38), channel_id=1, source_target_pairs={{1,0},{2,1},{3,2},{4,3},{5,4},{6,5},{7,6},{9,8},{10,9},{11,10},{12... | collective-permute-start | bytes 1572872 | tf_op jit(solution)/shard_map/ppermute | solution.py:32
  11.7 9.1 %collective-permute-start.1 = (f32[8,128]{1,0:T(8,128)}, f32[8,128]{1,0:T(8,128)S(1)}, u32[]{:S(2)}, u32[]{:S(2)}) collective-permute-start(f32[8,128]{1,0:T(8,128)} %get-tuple-element.39), channel_id=1, source_target_pairs={{0,1},{1,2},{2,3},{3,4},{4,5},{5,6},{6,7},{8,9},{9,10},{10,11},{11... | collective-permute-start | bytes 12296 | tf_op jit(solution)/shard_map/ppermute | solution.py:32
  13.6 7.2 %copy-start.2 = (f32[17,8,128]{2,1,0:T(8,128)S(1)}, f32[17,8,128]{2,1,0:T(8,128)}, u32[]{:S(2)}) copy-start(f32[17,8,128]{2,1,0:T(8,128)} %get-tuple-element.36.table_ref) | copy-start | bytes 208900
  13.6 7.2 %copy-start.7 = (f32[2,8192]{1,0:T(2,128)S(1)}, f32[2,8192]{1,0:T(2,128)}, u32[]{:S(2)}) copy-start(f32[2,8192]{1,0:T(2,128)} %upper_ref.5) | copy-start | bytes 196612
  20.9 1.2 %copy-start.6 = (f32[512,512]{1,0:T(8,128)S(1)}, f32[512,512]{1,0:T(8,128)}, u32[]{:S(2)}) copy-start(f32[512,512]{1,0:T(8,128)} %get-tuple-element.37.raw_ref) | copy-start | bytes 3145732
  22.1 54.8 %copy-start.1 = (bf16[3,512,512]{2,1,0:T(8,128)(2,1)S(1)}, bf16[3,512,512]{2,1,0:T(8,128)(2,1)}, u32[]{:S(2)}) copy-start(bf16[3,512,512]{2,1,0:T(8,128)(2,1)} %get-tuple-element.49.low_ref) | copy-start | bytes 4718596
  22.9 54.1 %copy-start = (bf16[3,512,512]{2,1,0:T(8,128)(2,1)S(1)}, bf16[3,512,512]{2,1,0:T(8,128)(2,1)}, u32[]{:S(2)}) copy-start(bf16[3,512,512]{2,1,0:T(8,128)(2,1)} %get-tuple-element.48.high_ref) | copy-start | bytes 4718596
  22.9 54.1 %copy-start.3 = (f32[2,8192]{1,0:T(2,128)S(1)}, f32[2,8192]{1,0:T(2,128)}, u32[]{:S(2)}) copy-start(f32[2,8192]{1,0:T(2,128)} %carry_ref.15) | copy-start | bytes 196612
  22.9 54.1 %copy-start.8 = (s32[2,16,3]{1,0,2:T(2,128)S(1)}, s32[2,16,3]{1,0,2:T(2,128)}, u32[]{:S(2)}) copy-start(s32[2,16,3]{1,0,2:T(2,128)} %param.20) | copy-start | bytes 1156
  22.9 54.1 %copy-start.9 = (s32[2,16,3]{1,0,2:T(2,128)S(1)}, s32[2,16,3]{1,0,2:T(2,128)}, u32[]{:S(2)}) copy-start(s32[2,16,3]{1,0,2:T(2,128)} %param.21) | copy-start | bytes 1156
  78.2 10.8 %collective-permute-start.2 = (f32[18,8,512]{2,1,0:T(8,128)S(1)}, f32[18,8,512]{2,1,0:T(8,128)S(1)}, u32[]{:S(2)}, u32[]{:S(2)}) collective-permute-start(f32[18,8,512]{2,1,0:T(8,128)S(1)} %push_first.1), channel_id=1, source_target_pairs={{1,0},{2,1},{3,2},{4,3},{5,4},{6,5},{7,6},{9,8},{10,9},{11,10},{12... | collective-permute-start | bytes 884744 | tf_op jit(solution)/shard_map/ppermute | solution.py:32
  83.4 9.9 %collective-permute-start.3 = (f32[16,8,512]{2,1,0:T(8,128)S(1)}, f32[16,8,512]{2,1,0:T(8,128)S(1)}, u32[]{:S(2)}, u32[]{:S(2)}) collective-permute-start(f32[16,8,512]{2,1,0:T(8,128)S(1)} %get-tuple-element.50.late_ref.new_ref), channel_id=1, source_target_pairs={{0,1},{1,2},{2,3},{3,4},{4,5},{5,6},{6,7},{8,9},{9,10},{10,11},{11... | collective-permute-start | bytes 786440 | tf_op jit(solution)/shard_map/ppermute | solution.py:32
  89.1 8.8 %collective-permute-start.4 = (f32[16,8,512]{2,1,0:T(8,128)S(1)}, f32[16,8,512]{2,1,0:T(8,128)S(1)}, u32[]{:S(2)}, u32[]{:S(2)}) collective-permute-start(f32[16,8,512]{2,1,0:T(8,128)S(1)} %get-tuple-element.63.late_probe_ref), channel_id=1, source_target_pairs={{0,1},{1,2},{2,3},{3,4},{4,5},{5,6},{6,7},{8,9},{9,10},{10,11},{11... | collective-permute-start | bytes 786440 | tf_op jit(solution)/shard_map/ppermute | solution.py:32
  94.3 1.0 %copy-start.4 = (f32[8,2,8192]{2,1,0:T(2,128)S(1)}, f32[8,2,8192]{2,1,0:T(2,128)}, u32[]{:S(2)}) copy-start(f32[8,2,8192]{2,1,0:T(2,128)} %dual_ref.1) | copy-start | bytes 1572868
  94.4 1.2 %copy-start.5 = (f32[8,2,8192]{2,1,0:T(2,128)S(1)}, f32[8,2,8192]{2,1,0:T(2,128)}, u32[]{:S(2)}) copy-start(f32[8,2,8192]{2,1,0:T(2,128)} %demand_ref.1) | copy-start | bytes 1572868
